TPU v7x, 256 devices: a whole 4x4x8 slice. The times are simulated.
256 devices in a mesh: ctx: 32 (over z, x_hi, core), head: 8 (over y, x_lo).
Axes of the slice: x: 4 (x_hi: 2, x_lo: 2; x = x_hi * 2 + x_lo), y: 4, z: 8, core: 2. Of those that a mesh axis runs over, the one named last changes fastest.
Arguments:
- target: bfloat16 [2048, 3072], P(('ctx', 'head')), may hold values from -6 to 6
- query_weight: bfloat16 [3072, 3072], P(None, 'head'), may hold values from -0.109375 to 0.109375
- source_keys: bfloat16 [65536, 3072], P('ctx', 'head'), may hold values from -210 to 210
- source_values: bfloat16 [65536, 3072], P('ctx', 'head'), may hold values from -6 to 6
- out_weight: bfloat16 [3072, 3072], P('head'), may hold values from -0.109375 to 0.109375
Outputs:
- attended: bfloat16 [2048, 3072], P(('ctx', 'head'))
All inputs are finite; a program needn't handle non-finite values.
Results may differ from a plain program's by a relative error of at most 0.022.
Values may be sent and summed in bfloat16 or wider, within the bound.
No kernel may reach another device: no remote copies, remote signals or barrier semaphores. Data moves between devices by JAX's collectives and lax.ppermute only.
A program may use at most 64 MiB of HBM per device.

v0:
```python
import math

import jax
import jax.numpy as jnp
from jax import lax
from jax.sharding import PartitionSpec as P

HD = 128


def passed_along(value, axis, steps):
    count = lax.axis_size(axis)
    pairs = [(source, (source + steps) % count) for source in range(count)]
    return lax.ppermute(value, axis, pairs)


def attend(queries, source_keys, source_values, maxima, totals, numerator):
    row_count = queries.shape[0]
    head_count = source_keys.shape[1] // HD
    q_heads = queries.reshape(row_count, head_count, HD)
    k_heads = source_keys.reshape(-1, head_count, HD)
    v_heads = source_values.reshape(-1, head_count, HD)
    scores = jnp.einsum("qhd,khd->qhk", q_heads, k_heads, preferred_element_type=jnp.float32)
    new_maxima = jnp.maximum(maxima, jnp.max(scores, axis=-1))
    weights = jnp.exp(scores - new_maxima[:, :, None])
    rescale = jnp.exp(maxima - new_maxima)
    new_totals = totals * rescale + jnp.sum(weights, axis=-1)
    weighted = jnp.einsum(
        "qhk,khd->qhd", weights.astype(jnp.bfloat16), v_heads, preferred_element_type=jnp.float32
    )
    return (new_maxima, new_totals, numerator * rescale[:, :, None] + weighted)


def shards(target, query_weight, source_keys, source_values, out_weight):
    scale = 1.0 / math.sqrt(HD)
    queries = (
        jnp.dot(
            lax.all_gather(target, "head", axis=0, tiled=True),
            query_weight,
            preferred_element_type=jnp.float32,
        )
        * scale
    ).astype(jnp.bfloat16)
    row_count = queries.shape[0]
    head_count = queries.shape[1] // HD
    lowest = jnp.full((row_count, head_count), -jnp.inf, jnp.float32)
    empty = jnp.zeros((row_count, head_count), jnp.float32)
    blank = jnp.zeros((row_count, head_count, HD), jnp.float32)
    state = (queries,) + attend(queries, source_keys, source_values, lowest, empty, blank)

    def advance(state):
        moving = passed_along(state[0], "ctx", 1)
        maxima, totals, numerator = passed_along((state[1], state[2], state[3]), "ctx", 1)
        return (moving,) + attend(moving, source_keys, source_values, maxima, totals, numerator)

    def advance_twice(unused, state):
        return advance(advance(state))

    state = lax.fori_loop(0, (lax.axis_size("ctx") - 2) // 2, advance_twice, state)
    state = advance(state)
    mixed = (state[3] / state[2][:, :, None]).reshape(row_count, -1).astype(jnp.bfloat16)
    mixed = passed_along(mixed, "ctx", 1)
    return lax.psum_scatter(
        jnp.dot(mixed, out_weight, preferred_element_type=jnp.float32).astype(jnp.bfloat16),
        "head",
        scatter_dimension=0,
        tiled=True,
    )


def solution(mesh):
    in_specs = (
        P(("ctx", "head"), None),
        P(None, "head"),
        P("ctx", "head"),
        P("ctx", "head"),
        P("head", None),
    )
    out_specs = P(("ctx", "head"), None)
    return jax.shard_map(shards, mesh=mesh, in_specs=in_specs, out_specs=out_specs, check_vma=False)
```

profile of v0, /device:TPU:4, one launch (start us, length us, event | category | flops | bytes accessed | tf_op | source)
XLA Modules:
  0.0 409.2 jit_solution(7126517284303664966)
XLA Ops:
  6.5 30.1 %all_gather.3 = bf16[64,3072]{1,0:T(8,128)(2,1)S(1)} all-gather(bf16[8,3072]{1,0:T(8,128)(2,1)} %param.7), channel_id=1, replica_groups=mesh['ctx'=32,'head'=8] {'head'}, dimensions={0}, use_global_device_ids=true | all-gather | bytes 442368 | tf_op jit(solution)/shard_map/all_gather | solution.py:38
  46.7 292.0 %while.16 = (s32[]{:T(128)}, bf16[64,384]{1,0:T(8,128)(2,1)S(1)}, f32[64,3]{0,1:T(4,128)S(1)}, f32[64,3]{0,1:T(4,128)S(1)}, f32[64,3,128]{2,0,1:T(8,128)S(1)}, /...) while((s32[]{:T(128)}, bf16[64,384]{1,0:T(8,128)(2,1)S(1)}, f32[64,3]{0,1:T(4,128)S(1)}, ...), condition=%wide.region_7.0_spmd, body=%wide.region_2.0_spmd.sunk | while | flops 406684416 | bytes 30016972 | solution.py:59
  54.3 3.4 collective-permute-start.5
  72.6 3.4 collective-permute-start.5
  91.1 4.6 %collective-permute-start.5 = (f32[64,3]{0,1:T(4,128)S(1)}, f32[64,3]{0,1:T(4,128)S(1)}, u32[]{:S(2)}, u32[]{:S(2)}) collective-permute-start(f32[64,3]{0,1:T(4,128)S(1)} %get-tuple-element.141), channel_id=1, source_target_pairs={{0,8},{8,16},{16,24},{24,32},{32,40},{40,48},{48,56},{56,64},{64,7... | collective-permute-start | bytes 2312 | tf_op jit(solution)/shard_map/while/body/eval_jaxpr/ppermute | solution.py:14
  111.5 3.8 collective-permute-start.5
  130.9 4.0 collective-permute-start.5
  142.2 3.4 collective-permute-start.4
  150.6 4.0 collective-permute-start.5
  161.8 3.4 collective-permute-start.4
  170.3 4.0 collective-permute-start.5
  189.9 4.0 collective-permute-start.5
  209.6 4.0 collective-permute-start.5
  229.2 4.0 collective-permute-start.5
  248.9 4.0 collective-permute-start.5
  268.5 4.0 collective-permute-start.5
  279.8 3.4 collective-permute-start.4
  288.2 4.0 collective-permute-start.5
  307.9 4.0 collective-permute-start.5
  319.1 3.4 collective-permute-start.4
  327.5 4.0 collective-permute-start.5
  338.7 3.4 collective-permute-start.9
  349.1 4.7 %collective-permute-done.12 = bf16[64,384]{1,0:T(8,128)(2,1)S(1)} collective-permute-done((bf16[64,384]{1,0:T(8,128)(2,1)S(1)}, bf16[64,384]{1,0:T(8,128)(2,1)S(1)}, u32[]{:S(2)}, u32[]{:S(2)}) %collective-permute-start.12) | collective-permute-done | bytes 49184 | tf_op jit(solution)/shard_map/ppermute | solution.py:14
  355.2 47.2 %reduce-scatter.2.cloned.1.call-done = bf16[8,3072]{1,0:T(8,128)(2,1)} async-done(((bf16[64,3072]{1,0:T(8,128)(2,1)}), bf16[8,3072]{1,0:T(8,128)(2,1)}) %reduce-scatter.2.cloned.1.call-update) | async-done | bytes 49168 | tf_op jit(solution)/shard_map/reduce_scatter | solution.py:63
  (463 shorter events, 236.4 us)
Async XLA Ops:
  6.5 395.8 %reduce-scatter.2.cloned.1.call-start = ((), (), s32[]{:S(2)}) async-start(), calls=%async_computation.1 | async-start | bytes 442368 | tf_op jit(solution)/shard_map/reduce_scatter | solution.py:63
  85.9 10.0 %collective-permute-start.6 = (f32[64,3,128]{2,0,1:T(8,128)S(1)}, f32[64,3,128]{2,0,1:T(8,128)S(1)}, u32[]{:S(2)}, u32[]{:S(2)}) collective-permute-start(f32[64,3,128]{2,0,1:T(8,128)S(1)} %get-tuple-element.157), channel_id=1, source_target_pairs={{0,8},{8,16},{16,24},{24,32},{32,40},{40,48},{48,56},{56,64},{64,7... | collective-permute-start | bytes 294920 | tf_op jit(solution)/shard_map/while/body/eval_jaxpr/ppermute | solution.py:14
  90.6 10.7 %collective-permute-start.3 = (f32[64,3]{0,1:T(4,128)S(1)}, f32[64,3]{0,1:T(4,128)S(1)}, u32[]{:S(2)}, u32[]{:S(2)}) collective-permute-start(f32[64,3]{0,1:T(4,128)S(1)} %max.12), channel_id=1, source_target_pairs={{0,8},{8,16},{16,24},{24,32},{32,40},{40,48},{48,56},{56,64},{64,7... | collective-permute-start | bytes 2312 | tf_op jit(solution)/shard_map/while/body/eval_jaxpr/ppermute | solution.py:14
  91.1 10.5 %collective-permute-start.5 = (f32[64,3]{0,1:T(4,128)S(1)}, f32[64,3]{0,1:T(4,128)S(1)}, u32[]{:S(2)}, u32[]{:S(2)}) collective-permute-start(f32[64,3]{0,1:T(4,128)S(1)} %get-tuple-element.141), channel_id=1, source_target_pairs={{0,8},{8,16},{16,24},{24,32},{32,40},{40,48},{48,56},{56,64},{64,7... | collective-permute-start | bytes 2312 | tf_op jit(solution)/shard_map/while/body/eval_jaxpr/ppermute | solution.py:14
  130.5 9.9 %collective-permute-start.3 = (f32[64,3]{0,1:T(4,128)S(1)}, f32[64,3]{0,1:T(4,128)S(1)}, u32[]{:S(2)}, u32[]{:S(2)}) collective-permute-start(f32[64,3]{0,1:T(4,128)S(1)} %max.12), channel_id=1, source_target_pairs={{0,8},{8,16},{16,24},{24,32},{32,40},{40,48},{48,56},{56,64},{64,7... | collective-permute-start | bytes 2312 | tf_op jit(solution)/shard_map/while/body/eval_jaxpr/ppermute | solution.py:14
  130.9 9.8 %collective-permute-start.5 = (f32[64,3]{0,1:T(4,128)S(1)}, f32[64,3]{0,1:T(4,128)S(1)}, u32[]{:S(2)}, u32[]{:S(2)}) collective-permute-start(f32[64,3]{0,1:T(4,128)S(1)} %get-tuple-element.141), channel_id=1, source_target_pairs={{0,8},{8,16},{16,24},{24,32},{32,40},{40,48},{48,56},{56,64},{64,7... | collective-permute-start | bytes 2312 | tf_op jit(solution)/shard_map/while/body/eval_jaxpr/ppermute | solution.py:14
  150.1 9.9 %collective-permute-start.3 = (f32[64,3]{0,1:T(4,128)S(1)}, f32[64,3]{0,1:T(4,128)S(1)}, u32[]{:S(2)}, u32[]{:S(2)}) collective-permute-start(f32[64,3]{0,1:T(4,128)S(1)} %max.12), channel_id=1, source_target_pairs={{0,8},{8,16},{16,24},{24,32},{32,40},{40,48},{48,56},{56,64},{64,7... | collective-permute-start | bytes 2312 | tf_op jit(solution)/shard_map/while/body/eval_jaxpr/ppermute | solution.py:14
  150.6 9.8 %collective-permute-start.5 = (f32[64,3]{0,1:T(4,128)S(1)}, f32[64,3]{0,1:T(4,128)S(1)}, u32[]{:S(2)}, u32[]{:S(2)}) collective-permute-start(f32[64,3]{0,1:T(4,128)S(1)} %get-tuple-element.141), channel_id=1, source_target_pairs={{0,8},{8,16},{16,24},{24,32},{32,40},{40,48},{48,56},{56,64},{64,7... | collective-permute-start | bytes 2312 | tf_op jit(solution)/shard_map/while/body/eval_jaxpr/ppermute | solution.py:14
  169.8 9.9 %collective-permute-start.3 = (f32[64,3]{0,1:T(4,128)S(1)}, f32[64,3]{0,1:T(4,128)S(1)}, u32[]{:S(2)}, u32[]{:S(2)}) collective-permute-start(f32[64,3]{0,1:T(4,128)S(1)} %max.12), channel_id=1, source_target_pairs={{0,8},{8,16},{16,24},{24,32},{32,40},{40,48},{48,56},{56,64},{64,7... | collective-permute-start | bytes 2312 | tf_op jit(solution)/shard_map/while/body/eval_jaxpr/ppermute | solution.py:14
  170.3 9.8 %collective-permute-start.5 = (f32[64,3]{0,1:T(4,128)S(1)}, f32[64,3]{0,1:T(4,128)S(1)}, u32[]{:S(2)}, u32[]{:S(2)}) collective-permute-start(f32[64,3]{0,1:T(4,128)S(1)} %get-tuple-element.141), channel_id=1, source_target_pairs={{0,8},{8,16},{16,24},{24,32},{32,40},{40,48},{48,56},{56,64},{64,7... | collective-permute-start | bytes 2312 | tf_op jit(solution)/shard_map/while/body/eval_jaxpr/ppermute | solution.py:14
  189.4 9.9 %collective-permute-start.3 = (f32[64,3]{0,1:T(4,128)S(1)}, f32[64,3]{0,1:T(4,128)S(1)}, u32[]{:S(2)}, u32[]{:S(2)}) collective-permute-start(f32[64,3]{0,1:T(4,128)S(1)} %max.12), channel_id=1, source_target_pairs={{0,8},{8,16},{16,24},{24,32},{32,40},{40,48},{48,56},{56,64},{64,7... | collective-permute-start | bytes 2312 | tf_op jit(solution)/shard_map/while/body/eval_jaxpr/ppermute | solution.py:14
  189.9 9.8 %collective-permute-start.5 = (f32[64,3]{0,1:T(4,128)S(1)}, f32[64,3]{0,1:T(4,128)S(1)}, u32[]{:S(2)}, u32[]{:S(2)}) collective-permute-start(f32[64,3]{0,1:T(4,128)S(1)} %get-tuple-element.141), channel_id=1, source_target_pairs={{0,8},{8,16},{16,24},{24,32},{32,40},{40,48},{48,56},{56,64},{64,7... | collective-permute-start | bytes 2312 | tf_op jit(solution)/shard_map/while/body/eval_jaxpr/ppermute | solution.py:14
  209.1 9.9 %collective-permute-start.3 = (f32[64,3]{0,1:T(4,128)S(1)}, f32[64,3]{0,1:T(4,128)S(1)}, u32[]{:S(2)}, u32[]{:S(2)}) collective-permute-start(f32[64,3]{0,1:T(4,128)S(1)} %max.12), channel_id=1, source_target_pairs={{0,8},{8,16},{16,24},{24,32},{32,40},{40,48},{48,56},{56,64},{64,7... | collective-permute-start | bytes 2312 | tf_op jit(solution)/shard_map/while/body/eval_jaxpr/ppermute | solution.py:14
  209.6 9.8 %collective-permute-start.5 = (f32[64,3]{0,1:T(4,128)S(1)}, f32[64,3]{0,1:T(4,128)S(1)}, u32[]{:S(2)}, u32[]{:S(2)}) collective-permute-start(f32[64,3]{0,1:T(4,128)S(1)} %get-tuple-element.141), channel_id=1, source_target_pairs={{0,8},{8,16},{16,24},{24,32},{32,40},{40,48},{48,56},{56,64},{64,7... | collective-permute-start | bytes 2312 | tf_op jit(solution)/shard_map/while/body/eval_jaxpr/ppermute | solution.py:14
  228.8 9.9 %collective-permute-start.3 = (f32[64,3]{0,1:T(4,128)S(1)}, f32[64,3]{0,1:T(4,128)S(1)}, u32[]{:S(2)}, u32[]{:S(2)}) collective-permute-start(f32[64,3]{0,1:T(4,128)S(1)} %max.12), channel_id=1, source_target_pairs={{0,8},{8,16},{16,24},{24,32},{32,40},{40,48},{48,56},{56,64},{64,7... | collective-permute-start | bytes 2312 | tf_op jit(solution)/shard_map/while/body/eval_jaxpr/ppermute | solution.py:14
  229.2 9.8 %collective-permute-start.5 = (f32[64,3]{0,1:T(4,128)S(1)}, f32[64,3]{0,1:T(4,128)S(1)}, u32[]{:S(2)}, u32[]{:S(2)}) collective-permute-start(f32[64,3]{0,1:T(4,128)S(1)} %get-tuple-element.141), channel_id=1, source_target_pairs={{0,8},{8,16},{16,24},{24,32},{32,40},{40,48},{48,56},{56,64},{64,7... | collective-permute-start | bytes 2312 | tf_op jit(solution)/shard_map/while/body/eval_jaxpr/ppermute | solution.py:14
  248.4 9.9 %collective-permute-start.3 = (f32[64,3]{0,1:T(4,128)S(1)}, f32[64,3]{0,1:T(4,128)S(1)}, u32[]{:S(2)}, u32[]{:S(2)}) collective-permute-start(f32[64,3]{0,1:T(4,128)S(1)} %max.12), channel_id=1, source_target_pairs={{0,8},{8,16},{16,24},{24,32},{32,40},{40,48},{48,56},{56,64},{64,7... | collective-permute-start | bytes 2312 | tf_op jit(solution)/shard_map/while/body/eval_jaxpr/ppermute | solution.py:14
  268.1 9.9 %collective-permute-start.3 = (f32[64,3]{0,1:T(4,128)S(1)}, f32[64,3]{0,1:T(4,128)S(1)}, u32[]{:S(2)}, u32[]{:S(2)}) collective-permute-start(f32[64,3]{0,1:T(4,128)S(1)} %max.12), channel_id=1, source_target_pairs={{0,8},{8,16},{16,24},{24,32},{32,40},{40,48},{48,56},{56,64},{64,7... | collective-permute-start | bytes 2312 | tf_op jit(solution)/shard_map/while/body/eval_jaxpr/ppermute | solution.py:14
  268.5 9.8 %collective-permute-start.5 = (f32[64,3]{0,1:T(4,128)S(1)}, f32[64,3]{0,1:T(4,128)S(1)}, u32[]{:S(2)}, u32[]{:S(2)}) collective-permute-start(f32[64,3]{0,1:T(4,128)S(1)} %get-tuple-element.141), channel_id=1, source_target_pairs={{0,8},{8,16},{16,24},{24,32},{32,40},{40,48},{48,56},{56,64},{64,7... | collective-permute-start | bytes 2312 | tf_op jit(solution)/shard_map/while/body/eval_jaxpr/ppermute | solution.py:14
  287.7 9.9 %collective-permute-start.3 = (f32[64,3]{0,1:T(4,128)S(1)}, f32[64,3]{0,1:T(4,128)S(1)}, u32[]{:S(2)}, u32[]{:S(2)}) collective-permute-start(f32[64,3]{0,1:T(4,128)S(1)} %max.12), channel_id=1, source_target_pairs={{0,8},{8,16},{16,24},{24,32},{32,40},{40,48},{48,56},{56,64},{64,7... | collective-permute-start | bytes 2312 | tf_op jit(solution)/shard_map/while/body/eval_jaxpr/ppermute | solution.py:14
  288.2 9.8 %collective-permute-start.5 = (f32[64,3]{0,1:T(4,128)S(1)}, f32[64,3]{0,1:T(4,128)S(1)}, u32[]{:S(2)}, u32[]{:S(2)}) collective-permute-start(f32[64,3]{0,1:T(4,128)S(1)} %get-tuple-element.141), channel_id=1, source_target_pairs={{0,8},{8,16},{16,24},{24,32},{32,40},{40,48},{48,56},{56,64},{64,7... | collective-permute-start | bytes 2312 | tf_op jit(solution)/shard_map/while/body/eval_jaxpr/ppermute | solution.py:14
  307.4 9.9 %collective-permute-start.3 = (f32[64,3]{0,1:T(4,128)S(1)}, f32[64,3]{0,1:T(4,128)S(1)}, u32[]{:S(2)}, u32[]{:S(2)}) collective-permute-start(f32[64,3]{0,1:T(4,128)S(1)} %max.12), channel_id=1, source_target_pairs={{0,8},{8,16},{16,24},{24,32},{32,40},{40,48},{48,56},{56,64},{64,7... | collective-permute-start | bytes 2312 | tf_op jit(solution)/shard_map/while/body/eval_jaxpr/ppermute | solution.py:14
  327.0 9.9 %collective-permute-start.3 = (f32[64,3]{0,1:T(4,128)S(1)}, f32[64,3]{0,1:T(4,128)S(1)}, u32[]{:S(2)}, u32[]{:S(2)}) collective-permute-start(f32[64,3]{0,1:T(4,128)S(1)} %max.12), channel_id=1, source_target_pairs={{0,8},{8,16},{16,24},{24,32},{32,40},{40,48},{48,56},{56,64},{64,7... | collective-permute-start | bytes 2312 | tf_op jit(solution)/shard_map/while/body/eval_jaxpr/ppermute | solution.py:14
  327.5 9.8 %collective-permute-start.5 = (f32[64,3]{0,1:T(4,128)S(1)}, f32[64,3]{0,1:T(4,128)S(1)}, u32[]{:S(2)}, u32[]{:S(2)}) collective-permute-start(f32[64,3]{0,1:T(4,128)S(1)} %get-tuple-element.141), channel_id=1, source_target_pairs={{0,8},{8,16},{16,24},{24,32},{32,40},{40,48},{48,56},{56,64},{64,7... | collective-permute-start | bytes 2312 | tf_op jit(solution)/shard_map/while/body/eval_jaxpr/ppermute | solution.py:14
  (136 other events, 1167.0 us)
Sparse Core Ops, SparseCore 0:
  355.3 47.0 reduce-scatter.1
where the time goes:
time: 410 us; the launch traced here: 409 us
  starting transfers between devices  193 us (47%)
  waiting for transfers between devices  89.6 us (22%)
  matrix products  63.1 us (15%)
  blocking collectives  30.1 us (7%)
  between operations  13.5 us (3%)
  other arithmetic  12 us (3%)
  local copies, waits for them, and re-layouts  6.41 us (2%)
    ppermute x125, starting transfers between devices, passed_along(): return lax.ppermute(value, axis, pairs)  193 us
    reduce_scatter x1, waiting for transfers between devices, shards(): lax.psum_scatter(jnp.dot(mixed, out_weight, preferred_element_type=jnp.fl...  47.2 us
    ppermute x125, waiting for transfers between devices, passed_along(): return lax.ppermute(value, axis, pairs)  42.3 us
    dot_general x32, matrix products, attend(): jnp.einsum('qhd,khd->qhk', q_heads, k_heads, preferred_element_type=jnp.f...  36.9 us
    all_gather x1, blocking collectives, shards(): lax.all_gather(target, 'head', axis=0, tiled=True)  30.1 us
    dot_general x32, matrix products, attend(): jnp.einsum('qhk,khd->qhd', weights.astype(jnp.bfloat16), v_heads, preferr...  22.7 us
    reduce_sum x32, other arithmetic, attend(): new_totals = totals * rescale + jnp.sum(weights, axis=-1)  11.7 us
  transfers between devices with their start and end apart: 126, of which 46 were waited for; matrix products, arithmetic and copies ran while one was open for 14% of the time, Pallas kernels for 0%

commit v1 on v0

v1 whole, which is shorter than its diff:
```python
import functools
import math

import jax
import jax.numpy as jnp
from jax import lax
from jax.experimental import pallas as pl
from jax.experimental.pallas import tpu as pltpu
from jax.sharding import PartitionSpec as P

HD = 128
BLOCK = 512
GROUP = 1024
PART = 64
TAIL = 16
AHEAD = 2
MERGE_FLOPS = 10**10
LOG2E = math.log2(math.e)
Z = 8


def vmem():
    return pl.BlockSpec(memory_space=pltpu.VMEM)


def move(value, dz=0, dx=0, dcore=0):
    pairs = []
    for source in range(Z * 4):
        z, x, core = source // 4, source // 2 % 2, source % 2
        pairs.append((source, (z + dz) % Z * 4 + (x ^ dx) * 2 + (core ^ dcore)))
    return lax.ppermute(value, "ctx", pairs)


def carry(value, steps):
    pairs = []
    for source in range(Z * 4):
        z, core = source // 4, source % 2
        pairs.append((source, (z + (steps if core else -steps)) % Z * 4 + source % 4))
    return lax.ppermute(value, "ctx", pairs)


def exchange(value):
    return lax.all_to_all(value, "head", 0, 0)


def parts_of(level):
    high = level.astype(jnp.bfloat16).astype(jnp.float32)
    middle = (level - high).astype(jnp.bfloat16).astype(jnp.float32)
    return high, middle, level - high - middle


def project_kernel(rows, weight, out):
    result = jnp.dot(rows[...], weight[...], preferred_element_type=jnp.float32)
    out[...] = (result * (1.0 / math.sqrt(HD))).astype(jnp.bfloat16)


def repeat_kernel(value, out):
    for at in range(out.shape[0]):
        out[at] = value[...]


def attend_kernel(count, *refs):
    asked, (key_a, key_b, value_a, value_b), rest = refs[:count], refs[count : count + 4], refs[count + 4 :]
    outs, held, weights = rest[:count], rest[count : count + AHEAD + 1], rest[count + AHEAD + 1 :]
    heads = asked[0].shape[1] // HD
    half = key_a.shape[0]
    across = sum(ref.shape[0] for ref in asked)
    steps = [(head, at) for head in range(heads) for at in range(0, 2 * half, GROUP)]
    row = lax.broadcasted_iota(jnp.int32, (TAIL, across), 0)

    def columns(head):
        return slice(head * HD, (head + 1) * HD)

    def turned_queries(head):
        return jnp.transpose(jnp.concatenate([ref[:, columns(head)] for ref in asked], axis=0))

    queries = [turned_queries(head) for head in range(heads)]

    def score(step, part, peak):
        head, at = steps[step]
        keys, place = (key_a, at + part) if at < half else (key_b, at + part - half)
        block = LOG2E * jnp.dot(
            keys[place : place + BLOCK, columns(head)], queries[head], preferred_element_type=jnp.float32
        )
        held[step % len(held)][part : part + BLOCK, :] = block
        top = jnp.max(block.reshape(BLOCK // 8, 8, across), axis=0)
        return top if peak is None else jnp.maximum(peak, top)

    def weigh(step, start, peak, total):
        for part in range(start, start + BLOCK, PART):
            block = held[step % len(held)][part : part + PART, :].reshape(PART // 8, 8, across)
            block = jnp.exp2(block - peak[None])
            total = total + jnp.sum(block, axis=0)
            block = block.reshape(PART, across).astype(jnp.bfloat16)
            weights[step % 2][part : part + PART, :] = block
        return total

    def weighted(step):
        head, at = steps[step]
        values, place = (value_a, at) if at < half else (value_b, at - half)
        return jnp.dot(
            values[columns(head), place : place + GROUP],
            weights[step % 2][...],
            preferred_element_type=jnp.float32,
        )

    stats = jnp.zeros((TAIL, across), jnp.float32)
    numerator = None

    def add_values(step, rescale, top, total):
        nonlocal numerator, stats
        head, at = steps[step]
        here = weighted(step)
        numerator = here if at == 0 else numerator * rescale + here
        if at + GROUP == 2 * half:
            total = jnp.sum(total, axis=0, keepdims=True)
            partial = jnp.transpose(numerator / total).astype(jnp.bfloat16)
            place = 0
            for ref, out in zip(asked, outs):
                out[: ref.shape[0], columns(head)] = partial[place : place + ref.shape[0]]
                place += ref.shape[0]
            for index, part in enumerate(parts_of(top + LOG2E * jnp.log(total))):
                stats = jnp.where(row == head * 3 + index, part, stats)

    peaks = [None] * len(steps)

    def score_ahead(step, part):
        if step < len(steps):
            peaks[step] = score(step, part, peaks[step])

    for step in range(AHEAD):
        for part in range(0, GROUP, BLOCK):
            score_ahead(step, part)
    pending = top = total = None
    for step, (head, at) in enumerate(steps):
        rescale, highest = None, jnp.max(peaks[step], axis=0, keepdims=True)
        if at:
            highest = jnp.maximum(top, highest)
            rescale = jnp.exp2(top - highest)
            total = total * rescale
        else:
            total = jnp.zeros((8, across), jnp.float32)
        top = highest
        wide = jnp.broadcast_to(top, (8, across))
        for part in range(0, GROUP, BLOCK):
            score_ahead(step + AHEAD, part)
            total = weigh(step, part, wide, total)
            if part == 0 and pending:
                add_values(*pending)
        pending = (step, rescale, top, total)
    add_values(*pending)
    stats = stats.astype(jnp.bfloat16)
    place = 0
    for ref, out in zip(asked, outs):
        rows = ref.shape[0]
        out[rows:, :] = jnp.zeros((TAIL, heads * HD), jnp.bfloat16)
        out[rows:, :rows] = stats[:, place : place + rows]
        place += rows


def merged(parts, tails):
    rows = parts[0].shape[0]
    heads = parts[0].shape[1] // HD
    shares, levels = [], []
    for head in range(heads):
        heights = [sum(tail[3 * head + index : 3 * head + index + 1, :] for index in range(3)) for tail in tails]
        peak = heights[0]
        for height in heights[1:]:
            peak = jnp.maximum(peak, height)
        powers = [jnp.exp2(height - peak) for height in heights]
        total = sum(powers)
        shares += [power / total for power in powers]
        levels.append(peak + LOG2E * jnp.log(total))
    place = lax.broadcasted_iota(jnp.int32, (HD, rows), 0)
    table = jnp.zeros((HD, rows), jnp.float32)
    for index, share in enumerate(shares):
        table = jnp.where(place == index, share, table)
    table = jnp.transpose(table)
    means = []
    for head in range(heads):
        columns = slice(head * HD, (head + 1) * HD)
        mean = 0.0
        for index, part in enumerate(parts):
            at = head * len(parts) + index
            mean += table[:, at : at + 1] * part[:, columns].astype(jnp.float32)
        means.append(mean.astype(jnp.bfloat16))
    return jnp.concatenate(means, axis=1), levels


def tail_of(levels):
    width = levels[0].shape[1]
    row = lax.broadcasted_iota(jnp.int32, (TAIL, width), 0)
    tail = jnp.zeros((TAIL, width), jnp.float32)
    for head, level in enumerate(levels):
        for index, part in enumerate(parts_of(level)):
            tail = jnp.where(row == head * 3 + index, part, tail)
    return tail.astype(jnp.bfloat16)


def piece(ref, start, rows):
    tail = ref[ref.shape[0] - TAIL :, start : start + rows].astype(jnp.float32)
    return ref[start : start + rows, :], tail


def merge_kernel(starts, *refs):
    out = refs[-1]
    rows = out.shape[0] - TAIL
    mean, levels = merged(*zip(*[piece(ref, start, rows) for ref, start in zip(refs, starts)]))
    out[:rows, :] = mean
    out[rows:, :] = jnp.zeros((TAIL, out.shape[1]), jnp.bfloat16)
    out[rows:, :rows] = tail_of(levels)


def finish_kernel(*refs):
    weight, out = refs[-2:]
    rows = out.shape[0]
    mixed, _ = merged(*zip(*[piece(ref, 0, rows) for ref in refs[:-2]]))
    out[...] = jnp.dot(mixed, weight[...], preferred_element_type=jnp.float32).astype(jnp.bfloat16)


def call(kernel, name, out_shape, operands, flops=0, read=0, exps=0, limit=16, scratch=()):
    return pl.pallas_call(
        kernel,
        out_shape=out_shape,
        in_specs=[vmem()] * len(operands),
        out_specs=jax.tree.map(lambda _: vmem(), out_shape),
        scratch_shapes=scratch,
        compiler_params=pltpu.CompilerParams(vmem_limit_bytes=limit << 20),
        cost_estimate=pl.CostEstimate(flops=flops, bytes_accessed=read, transcendentals=exps),
        name=name,
    )(*operands)


def shape(*dims):
    return jax.ShapeDtypeStruct(dims, jnp.bfloat16)


def project(rows, weight):
    out_shape = shape(rows.shape[0], weight.shape[1])
    flops = 2 * rows.shape[0] * weight.size
    return call(project_kernel, "project", out_shape, (rows, weight), flops, 2 * weight.size)


def repeat(value, count):
    return call(repeat_kernel, "repeat", shape(count, *value.shape), (value,), MERGE_FLOPS)


def attend(asked, keys, values):
    width = asked[0].shape[1]
    across = sum(queries.shape[0] for queries in asked)
    pairs = 2 * across * keys[0].shape[0] * (width // HD)
    out_shape = [shape(queries.shape[0] + TAIL, width) for queries in asked]
    scratch = [pltpu.VMEM((GROUP, across), kind) for kind in (jnp.float32,) * (AHEAD + 1) + (jnp.bfloat16,) * 2]
    kernel = functools.partial(attend_kernel, len(asked))
    operands = (*asked, *keys, *values)
    return call(kernel, "attend", out_shape, operands, 8 * pairs * HD, 8 * keys[0].size, pairs, 32, scratch)


def turn_kernel(value, out):
    for head in range(value.shape[1] // HD):
        out[head * HD : (head + 1) * HD, :] = jnp.transpose(value[:, head * HD : (head + 1) * HD])


def turn(value):
    return call(turn_kernel, "turn", shape(*value.shape[::-1]), (value,), 0, 4 * value.size)


def merge(rows, *places):
    parts, starts = zip(*places)
    out_shape = shape(rows + TAIL, parts[0].shape[1])
    return call(functools.partial(merge_kernel, starts), "merge", out_shape, parts, MERGE_FLOPS)


def finish(parts, weight):
    out_shape = shape(parts[-1].shape[0] - TAIL, weight.shape[1])
    flops = 2 * out_shape.shape[0] * weight.size
    return call(finish_kernel, "finish", out_shape, (*parts, weight), flops, 2 * weight.size)


def tied(*values):
    return lax.optimization_barrier(values)


def shards(target, query_weight, source_keys, source_values, out_weight):
    groups = lax.axis_size("head")
    rows, depth = target.shape
    keys = (source_keys, move(source_keys, dcore=1))
    other_values = move(source_values, dcore=1)
    gathered = exchange(repeat(target, groups))
    queries = project(gathered.reshape(groups * rows, depth), query_weight)
    few = queries.shape[0]
    queries, source_values = tied(queries, source_values)
    partner, turned = tied(move(queries, dx=1), turn(source_values))
    mine = jnp.concatenate([queries, partner], axis=0)
    sibling, other_values = tied(move(mine, dcore=1), other_values)
    near = carry(jnp.concatenate([mine, sibling], axis=0), 1)
    values = (turned, turn(other_values))
    part_own, = attend((mine,), keys, values)
    part_own, near = tied(part_own, near)
    second = carry(near, 1)
    part, = attend((near,), keys, values)
    part, second = tied(part, second)
    third, far = carry(second, 1), carry(second[: 2 * few], 2)
    back_near = carry(part, -1)
    part, = attend((third,), keys, values)
    part, second, far, back_near = tied(part, second, far, back_near)
    back_third = carry(part, -3)
    part_far, = attend((far,), keys, values)
    part_far, second = tied(part_far, second)
    back_far = carry(part_far, -4)
    part, = attend((second,), keys, values)
    early = merge(2 * few, (part_own, 0), (back_far, 0), (back_near, 0), (back_third, 0))
    back_second, early = tied(carry(part, -2), early)
    others = merge(2 * few, *[(part, 2 * few) for part in (back_near, back_second, back_third)])
    others = move(others, dcore=1)
    kept = merge(2 * few, (early, 0), (back_second, 0))
    other = move(merge(few, (kept, few), (others, few)), dx=1)
    projected = finish((kept, others, other), out_weight)
    received = exchange(projected.reshape(groups, rows, depth))
    return jnp.sum(received.astype(jnp.float32), axis=0).astype(jnp.bfloat16)


def solution(mesh):
    in_specs = (
        P(("ctx", "head"), None),
        P(None, "head"),
        P("ctx", "head"),
        P("ctx", "head"),
        P("head", None),
    )
    out_specs = P(("ctx", "head"), None)
    return jax.shard_map(shards, mesh=mesh, in_specs=in_specs, out_specs=out_specs, check_vma=False)
```

time: 410 us -> 96.5 us (0.24)
  starting transfers between devices: 193 us -> 21 us
  waiting for transfers between devices: 89.6 us -> 24.4 us
  matrix products: 63.1 us -> 0 us
  Pallas kernels: 0 us -> 23 us
  between operations: 13.5 us -> 0.18 us
  other arithmetic: 12 us -> 0.7 us
  local copies, waits for them, and re-layouts: 6.41 us -> 0.84 us
  blocking collectives: 30.1 us -> 24.6 us
    ppermute x125 -> x14, starting transfers between devices: 193 us -> 21 us  [the longest x8 18.5 us: carry(): return lax.ppermute(value, 'ctx', pairs)]
    dot_general x66 -> x0, matrix products: 63.1 us -> none  [the longest x32 36.9 us: attend(): jnp.einsum('qhd,khd->qhk', q_heads, k_heads, preferred_element_type=jnp.f...]
    reduce_scatter x1 -> x0, waiting for transfers between devices: 47.2 us -> none  [shards(): lax.psum_scatter(jnp.dot(mixed, out_weight, preferred_element_type=jnp.fl...]
    all_gather x1 -> x0, blocking collectives: 30.1 us -> none  [shards(): lax.all_gather(target, 'head', axis=0, tiled=True)]
    all_to_all x0 -> x2, blocking collectives: none -> 24.6 us  [exchange(): return lax.all_to_all(value, 'head', 0, 0)]
    pallas_call x0 -> x14, Pallas kernels: none -> 23 us  [call(): pl.pallas_call(kernel, out_shape=out_shape, in_specs=[vmem()] * len(opera...]
    ppermute x125 -> x14, waiting for transfers between devices: 42.3 us -> 24.4 us  [the longest x8 12.8 us: carry(): return lax.ppermute(value, 'ctx', pairs)]
    reduce_sum x32 -> x1, other arithmetic: 11.7 us -> 0.68 us  [shards(): return jnp.sum(received.astype(jnp.float32), axis=0).astype(jnp.bfloat16)]
  transfers between devices with their start and end apart: 126 -> 14, of which waited for: 46 -> 7; matrix products, arithmetic and copies ran while one was open for 14% -> 0% of each run, Pallas kernels for 0% -> 20%
where the time goes in v1:
time: 96.5 us; the launch traced here: 94.7 us
  blocking collectives  24.6 us (25%)
  waiting for transfers between devices  24.4 us (25%)
  Pallas kernels  23 us (24%)
  starting transfers between devices  21 us (22%)
    all_to_all x2, blocking collectives, exchange(): return lax.all_to_all(value, 'head', 0, 0)  24.6 us
    pallas_call x14, Pallas kernels, call(): pl.pallas_call(kernel, out_shape=out_shape, in_specs=[vmem()] * len(opera...  23 us
    ppermute x8, starting transfers between devices, carry(): return lax.ppermute(value, 'ctx', pairs)  18.5 us
    ppermute x8, waiting for transfers between devices, carry(): return lax.ppermute(value, 'ctx', pairs)  12.8 us
    ppermute x6, waiting for transfers between devices, move(): return lax.ppermute(value, 'ctx', pairs)  11.5 us
    ppermute x6, starting transfers between devices, move(): return lax.ppermute(value, 'ctx', pairs)  2.46 us
  transfers between devices with their start and end apart: 14, of which 7 were waited for; matrix products, arithmetic and copies ran while one was open for 0% of the time, Pallas kernels for 20%

profile of v1, /device:TPU:4, one launch (start us, length us, event | category | flops | bytes accessed | tf_op | source)
XLA Modules:
  0.0 94.7 jit_solution(10358151183875011859)
XLA Ops:
  0.5 0.8 copy-done.4
  1.3 14.0 %all_to_all.10 = bf16[8,8,3072]{2,1,0:T(8,128)(2,1)S(1)} all-to-all(bf16[8,8,3072]{2,1,0:T(8,128)(2,1)S(1)} %repeat.1), channel_id=1, replica_groups=mesh['ctx'=32,'head'=8] {'head'}, dimensions={0} | all-to-all | bytes 786432 | tf_op jit(solution)/shard_map/all_to_all | solution.py:43
  15.8 0.9 collective-permute-start
  17.2 4.3 %collective-permute-done = bf16[64,384]{1,0:T(8,128)(2,1)S(1)} collective-permute-done((bf16[64,384]{1,0:T(8,128)(2,1)S(1)}, bf16[64,384]{1,0:T(8,128)(2,1)S(1)}, u32[]{:S(2)}, u32[]{:S(2)}) %collective-permute-start) | collective-permute-done | bytes 49184 | tf_op jit(solution)/shard_map/ppermute | solution.py:31
  21.6 1.3 %collective-permute-done.2 = bf16[128,384]{1,0:T(8,128)(2,1)S(1)} collective-permute-done((bf16[128,384]{1,0:T(8,128)(2,1)S(1)}, bf16[128,384]{1,0:T(8,128)(2,1)S(1)}, u32[]{:S(2)}, u32[]{:S(2)}) %collective-permute-start.2) | collective-permute-done | bytes 98336 | tf_op jit(solution)/shard_map/ppermute | solution.py:31
  23.0 5.9 %collective-permute-start.4 = (bf16[256,384]{1,0:T(8,128)(2,1)S(1)}, bf16[256,384]{1,0:T(8,128)(2,1)S(1)}, u32[]{:S(2)}, u32[]{:S(2)}) collective-permute-start(bf16[256,384]{1,0:T(8,128)(2,1)S(1)} %pad_maximum_fusion), channel_id=1, source_target_pairs={{0,224},{8,40},{16,240},{24,56},{32,0},{40,72},{48,16},{56,88},{64... | collective-permute-start | bytes 589832 | tf_op jit(solution)/shard_map/ppermute | solution.py:39
  29.4 2.8 %attend.5.refs_0_ = bf16[144,384]{1,0:T(8,128)(2,1)S(1)} custom-call(bf16[128,384]{1,0:T(8,128)(2,1)S(1)} %constant_dynamic-update-slice_fusion.refs_0_, bf16[2048,384]{1,0:T(8,128)(2,1)S(1)} %copy-done, bf16[2048,384]{1,0:T(8,128)(2,1)S(1)} %collective-permute-done.1.refs_2_, bf16[384,2048]{1,0:T(8,128)(2,1)S(1)} %turn.2.refs_3_, ...), custom_call_target="tpu_custom_call" | custom-call | flops 1610612736 | bytes 6291456 | tf_op jit(solution)/shard_map/attend/pallas_call | solution.py:222
  32.2 3.6 %collective-permute-start.5 = (bf16[256,384]{1,0:T(8,128)(2,1)S(1)}, bf16[256,384]{1,0:T(8,128)(2,1)S(1)}, u32[]{:S(2)}, u32[]{:S(2)}) collective-permute-start(bf16[256,384]{1,0:T(8,128)(2,1)S(1)} %collective-permute-done.4.refs_0_), channel_id=1, source_target_pairs={{0,224},{8,40},{16,240},{24,56},{32,0},{40,72},{48,16},{56,88},{64... | collective-permute-start | bytes 589832 | tf_op jit(solution)/shard_map/ppermute | solution.py:39
  35.8 4.5 %attend.6 = bf16[272,384]{1,0:T(8,128)(2,1)S(1)} custom-call(bf16[256,384]{1,0:T(8,128)(2,1)S(1)} %collective-permute-done.4.refs_0_, bf16[2048,384]{1,0:T(8,128)(2,1)S(1)} %copy-done, bf16[2048,384]{1,0:T(8,128)(2,1)S(1)} %collective-permute-done.1.refs_2_, bf16[384,2048]{1,0:T(8,128)(2,1)S(1)} %turn.2.refs_3_, bf16[384,2048]{1,0:T(8,128)(2,1)S(1)} %turn.3.refs_4_), custom_call_target="tpu_custom_call" | custom-call | flops 3221225472 | bytes 6291456 | tf_op jit(solution)/shard_map/attend/pallas_call | solution.py:222
  40.4 2.3 %collective-permute-start.6 = (bf16[256,384]{1,0:T(8,128)(2,1)S(1)}, bf16[256,384]{1,0:T(8,128)(2,1)S(1)}, u32[]{:S(2)}, u32[]{:S(2)}) collective-permute-start(bf16[256,384]{1,0:T(8,128)(2,1)S(1)} %collective-permute-done.5.refs_0_), channel_id=1, source_target_pairs={{0,224},{8,40},{16,240},{24,56},{32,0},{40,72},{48,16},{56,88},{64... | collective-permute-start | bytes 589832 | tf_op jit(solution)/shard_map/ppermute | solution.py:39
  42.8 1.5 %collective-permute-start.8 = (bf16[272,384]{1,0:T(8,128)(2,1)S(1)}, bf16[272,384]{1,0:T(8,128)(2,1)S(1)}, u32[]{:S(2)}, u32[]{:S(2)}) collective-permute-start(bf16[272,384]{1,0:T(8,128)(2,1)S(1)} %attend.6), channel_id=1, source_target_pairs={{0,32},{8,232},{16,48},{24,248},{32,64},{40,8},{48,80},{56,24},{64... | collective-permute-start | bytes 626696 | tf_op jit(solution)/shard_map/ppermute | solution.py:39
  44.2 4.9 %collective-permute-done.6.refs_0_ = bf16[256,384]{1,0:T(8,128)(2,1)S(1)} collective-permute-done((bf16[256,384]{1,0:T(8,128)(2,1)S(1)}, bf16[256,384]{1,0:T(8,128)(2,1)S(1)}, u32[]{:S(2)}, u32[]{:S(2)}) %collective-permute-start.6) | collective-permute-done | bytes 196640 | tf_op jit(solution)/shard_map/ppermute | solution.py:39
  49.1 4.6 %attend.7 = bf16[272,384]{1,0:T(8,128)(2,1)S(1)} custom-call(bf16[256,384]{1,0:T(8,128)(2,1)S(1)} %collective-permute-done.6.refs_0_, bf16[2048,384]{1,0:T(8,128)(2,1)S(1)} %copy-done, bf16[2048,384]{1,0:T(8,128)(2,1)S(1)} %collective-permute-done.1.refs_2_, bf16[384,2048]{1,0:T(8,128)(2,1)S(1)} %turn.2.refs_3_, bf16[384,2048]{1,0:T(8,128)(2,1)S(1)} %turn.3.refs_4_), custom_call_target="tpu_custom_call" | custom-call | flops 3221225472 | bytes 6291456 | tf_op jit(solution)/shard_map/attend/pallas_call | solution.py:222
  53.7 2.8 %attend.8 = bf16[144,384]{1,0:T(8,128)(2,1)S(1)} custom-call(bf16[128,384]{1,0:T(8,128)(2,1)S(1)} %collective-permute-done.7.refs_0_, bf16[2048,384]{1,0:T(8,128)(2,1)S(1)} %copy-done, bf16[2048,384]{1,0:T(8,128)(2,1)S(1)} %collective-permute-done.1.refs_2_, bf16[384,2048]{1,0:T(8,128)(2,1)S(1)} %turn.2.refs_3_, bf16[384,2048]{1,0:T(8,128)(2,1)S(1)} %turn.3.refs_4_), custom_call_target="tpu_custom_call" | custom-call | flops 1610612736 | bytes 6291456 | tf_op jit(solution)/shard_map/attend/pallas_call | solution.py:222
  56.6 1.0 %collective-permute-start.10 = (bf16[144,384]{1,0:T(8,128)(2,1)S(1)}, bf16[144,384]{1,0:T(8,128)(2,1)S(1)}, u32[]{:S(2)}, u32[]{:S(2)}) collective-permute-start(bf16[144,384]{1,0:T(8,128)(2,1)S(1)} %attend.8), channel_id=1, source_target_pairs={{0,128},{8,136},{16,144},{24,152},{32,160},{40,168},{48,176},{56,1... | collective-permute-start | bytes 331784 | tf_op jit(solution)/shard_map/ppermute | solution.py:39
  57.5 3.3 %collective-permute-start.11 = (bf16[272,384]{1,0:T(8,128)(2,1)S(1)}, bf16[272,384]{1,0:T(8,128)(2,1)S(1)}, u32[]{:S(2)}, u32[]{:S(2)}) collective-permute-start(bf16[272,384]{1,0:T(8,128)(2,1)S(1)} %attend.7), channel_id=1, source_target_pairs={{0,96},{8,168},{16,112},{24,184},{32,128},{40,200},{48,144},{56,21... | collective-permute-start | bytes 626696 | tf_op jit(solution)/shard_map/ppermute | solution.py:39
  60.9 4.6 %attend.9 = bf16[272,384]{1,0:T(8,128)(2,1)S(1)} custom-call(bf16[256,384]{1,0:T(8,128)(2,1)S(1)} %collective-permute-done.5.refs_0_, bf16[2048,384]{1,0:T(8,128)(2,1)S(1)} %copy-done, bf16[2048,384]{1,0:T(8,128)(2,1)S(1)} %collective-permute-done.1.refs_2_, bf16[384,2048]{1,0:T(8,128)(2,1)S(1)} %turn.2.refs_3_, bf16[384,2048]{1,0:T(8,128)(2,1)S(1)} %turn.3.refs_4_), custom_call_target="tpu_custom_call" | custom-call | flops 3221225472 | bytes 6291456 | tf_op jit(solution)/shard_map/attend/pallas_call | solution.py:222
  65.5 0.9 collective-permute-start.9
  66.3 2.3 %collective-permute-done.11.refs_3_.refs_2_ = bf16[272,384]{1,0:T(8,128)(2,1)S(1)} collective-permute-done((bf16[272,384]{1,0:T(8,128)(2,1)S(1)}, bf16[272,384]{1,0:T(8,128)(2,1)S(1)}, u32[]{:S(2)}, u32[]{:S(2)}) %collective-permute-start.11) | collective-permute-done | bytes 208928 | tf_op jit(solution)/shard_map/ppermute | solution.py:39
  69.1 5.6 %collective-permute-done.9.refs_1_ = bf16[272,384]{1,0:T(8,128)(2,1)S(1)} collective-permute-done((bf16[272,384]{1,0:T(8,128)(2,1)S(1)}, bf16[272,384]{1,0:T(8,128)(2,1)S(1)}, u32[]{:S(2)}, u32[]{:S(2)}) %collective-permute-start.9) | collective-permute-done | bytes 208928 | tf_op jit(solution)/shard_map/ppermute | solution.py:39
  75.5 1.0 %collective-permute-done.12.refs_1_ = bf16[144,384]{1,0:T(8,128)(2,1)S(1)} collective-permute-done((bf16[144,384]{1,0:T(8,128)(2,1)S(1)}, bf16[144,384]{1,0:T(8,128)(2,1)S(1)}, u32[]{:S(2)}, u32[]{:S(2)}) %collective-permute-start.12) | collective-permute-done | bytes 110624 | tf_op jit(solution)/shard_map/ppermute | solution.py:31
  76.8 0.9 collective-permute-start.13
  77.7 4.9 %collective-permute-done.13.refs_2_ = bf16[80,384]{1,0:T(8,128)(2,1)S(1)} collective-permute-done((bf16[80,384]{1,0:T(8,128)(2,1)S(1)}, bf16[80,384]{1,0:T(8,128)(2,1)S(1)}, u32[]{:S(2)}, u32[]{:S(2)}) %collective-permute-start.13) | collective-permute-done | bytes 61472 | tf_op jit(solution)/shard_map/ppermute | solution.py:31
  83.4 10.6 %all_to_all.11 = bf16[8,8,3072]{2,1,0:T(8,128)(2,1)S(1)} all-to-all(bf16[8,8,3072]{2,1,0:T(8,128)(2,1)S(1)} %bitcast.2), channel_id=1, replica_groups=mesh['ctx'=32,'head'=8] {'head'}, dimensions={0} | all-to-all | bytes 786432 | tf_op jit(solution)/shard_map/all_to_all | solution.py:43
  (35 shorter events, 5.2 us)
Async XLA Ops:
  0.0 22.9 %collective-permute-start.3 = (bf16[2048,384]{1,0:T(8,128)(2,1)}, bf16[2048,384]{1,0:T(8,128)(2,1)S(1)}, u32[]{:S(2)}, u32[]{:S(2)}) collective-permute-start(bf16[2048,384]{1,0:T(8,128)(2,1)} %value.2), channel_id=1, source_target_pairs={{0,8},{8,0},{16,24},{24,16},{32,40},{40,32},{48,56},{56,48},{64,72... | collective-permute-start | bytes 4718600 | tf_op jit(solution)/shard_map/ppermute | solution.py:31
  0.0 29.4 %collective-permute-start.1 = (bf16[2048,384]{1,0:T(8,128)(2,1)}, bf16[2048,384]{1,0:T(8,128)(2,1)S(1)}, u32[]{:S(2)}, u32[]{:S(2)}) collective-permute-start(bf16[2048,384]{1,0:T(8,128)(2,1)} %refs_1_.9), channel_id=1, source_target_pairs={{0,8},{8,0},{16,24},{24,16},{32,40},{40,32},{48,56},{56,48},{64,72... | collective-permute-start | bytes 4718600 | tf_op jit(solution)/shard_map/ppermute | solution.py:31
  0.5 0.8 copy-start.4
  1.3 14.0 %copy-start.1 = (bf16[3072,384]{1,0:T(8,128)(2,1)S(1)}, bf16[3072,384]{1,0:T(8,128)(2,1)}, u32[]{:S(2)}) copy-start(bf16[3072,384]{1,0:T(8,128)(2,1)} %weight.1) | copy-start | bytes 7077892
  15.3 1.4 %copy-start.3 = (bf16[2048,384]{1,0:T(8,128)(2,1)S(1)}, bf16[2048,384]{1,0:T(8,128)(2,1)}, u32[]{:S(2)}) copy-start(bf16[2048,384]{1,0:T(8,128)(2,1)} %value.2) | copy-start | bytes 4718596
  15.8 5.7 %collective-permute-start = (bf16[64,384]{1,0:T(8,128)(2,1)S(1)}, bf16[64,384]{1,0:T(8,128)(2,1)S(1)}, u32[]{:S(2)}, u32[]{:S(2)}) collective-permute-start(bf16[64,384]{1,0:T(8,128)(2,1)S(1)} %project.1), channel_id=1, source_target_pairs={{0,16},{8,24},{16,0},{24,8},{32,48},{40,56},{48,32},{56,40},{64,80... | collective-permute-start | bytes 147464 | tf_op jit(solution)/shard_map/ppermute | solution.py:31
  21.5 1.4 %collective-permute-start.2 = (bf16[128,384]{1,0:T(8,128)(2,1)S(1)}, bf16[128,384]{1,0:T(8,128)(2,1)S(1)}, u32[]{:S(2)}, u32[]{:S(2)}) collective-permute-start(bf16[128,384]{1,0:T(8,128)(2,1)S(1)} %constant_dynamic-update-slice_fusion.refs_0_), channel_id=1, source_target_pairs={{0,8},{8,0},{16,24},{24,16},{32,40},{40,32},{48,56},{56,48},{64,72... | collective-permute-start | bytes 294920 | tf_op jit(solution)/shard_map/ppermute | solution.py:31
  23.0 6.4 %copy-start = (bf16[2048,384]{1,0:T(8,128)(2,1)S(1)}, bf16[2048,384]{1,0:T(8,128)(2,1)}, u32[]{:S(2)}) copy-start(bf16[2048,384]{1,0:T(8,128)(2,1)} %refs_1_.9) | copy-start | bytes 4718596
  23.0 9.3 %collective-permute-start.4 = (bf16[256,384]{1,0:T(8,128)(2,1)S(1)}, bf16[256,384]{1,0:T(8,128)(2,1)S(1)}, u32[]{:S(2)}, u32[]{:S(2)}) collective-permute-start(bf16[256,384]{1,0:T(8,128)(2,1)S(1)} %pad_maximum_fusion), channel_id=1, source_target_pairs={{0,224},{8,40},{16,240},{24,56},{32,0},{40,72},{48,16},{56,88},{64... | collective-permute-start | bytes 589832 | tf_op jit(solution)/shard_map/ppermute | solution.py:39
  32.2 8.1 %collective-permute-start.5 = (bf16[256,384]{1,0:T(8,128)(2,1)S(1)}, bf16[256,384]{1,0:T(8,128)(2,1)S(1)}, u32[]{:S(2)}, u32[]{:S(2)}) collective-permute-start(bf16[256,384]{1,0:T(8,128)(2,1)S(1)} %collective-permute-done.4.refs_0_), channel_id=1, source_target_pairs={{0,224},{8,40},{16,240},{24,56},{32,0},{40,72},{48,16},{56,88},{64... | collective-permute-start | bytes 589832 | tf_op jit(solution)/shard_map/ppermute | solution.py:39
  40.4 8.8 %collective-permute-start.6 = (bf16[256,384]{1,0:T(8,128)(2,1)S(1)}, bf16[256,384]{1,0:T(8,128)(2,1)S(1)}, u32[]{:S(2)}, u32[]{:S(2)}) collective-permute-start(bf16[256,384]{1,0:T(8,128)(2,1)S(1)} %collective-permute-done.5.refs_0_), channel_id=1, source_target_pairs={{0,224},{8,40},{16,240},{24,56},{32,0},{40,72},{48,16},{56,88},{64... | collective-permute-start | bytes 589832 | tf_op jit(solution)/shard_map/ppermute | solution.py:39
  42.7 11.0 %collective-permute-start.7 = (bf16[128,384]{1,0:T(8,128)(2,1)S(1)}, bf16[128,384]{1,0:T(8,128)(2,1)S(1)}, u32[]{:S(2)}, u32[]{:S(2)}) collective-permute-start(bf16[128,384]{1,0:T(8,128)(2,1)S(1)} %slice.3), channel_id=1, source_target_pairs={{0,192},{8,72},{16,208},{24,88},{32,224},{40,104},{48,240},{56,120... | collective-permute-start | bytes 294920 | tf_op jit(solution)/shard_map/ppermute | solution.py:39
  42.8 10.9 %collective-permute-start.8 = (bf16[272,384]{1,0:T(8,128)(2,1)S(1)}, bf16[272,384]{1,0:T(8,128)(2,1)S(1)}, u32[]{:S(2)}, u32[]{:S(2)}) collective-permute-start(bf16[272,384]{1,0:T(8,128)(2,1)S(1)} %attend.6), channel_id=1, source_target_pairs={{0,32},{8,232},{16,48},{24,248},{32,64},{40,8},{48,80},{56,24},{64... | collective-permute-start | bytes 626696 | tf_op jit(solution)/shard_map/ppermute | solution.py:39
  56.6 9.8 %collective-permute-start.10 = (bf16[144,384]{1,0:T(8,128)(2,1)S(1)}, bf16[144,384]{1,0:T(8,128)(2,1)S(1)}, u32[]{:S(2)}, u32[]{:S(2)}) collective-permute-start(bf16[144,384]{1,0:T(8,128)(2,1)S(1)} %attend.8), channel_id=1, source_target_pairs={{0,128},{8,136},{16,144},{24,152},{32,160},{40,168},{48,176},{56,1... | collective-permute-start | bytes 331784 | tf_op jit(solution)/shard_map/ppermute | solution.py:39
  57.5 11.2 %collective-permute-start.11 = (bf16[272,384]{1,0:T(8,128)(2,1)S(1)}, bf16[272,384]{1,0:T(8,128)(2,1)S(1)}, u32[]{:S(2)}, u32[]{:S(2)}) collective-permute-start(bf16[272,384]{1,0:T(8,128)(2,1)S(1)} %attend.7), channel_id=1, source_target_pairs={{0,96},{8,168},{16,112},{24,184},{32,128},{40,200},{48,144},{56,21... | collective-permute-start | bytes 626696 | tf_op jit(solution)/shard_map/ppermute | solution.py:39
  65.5 9.2 %collective-permute-start.9 = (bf16[272,384]{1,0:T(8,128)(2,1)S(1)}, bf16[272,384]{1,0:T(8,128)(2,1)S(1)}, u32[]{:S(2)}, u32[]{:S(2)}) collective-permute-start(bf16[272,384]{1,0:T(8,128)(2,1)S(1)} %attend.9), channel_id=1, source_target_pairs={{0,64},{8,200},{16,80},{24,216},{32,96},{40,232},{48,112},{56,248}... | collective-permute-start | bytes 626696 | tf_op jit(solution)/shard_map/ppermute | solution.py:39
  75.1 1.4 %collective-permute-start.12 = (bf16[144,384]{1,0:T(8,128)(2,1)S(1)}, bf16[144,384]{1,0:T(8,128)(2,1)S(1)}, u32[]{:S(2)}, u32[]{:S(2)}) collective-permute-start(bf16[144,384]{1,0:T(8,128)(2,1)S(1)} %merge.6), channel_id=1, source_target_pairs={{0,8},{8,0},{16,24},{24,16},{32,40},{40,32},{48,56},{56,48},{64,72... | collective-permute-start | bytes 331784 | tf_op jit(solution)/shard_map/ppermute | solution.py:31
  76.5 6.1 %copy-start.2 = (bf16[384,3072]{1,0:T(8,128)(2,1)S(1)}, bf16[384,3072]{1,0:T(8,128)(2,1)}, u32[]{:S(2)}) copy-start(bf16[384,3072]{1,0:T(8,128)(2,1)} %refs_3_.1) | copy-start | bytes 7077892
  76.8 5.8 %collective-permute-start.13 = (bf16[80,384]{1,0:T(8,128)(2,1)S(1)}, bf16[80,384]{1,0:T(8,128)(2,1)S(1)}, u32[]{:S(2)}, u32[]{:S(2)}) collective-permute-start(bf16[80,384]{1,0:T(8,128)(2,1)S(1)} %merge.7), channel_id=1, source_target_pairs={{0,16},{8,24},{16,0},{24,8},{32,48},{40,56},{48,32},{56,40},{64,80... | collective-permute-start | bytes 184328 | tf_op jit(solution)/shard_map/ppermute | solution.py:31

commit v2 on v1

--- a/solution.py
+++ b/solution.py
@@ -143,8 +143,8 @@
         top = highest
         wide = jnp.broadcast_to(top, (8, across))
         for part in range(0, GROUP, BLOCK):
+            total = weigh(step, part, wide, total)
             score_ahead(step + AHEAD, part)
-            total = weigh(step, part, wide, total)
             if part == 0 and pending:
                 add_values(*pending)
         pending = (step, rescale, top, total)
@@ -265,10 +265,10 @@
     return call(turn_kernel, "turn", shape(*value.shape[::-1]), (value,), 0, 4 * value.size)
 
 
-def merge(rows, *places):
+def merge(rows, *places, flops=0):
     parts, starts = zip(*places)
     out_shape = shape(rows + TAIL, parts[0].shape[1])
-    return call(functools.partial(merge_kernel, starts), "merge", out_shape, parts, MERGE_FLOPS)
+    return call(functools.partial(merge_kernel, starts), "merge", out_shape, parts, flops)
 
 
 def finish(parts, weight):
@@ -302,17 +302,19 @@
     part, second = tied(part, second)
     third, far = carry(second, 1), carry(second[: 2 * few], 2)
     back_near = carry(part, -1)
+    part_others, = attend((second[2 * few :],), keys, values)
+    part_others, third, back_near = tied(part_others, third, back_near)
+    back_others = carry(part_others, -2)
     part, = attend((third,), keys, values)
-    part, second, far, back_near = tied(part, second, far, back_near)
+    part, second, far = tied(part, second, far)
     back_third = carry(part, -3)
     part_far, = attend((far,), keys, values)
-    part_far, second = tied(part_far, second)
+    part_far, second, back_others = tied(part_far, second, back_others)
     back_far = carry(part_far, -4)
-    part, = attend((second,), keys, values)
-    early = merge(2 * few, (part_own, 0), (back_far, 0), (back_near, 0), (back_third, 0))
-    back_second, early = tied(carry(part, -2), early)
-    others = merge(2 * few, *[(part, 2 * few) for part in (back_near, back_second, back_third)])
-    others = move(others, dcore=1)
+    part, = attend((second[: 2 * few],), keys, values)
+    early = merge(2 * few, (part_own, 0), (back_far, 0), (back_near, 0), (back_third, 0), flops=MERGE_FLOPS)
+    others = move(merge(2 * few, (back_others, 0), (back_near, 2 * few), (back_third, 2 * few)), dcore=1)
+    back_second, early, others = tied(carry(part, -2), early, others)
     kept = merge(2 * few, (early, 0), (back_second, 0))
     other = move(merge(few, (kept, few), (others, few)), dx=1)
     projected = finish((kept, others, other), out_weight)

time: 96.5 us -> 98.1 us (1.017); the launches traced: 94.7 us -> 97.9 us
  waiting for transfers between devices: 24.4 us -> 26.6 us
  Pallas kernels: 23 us -> 24.1 us
    ppermute x8 -> x9, waiting for transfers between devices: 12.8 us -> 15.5 us  [carry(): return lax.ppermute(value, 'ctx', pairs)]
    pallas_call x14 -> x15, Pallas kernels: 23 us -> 24.1 us  [call(): pl.pallas_call(kernel, out_shape=out_shape, in_specs=[vmem()] * len(opera...]
    ppermute x8 -> x9, starting transfers between devices: 18.5 us -> 18.5 us  [carry(): return lax.ppermute(value, 'ctx', pairs)]
  transfers between devices with their start and end apart: 14 -> 15, of which waited for: 7 -> 7; matrix products, arithmetic and copies ran while one was open for 0% -> 0% of each run, Pallas kernels for 20% -> 23%
where the time goes in v2:
time: 98.1 us; the launch traced here: 97.9 us
  waiting for transfers between devices  26.6 us (27%)
  blocking collectives  24.5 us (25%)
  Pallas kernels  24.1 us (25%)
  starting transfers between devices  20.9 us (21%)
    all_to_all x2, blocking collectives, exchange(): return lax.all_to_all(value, 'head', 0, 0)  24.5 us
    pallas_call x15, Pallas kernels, call(): pl.pallas_call(kernel, out_shape=out_shape, in_specs=[vmem()] * len(opera...  24.1 us
    ppermute x9, starting transfers between devices, carry(): return lax.ppermute(value, 'ctx', pairs)  18.5 us
    ppermute x9, waiting for transfers between devices, carry(): return lax.ppermute(value, 'ctx', pairs)  15.5 us
    ppermute x6, waiting for transfers between devices, move(): return lax.ppermute(value, 'ctx', pairs)  11.1 us
    ppermute x6, starting transfers between devices, move(): return lax.ppermute(value, 'ctx', pairs)  2.46 us
  transfers between devices with their start and end apart: 15, of which 7 were waited for; matrix products, arithmetic and copies ran while one was open for 0% of the time, Pallas kernels for 23%

profile of v2, /device:TPU:4, one launch (start us, length us, event | category | flops | bytes accessed | tf_op | source)
XLA Modules:
  0.0 97.9 jit_solution(12563498773357472064)
XLA Ops:
  0.5 0.8 copy-done.4
  1.3 14.0 %all_to_all.10 = bf16[8,8,3072]{2,1,0:T(8,128)(2,1)S(1)} all-to-all(bf16[8,8,3072]{2,1,0:T(8,128)(2,1)S(1)} %repeat.1), channel_id=1, replica_groups=mesh['ctx'=32,'head'=8] {'head'}, dimensions={0} | all-to-all | bytes 786432 | tf_op jit(solution)/shard_map/all_to_all | solution.py:43
  15.8 0.9 collective-permute-start
  17.2 4.3 %collective-permute-done = bf16[64,384]{1,0:T(8,128)(2,1)S(1)} collective-permute-done((bf16[64,384]{1,0:T(8,128)(2,1)S(1)}, bf16[64,384]{1,0:T(8,128)(2,1)S(1)}, u32[]{:S(2)}, u32[]{:S(2)}) %collective-permute-start) | collective-permute-done | bytes 49184 | tf_op jit(solution)/shard_map/ppermute | solution.py:31
  21.6 1.3 %collective-permute-done.2 = bf16[128,384]{1,0:T(8,128)(2,1)S(1)} collective-permute-done((bf16[128,384]{1,0:T(8,128)(2,1)S(1)}, bf16[128,384]{1,0:T(8,128)(2,1)S(1)}, u32[]{:S(2)}, u32[]{:S(2)}) %collective-permute-start.2) | collective-permute-done | bytes 98336 | tf_op jit(solution)/shard_map/ppermute | solution.py:31
  23.0 5.9 %collective-permute-start.4 = (bf16[256,384]{1,0:T(8,128)(2,1)S(1)}, bf16[256,384]{1,0:T(8,128)(2,1)S(1)}, u32[]{:S(2)}, u32[]{:S(2)}) collective-permute-start(bf16[256,384]{1,0:T(8,128)(2,1)S(1)} %pad_maximum_fusion), channel_id=1, source_target_pairs={{0,224},{8,40},{16,240},{24,56},{32,0},{40,72},{48,16},{56,88},{64... | collective-permute-start | bytes 589832 | tf_op jit(solution)/shard_map/ppermute | solution.py:39
  29.4 2.8 %attend.6.refs_0_ = bf16[144,384]{1,0:T(8,128)(2,1)S(1)} custom-call(bf16[128,384]{1,0:T(8,128)(2,1)S(1)} %constant_dynamic-update-slice_fusion.refs_0_, bf16[2048,384]{1,0:T(8,128)(2,1)S(1)} %copy-done, bf16[2048,384]{1,0:T(8,128)(2,1)S(1)} %collective-permute-done.1.refs_2_, bf16[384,2048]{1,0:T(8,128)(2,1)S(1)} %turn.2.refs_3_, ...), custom_call_target="tpu_custom_call" | custom-call | flops 1610612736 | bytes 6291456 | tf_op jit(solution)/shard_map/attend/pallas_call | solution.py:222
  32.2 3.6 %collective-permute-start.5 = (bf16[256,384]{1,0:T(8,128)(2,1)S(1)}, bf16[256,384]{1,0:T(8,128)(2,1)S(1)}, u32[]{:S(2)}, u32[]{:S(2)}) collective-permute-start(bf16[256,384]{1,0:T(8,128)(2,1)S(1)} %collective-permute-done.4.refs_0_), channel_id=1, source_target_pairs={{0,224},{8,40},{16,240},{24,56},{32,0},{40,72},{48,16},{56,88},{64... | collective-permute-start | bytes 589832 | tf_op jit(solution)/shard_map/ppermute | solution.py:39
  35.8 4.5 %attend.7 = bf16[272,384]{1,0:T(8,128)(2,1)S(1)} custom-call(bf16[256,384]{1,0:T(8,128)(2,1)S(1)} %collective-permute-done.4.refs_0_, bf16[2048,384]{1,0:T(8,128)(2,1)S(1)} %copy-done, bf16[2048,384]{1,0:T(8,128)(2,1)S(1)} %collective-permute-done.1.refs_2_, bf16[384,2048]{1,0:T(8,128)(2,1)S(1)} %turn.2.refs_3_, bf16[384,2048]{1,0:T(8,128)(2,1)S(1)} %turn.3.refs_4_), custom_call_target="tpu_custom_call" | custom-call | flops 3221225472 | bytes 6291456 | tf_op jit(solution)/shard_map/attend/pallas_call | solution.py:222
  40.4 2.3 %collective-permute-start.6 = (bf16[256,384]{1,0:T(8,128)(2,1)S(1)}, bf16[256,384]{1,0:T(8,128)(2,1)S(1)}, u32[]{:S(2)}, u32[]{:S(2)}) collective-permute-start(bf16[256,384]{1,0:T(8,128)(2,1)S(1)} %collective-permute-done.5), channel_id=1, source_target_pairs={{0,224},{8,40},{16,240},{24,56},{32,0},{40,72},{48,16},{56,88},{64... | collective-permute-start | bytes 589832 | tf_op jit(solution)/shard_map/ppermute | solution.py:39
  42.7 1.8 %collective-permute-start.8 = (bf16[128,384]{1,0:T(8,128)(2,1)S(1)}, bf16[128,384]{1,0:T(8,128)(2,1)S(1)}, u32[]{:S(2)}, u32[]{:S(2)}) collective-permute-start(bf16[128,384]{1,0:T(8,128)(2,1)S(1)} %get-tuple-element.49), channel_id=1, source_target_pairs={{0,192},{8,72},{16,208},{24,88},{32,224},{40,104},{48,240},{56,120... | collective-permute-start | bytes 294920 | tf_op jit(solution)/shard_map/ppermute | solution.py:39
  44.5 2.8 %attend.8 = bf16[144,384]{1,0:T(8,128)(2,1)S(1)} custom-call(bf16[128,384]{1,0:T(8,128)(2,1)S(1)} %get-tuple-element.50.refs_0_, bf16[2048,384]{1,0:T(8,128)(2,1)S(1)} %copy-done, bf16[2048,384]{1,0:T(8,128)(2,1)S(1)} %collective-permute-done.1.refs_2_, bf16[384,2048]{1,0:T(8,128)(2,1)S(1)} %turn.2.refs_3_, bf16[384,2048]{1,0:T(8,128)(2,1)S(1)} %turn.3.refs_4_), custom_call_target="tpu_custom_call" | custom-call | flops 1610612736 | bytes 6291456 | tf_op jit(solution)/shard_map/attend/pallas_call | solution.py:222
  47.3 2.4 %collective-permute-done.7.refs_2_.refs_1_ = bf16[272,384]{1,0:T(8,128)(2,1)S(1)} collective-permute-done((bf16[272,384]{1,0:T(8,128)(2,1)S(1)}, bf16[272,384]{1,0:T(8,128)(2,1)S(1)}, u32[]{:S(2)}, u32[]{:S(2)}) %collective-permute-start.7) | collective-permute-done | bytes 208928 | tf_op jit(solution)/shard_map/ppermute | solution.py:39
  49.7 4.6 %attend.9 = bf16[272,384]{1,0:T(8,128)(2,1)S(1)} custom-call(bf16[256,384]{1,0:T(8,128)(2,1)S(1)} %collective-permute-done.6.refs_0_, bf16[2048,384]{1,0:T(8,128)(2,1)S(1)} %copy-done, bf16[2048,384]{1,0:T(8,128)(2,1)S(1)} %collective-permute-done.1.refs_2_, bf16[384,2048]{1,0:T(8,128)(2,1)S(1)} %turn.2.refs_3_, bf16[384,2048]{1,0:T(8,128)(2,1)S(1)} %turn.3.refs_4_), custom_call_target="tpu_custom_call" | custom-call | flops 3221225472 | bytes 6291456 | tf_op jit(solution)/shard_map/attend/pallas_call | solution.py:222
  54.4 2.3 %collective-permute-start.12 = (bf16[272,384]{1,0:T(8,128)(2,1)S(1)}, bf16[272,384]{1,0:T(8,128)(2,1)S(1)}, u32[]{:S(2)}, u32[]{:S(2)}) collective-permute-start(bf16[272,384]{1,0:T(8,128)(2,1)S(1)} %attend.9), channel_id=1, source_target_pairs={{0,96},{8,168},{16,112},{24,184},{32,128},{40,200},{48,144},{56,21... | collective-permute-start | bytes 626696 | tf_op jit(solution)/shard_map/ppermute | solution.py:39
  56.7 2.8 %attend.10 = bf16[144,384]{1,0:T(8,128)(2,1)S(1)} custom-call(bf16[128,384]{1,0:T(8,128)(2,1)S(1)} %collective-permute-done.8.refs_0_, bf16[2048,384]{1,0:T(8,128)(2,1)S(1)} %copy-done, bf16[2048,384]{1,0:T(8,128)(2,1)S(1)} %collective-permute-done.1.refs_2_, bf16[384,2048]{1,0:T(8,128)(2,1)S(1)} %turn.2.refs_3_, bf16[384,2048]{1,0:T(8,128)(2,1)S(1)} %turn.3.refs_4_), custom_call_target="tpu_custom_call" | custom-call | flops 1610612736 | bytes 6291456 | tf_op jit(solution)/shard_map/attend/pallas_call | solution.py:222
  59.5 7.2 %collective-permute-done.9.refs_0_ = bf16[144,384]{1,0:T(8,128)(2,1)S(1)} collective-permute-done((bf16[144,384]{1,0:T(8,128)(2,1)S(1)}, bf16[144,384]{1,0:T(8,128)(2,1)S(1)}, u32[]{:S(2)}, u32[]{:S(2)}) %collective-permute-start.9) | collective-permute-done | bytes 110624 | tf_op jit(solution)/shard_map/ppermute | solution.py:39
  66.7 2.4 %collective-permute-start.11 = (bf16[144,384]{1,0:T(8,128)(2,1)S(1)}, bf16[144,384]{1,0:T(8,128)(2,1)S(1)}, u32[]{:S(2)}, u32[]{:S(2)}) collective-permute-start(bf16[144,384]{1,0:T(8,128)(2,1)S(1)} %attend.10), channel_id=1, source_target_pairs={{0,128},{8,136},{16,144},{24,152},{32,160},{40,168},{48,176},{56,1... | collective-permute-start | bytes 331784 | tf_op jit(solution)/shard_map/ppermute | solution.py:39
  69.2 2.8 %attend.11 = bf16[144,384]{1,0:T(8,128)(2,1)S(1)} custom-call(bf16[128,384]{1,0:T(8,128)(2,1)S(1)} %slice.11.refs_0_, bf16[2048,384]{1,0:T(8,128)(2,1)S(1)} %copy-done, bf16[2048,384]{1,0:T(8,128)(2,1)S(1)} %collective-permute-done.1.refs_2_, bf16[384,2048]{1,0:T(8,128)(2,1)S(1)} %turn.2.refs_3_, bf16[384,2048]{1,0:T(8,128)(2,1)S(1)} %turn.3.refs_4_), custom_call_target="tpu_custom_call" | custom-call | flops 1610612736 | bytes 6291456 | tf_op jit(solution)/shard_map/attend/pallas_call | solution.py:222
  72.6 3.4 %collective-permute-done.11.refs_1_ = bf16[144,384]{1,0:T(8,128)(2,1)S(1)} collective-permute-done((bf16[144,384]{1,0:T(8,128)(2,1)S(1)}, bf16[144,384]{1,0:T(8,128)(2,1)S(1)}, u32[]{:S(2)}, u32[]{:S(2)}) %collective-permute-start.11) | collective-permute-done | bytes 110624 | tf_op jit(solution)/shard_map/ppermute | solution.py:39
  76.4 2.5 %collective-permute-done.10.refs_1_ = bf16[144,384]{1,0:T(8,128)(2,1)S(1)} collective-permute-done((bf16[144,384]{1,0:T(8,128)(2,1)S(1)}, bf16[144,384]{1,0:T(8,128)(2,1)S(1)}, u32[]{:S(2)}, u32[]{:S(2)}) %collective-permute-start.10) | collective-permute-done | bytes 110624 | tf_op jit(solution)/shard_map/ppermute | solution.py:39
  79.6 0.9 collective-permute-start.14
  80.5 5.5 %collective-permute-done.14.refs_2_ = bf16[80,384]{1,0:T(8,128)(2,1)S(1)} collective-permute-done((bf16[80,384]{1,0:T(8,128)(2,1)S(1)}, bf16[80,384]{1,0:T(8,128)(2,1)S(1)}, u32[]{:S(2)}, u32[]{:S(2)}) %collective-permute-start.14) | collective-permute-done | bytes 61472 | tf_op jit(solution)/shard_map/ppermute | solution.py:31
  86.7 10.5 %all_to_all.11 = bf16[8,8,3072]{2,1,0:T(8,128)(2,1)S(1)} all-to-all(bf16[8,8,3072]{2,1,0:T(8,128)(2,1)S(1)} %bitcast.2), channel_id=1, replica_groups=mesh['ctx'=32,'head'=8] {'head'}, dimensions={0} | all-to-all | bytes 786432 | tf_op jit(solution)/shard_map/all_to_all | solution.py:43
  (39 shorter events, 5.3 us)
Async XLA Ops:
  0.0 22.9 %collective-permute-start.3 = (bf16[2048,384]{1,0:T(8,128)(2,1)}, bf16[2048,384]{1,0:T(8,128)(2,1)S(1)}, u32[]{:S(2)}, u32[]{:S(2)}) collective-permute-start(bf16[2048,384]{1,0:T(8,128)(2,1)} %value.2), channel_id=1, source_target_pairs={{0,8},{8,0},{16,24},{24,16},{32,40},{40,32},{48,56},{56,48},{64,72... | collective-permute-start | bytes 4718600 | tf_op jit(solution)/shard_map/ppermute | solution.py:31
  0.0 29.4 %collective-permute-start.1 = (bf16[2048,384]{1,0:T(8,128)(2,1)}, bf16[2048,384]{1,0:T(8,128)(2,1)S(1)}, u32[]{:S(2)}, u32[]{:S(2)}) collective-permute-start(bf16[2048,384]{1,0:T(8,128)(2,1)} %refs_1_.11), channel_id=1, source_target_pairs={{0,8},{8,0},{16,24},{24,16},{32,40},{40,32},{48,56},{56,48},{64,72... | collective-permute-start | bytes 4718600 | tf_op jit(solution)/shard_map/ppermute | solution.py:31
  0.5 0.8 copy-start.4
  1.3 14.0 %copy-start.1 = (bf16[3072,384]{1,0:T(8,128)(2,1)S(1)}, bf16[3072,384]{1,0:T(8,128)(2,1)}, u32[]{:S(2)}) copy-start(bf16[3072,384]{1,0:T(8,128)(2,1)} %weight.1) | copy-start | bytes 7077892
  15.3 1.4 %copy-start.3 = (bf16[2048,384]{1,0:T(8,128)(2,1)S(1)}, bf16[2048,384]{1,0:T(8,128)(2,1)}, u32[]{:S(2)}) copy-start(bf16[2048,384]{1,0:T(8,128)(2,1)} %value.2) | copy-start | bytes 4718596
  15.8 5.7 %collective-permute-start = (bf16[64,384]{1,0:T(8,128)(2,1)S(1)}, bf16[64,384]{1,0:T(8,128)(2,1)S(1)}, u32[]{:S(2)}, u32[]{:S(2)}) collective-permute-start(bf16[64,384]{1,0:T(8,128)(2,1)S(1)} %project.1), channel_id=1, source_target_pairs={{0,16},{8,24},{16,0},{24,8},{32,48},{40,56},{48,32},{56,40},{64,80... | collective-permute-start | bytes 147464 | tf_op jit(solution)/shard_map/ppermute | solution.py:31
  21.5 1.4 %collective-permute-start.2 = (bf16[128,384]{1,0:T(8,128)(2,1)S(1)}, bf16[128,384]{1,0:T(8,128)(2,1)S(1)}, u32[]{:S(2)}, u32[]{:S(2)}) collective-permute-start(bf16[128,384]{1,0:T(8,128)(2,1)S(1)} %constant_dynamic-update-slice_fusion.refs_0_), channel_id=1, source_target_pairs={{0,8},{8,0},{16,24},{24,16},{32,40},{40,32},{48,56},{56,48},{64,72... | collective-permute-start | bytes 294920 | tf_op jit(solution)/shard_map/ppermute | solution.py:31
  23.0 6.4 %copy-start = (bf16[2048,384]{1,0:T(8,128)(2,1)S(1)}, bf16[2048,384]{1,0:T(8,128)(2,1)}, u32[]{:S(2)}) copy-start(bf16[2048,384]{1,0:T(8,128)(2,1)} %refs_1_.11) | copy-start | bytes 4718596
  23.0 9.3 %collective-permute-start.4 = (bf16[256,384]{1,0:T(8,128)(2,1)S(1)}, bf16[256,384]{1,0:T(8,128)(2,1)S(1)}, u32[]{:S(2)}, u32[]{:S(2)}) collective-permute-start(bf16[256,384]{1,0:T(8,128)(2,1)S(1)} %pad_maximum_fusion), channel_id=1, source_target_pairs={{0,224},{8,40},{16,240},{24,56},{32,0},{40,72},{48,16},{56,88},{64... | collective-permute-start | bytes 589832 | tf_op jit(solution)/shard_map/ppermute | solution.py:39
  32.2 8.1 %collective-permute-start.5 = (bf16[256,384]{1,0:T(8,128)(2,1)S(1)}, bf16[256,384]{1,0:T(8,128)(2,1)S(1)}, u32[]{:S(2)}, u32[]{:S(2)}) collective-permute-start(bf16[256,384]{1,0:T(8,128)(2,1)S(1)} %collective-permute-done.4.refs_0_), channel_id=1, source_target_pairs={{0,224},{8,40},{16,240},{24,56},{32,0},{40,72},{48,16},{56,88},{64... | collective-permute-start | bytes 589832 | tf_op jit(solution)/shard_map/ppermute | solution.py:39
  40.4 6.9 %collective-permute-start.6 = (bf16[256,384]{1,0:T(8,128)(2,1)S(1)}, bf16[256,384]{1,0:T(8,128)(2,1)S(1)}, u32[]{:S(2)}, u32[]{:S(2)}) collective-permute-start(bf16[256,384]{1,0:T(8,128)(2,1)S(1)} %collective-permute-done.5), channel_id=1, source_target_pairs={{0,224},{8,40},{16,240},{24,56},{32,0},{40,72},{48,16},{56,88},{64... | collective-permute-start | bytes 589832 | tf_op jit(solution)/shard_map/ppermute | solution.py:39
  42.7 7.0 %collective-permute-start.7 = (bf16[272,384]{1,0:T(8,128)(2,1)S(1)}, bf16[272,384]{1,0:T(8,128)(2,1)S(1)}, u32[]{:S(2)}, u32[]{:S(2)}) collective-permute-start(bf16[272,384]{1,0:T(8,128)(2,1)S(1)} %attend.7), channel_id=1, source_target_pairs={{0,32},{8,232},{16,48},{24,248},{32,64},{40,8},{48,80},{56,24},{64... | collective-permute-start | bytes 626696 | tf_op jit(solution)/shard_map/ppermute | solution.py:39
  42.7 11.6 %collective-permute-start.8 = (bf16[128,384]{1,0:T(8,128)(2,1)S(1)}, bf16[128,384]{1,0:T(8,128)(2,1)S(1)}, u32[]{:S(2)}, u32[]{:S(2)}) collective-permute-start(bf16[128,384]{1,0:T(8,128)(2,1)S(1)} %get-tuple-element.49), channel_id=1, source_target_pairs={{0,192},{8,72},{16,208},{24,88},{32,224},{40,104},{48,240},{56,120... | collective-permute-start | bytes 294920 | tf_op jit(solution)/shard_map/ppermute | solution.py:39
  54.3 12.4 %collective-permute-start.9 = (bf16[144,384]{1,0:T(8,128)(2,1)S(1)}, bf16[144,384]{1,0:T(8,128)(2,1)S(1)}, u32[]{:S(2)}, u32[]{:S(2)}) collective-permute-start(bf16[144,384]{1,0:T(8,128)(2,1)S(1)} %attend.8), channel_id=1, source_target_pairs={{0,64},{8,200},{16,80},{24,216},{32,96},{40,232},{48,112},{56,248}... | collective-permute-start | bytes 331784 | tf_op jit(solution)/shard_map/ppermute | solution.py:39
  54.4 17.7 %collective-permute-start.12 = (bf16[272,384]{1,0:T(8,128)(2,1)S(1)}, bf16[272,384]{1,0:T(8,128)(2,1)S(1)}, u32[]{:S(2)}, u32[]{:S(2)}) collective-permute-start(bf16[272,384]{1,0:T(8,128)(2,1)S(1)} %attend.9), channel_id=1, source_target_pairs={{0,96},{8,168},{16,112},{24,184},{32,128},{40,200},{48,144},{56,21... | collective-permute-start | bytes 626696 | tf_op jit(solution)/shard_map/ppermute | solution.py:39
  66.7 9.2 %collective-permute-start.11 = (bf16[144,384]{1,0:T(8,128)(2,1)S(1)}, bf16[144,384]{1,0:T(8,128)(2,1)S(1)}, u32[]{:S(2)}, u32[]{:S(2)}) collective-permute-start(bf16[144,384]{1,0:T(8,128)(2,1)S(1)} %attend.10), channel_id=1, source_target_pairs={{0,128},{8,136},{16,144},{24,152},{32,160},{40,168},{48,176},{56,1... | collective-permute-start | bytes 331784 | tf_op jit(solution)/shard_map/ppermute | solution.py:39
  72.0 6.9 %collective-permute-start.10 = (bf16[144,384]{1,0:T(8,128)(2,1)S(1)}, bf16[144,384]{1,0:T(8,128)(2,1)S(1)}, u32[]{:S(2)}, u32[]{:S(2)}) collective-permute-start(bf16[144,384]{1,0:T(8,128)(2,1)S(1)} %attend.11), channel_id=1, source_target_pairs={{0,64},{8,200},{16,80},{24,216},{32,96},{40,232},{48,112},{56,248}... | collective-permute-start | bytes 331784 | tf_op jit(solution)/shard_map/ppermute | solution.py:39
  72.5 6.5 %collective-permute-start.13 = (bf16[144,384]{1,0:T(8,128)(2,1)S(1)}, bf16[144,384]{1,0:T(8,128)(2,1)S(1)}, u32[]{:S(2)}, u32[]{:S(2)}) collective-permute-start(bf16[144,384]{1,0:T(8,128)(2,1)S(1)} %merge.5), channel_id=1, source_target_pairs={{0,8},{8,0},{16,24},{24,16},{32,40},{40,32},{48,56},{56,48},{64,72... | collective-permute-start | bytes 331784 | tf_op jit(solution)/shard_map/ppermute | solution.py:31
  75.9 10.0 %copy-start.2 = (bf16[384,3072]{1,0:T(8,128)(2,1)S(1)}, bf16[384,3072]{1,0:T(8,128)(2,1)}, u32[]{:S(2)}) copy-start(bf16[384,3072]{1,0:T(8,128)(2,1)} %refs_3_.1) | copy-start | bytes 7077892
  79.6 6.4 %collective-permute-start.14 = (bf16[80,384]{1,0:T(8,128)(2,1)S(1)}, bf16[80,384]{1,0:T(8,128)(2,1)S(1)}, u32[]{:S(2)}, u32[]{:S(2)}) collective-permute-start(bf16[80,384]{1,0:T(8,128)(2,1)S(1)} %merge.7), channel_id=1, source_target_pairs={{0,16},{8,24},{16,0},{24,8},{32,48},{40,56},{48,32},{56,40},{64,80... | collective-permute-start | bytes 184328 | tf_op jit(solution)/shard_map/ppermute | solution.py:31

commit v3 on v2

--- a/solution.py
+++ b/solution.py
@@ -143,8 +143,8 @@
         top = highest
         wide = jnp.broadcast_to(top, (8, across))
         for part in range(0, GROUP, BLOCK):
+            score_ahead(step + AHEAD, part)
             total = weigh(step, part, wide, total)
-            score_ahead(step + AHEAD, part)
             if part == 0 and pending:
                 add_values(*pending)
         pending = (step, rescale, top, total)
@@ -309,7 +309,7 @@
     part, second, far = tied(part, second, far)
     back_third = carry(part, -3)
     part_far, = attend((far,), keys, values)
-    part_far, second, back_others = tied(part_far, second, back_others)
+    part_far, second = tied(part_far, second)
     back_far = carry(part_far, -4)
     part, = attend((second[: 2 * few],), keys, values)
     early = merge(2 * few, (part_own, 0), (back_far, 0), (back_near, 0), (back_third, 0), flops=MERGE_FLOPS)

time: 98.1 us -> 95.1 us (0.969)
  waiting for transfers between devices: 26.6 us -> 21 us
  starting transfers between devices: 20.9 us -> 23.4 us
    ppermute x9, waiting for transfers between devices: 15.5 us -> 10.3 us  [carry(): return lax.ppermute(value, 'ctx', pairs)]
    ppermute x9, starting transfers between devices: 18.5 us -> 20.9 us  [carry(): return lax.ppermute(value, 'ctx', pairs)]
  transfers between devices with their start and end apart: 15 -> 15, of which waited for: 7 -> 7; matrix products, arithmetic and copies ran while one was open for 0% -> 0% of each run, Pallas kernels for 23% -> 24%
where the time goes in v3:
time: 95.1 us; the launch traced here: 94.8 us
  blocking collectives  24.6 us (26%)
  Pallas kernels  24.1 us (25%)
  starting transfers between devices  23.4 us (25%)
  waiting for transfers between devices  21 us (22%)
    all_to_all x2, blocking collectives, exchange(): return lax.all_to_all(value, 'head', 0, 0)  24.6 us
    pallas_call x15, Pallas kernels, call(): pl.pallas_call(kernel, out_shape=out_shape, in_specs=[vmem()] * len(opera...  24.1 us
    ppermute x9, starting transfers between devices, carry(): return lax.ppermute(value, 'ctx', pairs)  20.9 us
    ppermute x6, waiting for transfers between devices, move(): return lax.ppermute(value, 'ctx', pairs)  10.7 us
    ppermute x9, waiting for transfers between devices, carry(): return lax.ppermute(value, 'ctx', pairs)  10.3 us
    ppermute x6, starting transfers between devices, move(): return lax.ppermute(value, 'ctx', pairs)  2.47 us
  transfers between devices with their start and end apart: 15, of which 7 were waited for; matrix products, arithmetic and copies ran while one was open for 0% of the time, Pallas kernels for 24%

profile of v3, /device:TPU:4, one launch (start us, length us, event | category | flops | bytes accessed | tf_op | source)
XLA Modules:
  0.0 94.8 jit_solution(17683556173417161021)
XLA Ops:
  0.5 0.8 copy-done.4
  1.3 14.0 %all_to_all.10 = bf16[8,8,3072]{2,1,0:T(8,128)(2,1)S(1)} all-to-all(bf16[8,8,3072]{2,1,0:T(8,128)(2,1)S(1)} %repeat.1), channel_id=1, replica_groups=mesh['ctx'=32,'head'=8] {'head'}, dimensions={0} | all-to-all | bytes 786432 | tf_op jit(solution)/shard_map/all_to_all | solution.py:43
  15.8 0.9 collective-permute-start
  17.2 4.3 %collective-permute-done = bf16[64,384]{1,0:T(8,128)(2,1)S(1)} collective-permute-done((bf16[64,384]{1,0:T(8,128)(2,1)S(1)}, bf16[64,384]{1,0:T(8,128)(2,1)S(1)}, u32[]{:S(2)}, u32[]{:S(2)}) %collective-permute-start) | collective-permute-done | bytes 49184 | tf_op jit(solution)/shard_map/ppermute | solution.py:31
  21.6 1.3 %collective-permute-done.2 = bf16[128,384]{1,0:T(8,128)(2,1)S(1)} collective-permute-done((bf16[128,384]{1,0:T(8,128)(2,1)S(1)}, bf16[128,384]{1,0:T(8,128)(2,1)S(1)}, u32[]{:S(2)}, u32[]{:S(2)}) %collective-permute-start.2) | collective-permute-done | bytes 98336 | tf_op jit(solution)/shard_map/ppermute | solution.py:31
  23.0 5.9 %collective-permute-start.4 = (bf16[256,384]{1,0:T(8,128)(2,1)S(1)}, bf16[256,384]{1,0:T(8,128)(2,1)S(1)}, u32[]{:S(2)}, u32[]{:S(2)}) collective-permute-start(bf16[256,384]{1,0:T(8,128)(2,1)S(1)} %pad_maximum_fusion), channel_id=1, source_target_pairs={{0,224},{8,40},{16,240},{24,56},{32,0},{40,72},{48,16},{56,88},{64... | collective-permute-start | bytes 589832 | tf_op jit(solution)/shard_map/ppermute | solution.py:39
  29.4 2.8 %attend.6.refs_0_ = bf16[144,384]{1,0:T(8,128)(2,1)S(1)} custom-call(bf16[128,384]{1,0:T(8,128)(2,1)S(1)} %constant_dynamic-update-slice_fusion.refs_0_, bf16[2048,384]{1,0:T(8,128)(2,1)S(1)} %copy-done, bf16[2048,384]{1,0:T(8,128)(2,1)S(1)} %collective-permute-done.1.refs_2_, bf16[384,2048]{1,0:T(8,128)(2,1)S(1)} %turn.2.refs_3_, ...), custom_call_target="tpu_custom_call" | custom-call | flops 1610612736 | bytes 6291456 | tf_op jit(solution)/shard_map/attend/pallas_call | solution.py:222
  32.2 3.6 %collective-permute-start.5 = (bf16[256,384]{1,0:T(8,128)(2,1)S(1)}, bf16[256,384]{1,0:T(8,128)(2,1)S(1)}, u32[]{:S(2)}, u32[]{:S(2)}) collective-permute-start(bf16[256,384]{1,0:T(8,128)(2,1)S(1)} %collective-permute-done.4.refs_0_), channel_id=1, source_target_pairs={{0,224},{8,40},{16,240},{24,56},{32,0},{40,72},{48,16},{56,88},{64... | collective-permute-start | bytes 589832 | tf_op jit(solution)/shard_map/ppermute | solution.py:39
  35.8 4.5 %attend.7 = bf16[272,384]{1,0:T(8,128)(2,1)S(1)} custom-call(bf16[256,384]{1,0:T(8,128)(2,1)S(1)} %collective-permute-done.4.refs_0_, bf16[2048,384]{1,0:T(8,128)(2,1)S(1)} %copy-done, bf16[2048,384]{1,0:T(8,128)(2,1)S(1)} %collective-permute-done.1.refs_2_, bf16[384,2048]{1,0:T(8,128)(2,1)S(1)} %turn.2.refs_3_, bf16[384,2048]{1,0:T(8,128)(2,1)S(1)} %turn.3.refs_4_), custom_call_target="tpu_custom_call" | custom-call | flops 3221225472 | bytes 6291456 | tf_op jit(solution)/shard_map/attend/pallas_call | solution.py:222
  40.4 2.3 %collective-permute-start.6 = (bf16[256,384]{1,0:T(8,128)(2,1)S(1)}, bf16[256,384]{1,0:T(8,128)(2,1)S(1)}, u32[]{:S(2)}, u32[]{:S(2)}) collective-permute-start(bf16[256,384]{1,0:T(8,128)(2,1)S(1)} %collective-permute-done.5), channel_id=1, source_target_pairs={{0,224},{8,40},{16,240},{24,56},{32,0},{40,72},{48,16},{56,88},{64... | collective-permute-start | bytes 589832 | tf_op jit(solution)/shard_map/ppermute | solution.py:39
  42.7 1.8 %collective-permute-start.8 = (bf16[128,384]{1,0:T(8,128)(2,1)S(1)}, bf16[128,384]{1,0:T(8,128)(2,1)S(1)}, u32[]{:S(2)}, u32[]{:S(2)}) collective-permute-start(bf16[128,384]{1,0:T(8,128)(2,1)S(1)} %get-tuple-element.47), channel_id=1, source_target_pairs={{0,192},{8,72},{16,208},{24,88},{32,224},{40,104},{48,240},{56,120... | collective-permute-start | bytes 294920 | tf_op jit(solution)/shard_map/ppermute | solution.py:39
  44.5 2.8 %attend.8 = bf16[144,384]{1,0:T(8,128)(2,1)S(1)} custom-call(bf16[128,384]{1,0:T(8,128)(2,1)S(1)} %get-tuple-element.48.refs_0_, bf16[2048,384]{1,0:T(8,128)(2,1)S(1)} %copy-done, bf16[2048,384]{1,0:T(8,128)(2,1)S(1)} %collective-permute-done.1.refs_2_, bf16[384,2048]{1,0:T(8,128)(2,1)S(1)} %turn.2.refs_3_, bf16[384,2048]{1,0:T(8,128)(2,1)S(1)} %turn.3.refs_4_), custom_call_target="tpu_custom_call" | custom-call | flops 1610612736 | bytes 6291456 | tf_op jit(solution)/shard_map/attend/pallas_call | solution.py:222
  47.3 2.4 %collective-permute-done.7.refs_2_.refs_1_ = bf16[272,384]{1,0:T(8,128)(2,1)S(1)} collective-permute-done((bf16[272,384]{1,0:T(8,128)(2,1)S(1)}, bf16[272,384]{1,0:T(8,128)(2,1)S(1)}, u32[]{:S(2)}, u32[]{:S(2)}) %collective-permute-start.7) | collective-permute-done | bytes 208928 | tf_op jit(solution)/shard_map/ppermute | solution.py:39
  49.7 4.6 %attend.9 = bf16[272,384]{1,0:T(8,128)(2,1)S(1)} custom-call(bf16[256,384]{1,0:T(8,128)(2,1)S(1)} %collective-permute-done.6.refs_0_, bf16[2048,384]{1,0:T(8,128)(2,1)S(1)} %copy-done, bf16[2048,384]{1,0:T(8,128)(2,1)S(1)} %collective-permute-done.1.refs_2_, bf16[384,2048]{1,0:T(8,128)(2,1)S(1)} %turn.2.refs_3_, bf16[384,2048]{1,0:T(8,128)(2,1)S(1)} %turn.3.refs_4_), custom_call_target="tpu_custom_call" | custom-call | flops 3221225472 | bytes 6291456 | tf_op jit(solution)/shard_map/attend/pallas_call | solution.py:222
  54.3 0.7 collective-permute-start.11
  55.0 2.8 %attend.10 = bf16[144,384]{1,0:T(8,128)(2,1)S(1)} custom-call(bf16[128,384]{1,0:T(8,128)(2,1)S(1)} %collective-permute-done.8.refs_0_, bf16[2048,384]{1,0:T(8,128)(2,1)S(1)} %copy-done, bf16[2048,384]{1,0:T(8,128)(2,1)S(1)} %collective-permute-done.1.refs_2_, bf16[384,2048]{1,0:T(8,128)(2,1)S(1)} %turn.2.refs_3_, bf16[384,2048]{1,0:T(8,128)(2,1)S(1)} %turn.3.refs_4_), custom_call_target="tpu_custom_call" | custom-call | flops 1610612736 | bytes 6291456 | tf_op jit(solution)/shard_map/attend/pallas_call | solution.py:222
  57.8 2.6 %collective-permute-start.10 = (bf16[144,384]{1,0:T(8,128)(2,1)S(1)}, bf16[144,384]{1,0:T(8,128)(2,1)S(1)}, u32[]{:S(2)}, u32[]{:S(2)}) collective-permute-start(bf16[144,384]{1,0:T(8,128)(2,1)S(1)} %attend.10), channel_id=1, source_target_pairs={{0,128},{8,136},{16,144},{24,152},{32,160},{40,168},{48,176},{56,1... | collective-permute-start | bytes 331784 | tf_op jit(solution)/shard_map/ppermute | solution.py:39
  60.4 3.7 %collective-permute-start.12 = (bf16[144,384]{1,0:T(8,128)(2,1)S(1)}, bf16[144,384]{1,0:T(8,128)(2,1)S(1)}, u32[]{:S(2)}, u32[]{:S(2)}) collective-permute-start(bf16[144,384]{1,0:T(8,128)(2,1)S(1)} %attend.8), channel_id=1, source_target_pairs={{0,64},{8,200},{16,80},{24,216},{32,96},{40,232},{48,112},{56,248}... | collective-permute-start | bytes 331784 | tf_op jit(solution)/shard_map/ppermute | solution.py:39
  64.1 2.8 %attend.11 = bf16[144,384]{1,0:T(8,128)(2,1)S(1)} custom-call(bf16[128,384]{1,0:T(8,128)(2,1)S(1)} %slice.11.refs_0_, bf16[2048,384]{1,0:T(8,128)(2,1)S(1)} %copy-done, bf16[2048,384]{1,0:T(8,128)(2,1)S(1)} %collective-permute-done.1.refs_2_, bf16[384,2048]{1,0:T(8,128)(2,1)S(1)} %turn.2.refs_3_, bf16[384,2048]{1,0:T(8,128)(2,1)S(1)} %turn.3.refs_4_), custom_call_target="tpu_custom_call" | custom-call | flops 1610612736 | bytes 6291456 | tf_op jit(solution)/shard_map/attend/pallas_call | solution.py:222
  67.3 7.2 %collective-permute-done.12.refs_0_ = bf16[144,384]{1,0:T(8,128)(2,1)S(1)} collective-permute-done((bf16[144,384]{1,0:T(8,128)(2,1)S(1)}, bf16[144,384]{1,0:T(8,128)(2,1)S(1)}, u32[]{:S(2)}, u32[]{:S(2)}) %collective-permute-start.12) | collective-permute-done | bytes 110624 | tf_op jit(solution)/shard_map/ppermute | solution.py:39
  76.9 0.9 collective-permute-start.14
  77.8 4.9 %collective-permute-done.14.refs_2_ = bf16[80,384]{1,0:T(8,128)(2,1)S(1)} collective-permute-done((bf16[80,384]{1,0:T(8,128)(2,1)S(1)}, bf16[80,384]{1,0:T(8,128)(2,1)S(1)}, u32[]{:S(2)}, u32[]{:S(2)}) %collective-permute-start.14) | collective-permute-done | bytes 61472 | tf_op jit(solution)/shard_map/ppermute | solution.py:31
  82.8 0.7 finish.1
  83.5 10.6 %all_to_all.11 = bf16[8,8,3072]{2,1,0:T(8,128)(2,1)S(1)} all-to-all(bf16[8,8,3072]{2,1,0:T(8,128)(2,1)S(1)} %bitcast.2), channel_id=1, replica_groups=mesh['ctx'=32,'head'=8] {'head'}, dimensions={0} | all-to-all | bytes 786432 | tf_op jit(solution)/shard_map/all_to_all | solution.py:43
  (39 shorter events, 5.6 us)
Async XLA Ops:
  0.0 22.9 %collective-permute-start.3 = (bf16[2048,384]{1,0:T(8,128)(2,1)}, bf16[2048,384]{1,0:T(8,128)(2,1)S(1)}, u32[]{:S(2)}, u32[]{:S(2)}) collective-permute-start(bf16[2048,384]{1,0:T(8,128)(2,1)} %value.2), channel_id=1, source_target_pairs={{0,8},{8,0},{16,24},{24,16},{32,40},{40,32},{48,56},{56,48},{64,72... | collective-permute-start | bytes 4718600 | tf_op jit(solution)/shard_map/ppermute | solution.py:31
  0.0 29.4 %collective-permute-start.1 = (bf16[2048,384]{1,0:T(8,128)(2,1)}, bf16[2048,384]{1,0:T(8,128)(2,1)S(1)}, u32[]{:S(2)}, u32[]{:S(2)}) collective-permute-start(bf16[2048,384]{1,0:T(8,128)(2,1)} %refs_1_.11), channel_id=1, source_target_pairs={{0,8},{8,0},{16,24},{24,16},{32,40},{40,32},{48,56},{56,48},{64,72... | collective-permute-start | bytes 4718600 | tf_op jit(solution)/shard_map/ppermute | solution.py:31
  0.5 0.8 copy-start.4
  1.3 14.0 %copy-start.1 = (bf16[3072,384]{1,0:T(8,128)(2,1)S(1)}, bf16[3072,384]{1,0:T(8,128)(2,1)}, u32[]{:S(2)}) copy-start(bf16[3072,384]{1,0:T(8,128)(2,1)} %weight.1) | copy-start | bytes 7077892
  15.3 1.4 %copy-start.3 = (bf16[2048,384]{1,0:T(8,128)(2,1)S(1)}, bf16[2048,384]{1,0:T(8,128)(2,1)}, u32[]{:S(2)}) copy-start(bf16[2048,384]{1,0:T(8,128)(2,1)} %value.2) | copy-start | bytes 4718596
  15.8 5.7 %collective-permute-start = (bf16[64,384]{1,0:T(8,128)(2,1)S(1)}, bf16[64,384]{1,0:T(8,128)(2,1)S(1)}, u32[]{:S(2)}, u32[]{:S(2)}) collective-permute-start(bf16[64,384]{1,0:T(8,128)(2,1)S(1)} %project.1), channel_id=1, source_target_pairs={{0,16},{8,24},{16,0},{24,8},{32,48},{40,56},{48,32},{56,40},{64,80... | collective-permute-start | bytes 147464 | tf_op jit(solution)/shard_map/ppermute | solution.py:31
  21.5 1.4 %collective-permute-start.2 = (bf16[128,384]{1,0:T(8,128)(2,1)S(1)}, bf16[128,384]{1,0:T(8,128)(2,1)S(1)}, u32[]{:S(2)}, u32[]{:S(2)}) collective-permute-start(bf16[128,384]{1,0:T(8,128)(2,1)S(1)} %constant_dynamic-update-slice_fusion.refs_0_), channel_id=1, source_target_pairs={{0,8},{8,0},{16,24},{24,16},{32,40},{40,32},{48,56},{56,48},{64,72... | collective-permute-start | bytes 294920 | tf_op jit(solution)/shard_map/ppermute | solution.py:31
  23.0 6.4 %copy-start = (bf16[2048,384]{1,0:T(8,128)(2,1)S(1)}, bf16[2048,384]{1,0:T(8,128)(2,1)}, u32[]{:S(2)}) copy-start(bf16[2048,384]{1,0:T(8,128)(2,1)} %refs_1_.11) | copy-start | bytes 4718596
  23.0 9.3 %collective-permute-start.4 = (bf16[256,384]{1,0:T(8,128)(2,1)S(1)}, bf16[256,384]{1,0:T(8,128)(2,1)S(1)}, u32[]{:S(2)}, u32[]{:S(2)}) collective-permute-start(bf16[256,384]{1,0:T(8,128)(2,1)S(1)} %pad_maximum_fusion), channel_id=1, source_target_pairs={{0,224},{8,40},{16,240},{24,56},{32,0},{40,72},{48,16},{56,88},{64... | collective-permute-start | bytes 589832 | tf_op jit(solution)/shard_map/ppermute | solution.py:39
  32.2 8.1 %collective-permute-start.5 = (bf16[256,384]{1,0:T(8,128)(2,1)S(1)}, bf16[256,384]{1,0:T(8,128)(2,1)S(1)}, u32[]{:S(2)}, u32[]{:S(2)}) collective-permute-start(bf16[256,384]{1,0:T(8,128)(2,1)S(1)} %collective-permute-done.4.refs_0_), channel_id=1, source_target_pairs={{0,224},{8,40},{16,240},{24,56},{32,0},{40,72},{48,16},{56,88},{64... | collective-permute-start | bytes 589832 | tf_op jit(solution)/shard_map/ppermute | solution.py:39
  40.4 6.9 %collective-permute-start.6 = (bf16[256,384]{1,0:T(8,128)(2,1)S(1)}, bf16[256,384]{1,0:T(8,128)(2,1)S(1)}, u32[]{:S(2)}, u32[]{:S(2)}) collective-permute-start(bf16[256,384]{1,0:T(8,128)(2,1)S(1)} %collective-permute-done.5), channel_id=1, source_target_pairs={{0,224},{8,40},{16,240},{24,56},{32,0},{40,72},{48,16},{56,88},{64... | collective-permute-start | bytes 589832 | tf_op jit(solution)/shard_map/ppermute | solution.py:39
  42.7 7.0 %collective-permute-start.7 = (bf16[272,384]{1,0:T(8,128)(2,1)S(1)}, bf16[272,384]{1,0:T(8,128)(2,1)S(1)}, u32[]{:S(2)}, u32[]{:S(2)}) collective-permute-start(bf16[272,384]{1,0:T(8,128)(2,1)S(1)} %attend.7), channel_id=1, source_target_pairs={{0,32},{8,232},{16,48},{24,248},{32,64},{40,8},{48,80},{56,24},{64... | collective-permute-start | bytes 626696 | tf_op jit(solution)/shard_map/ppermute | solution.py:39
  42.7 11.6 %collective-permute-start.8 = (bf16[128,384]{1,0:T(8,128)(2,1)S(1)}, bf16[128,384]{1,0:T(8,128)(2,1)S(1)}, u32[]{:S(2)}, u32[]{:S(2)}) collective-permute-start(bf16[128,384]{1,0:T(8,128)(2,1)S(1)} %get-tuple-element.47), channel_id=1, source_target_pairs={{0,192},{8,72},{16,208},{24,88},{32,224},{40,104},{48,240},{56,120... | collective-permute-start | bytes 294920 | tf_op jit(solution)/shard_map/ppermute | solution.py:39
  54.3 20.2 %collective-permute-start.11 = (bf16[272,384]{1,0:T(8,128)(2,1)S(1)}, bf16[272,384]{1,0:T(8,128)(2,1)S(1)}, u32[]{:S(2)}, u32[]{:S(2)}) collective-permute-start(bf16[272,384]{1,0:T(8,128)(2,1)S(1)} %attend.9), channel_id=1, source_target_pairs={{0,96},{8,168},{16,112},{24,184},{32,128},{40,200},{48,144},{56,21... | collective-permute-start | bytes 626696 | tf_op jit(solution)/shard_map/ppermute | solution.py:39
  57.8 17.2 %collective-permute-start.10 = (bf16[144,384]{1,0:T(8,128)(2,1)S(1)}, bf16[144,384]{1,0:T(8,128)(2,1)S(1)}, u32[]{:S(2)}, u32[]{:S(2)}) collective-permute-start(bf16[144,384]{1,0:T(8,128)(2,1)S(1)} %attend.10), channel_id=1, source_target_pairs={{0,128},{8,136},{16,144},{24,152},{32,160},{40,168},{48,176},{56,1... | collective-permute-start | bytes 331784 | tf_op jit(solution)/shard_map/ppermute | solution.py:39
  60.4 14.1 %collective-permute-start.12 = (bf16[144,384]{1,0:T(8,128)(2,1)S(1)}, bf16[144,384]{1,0:T(8,128)(2,1)S(1)}, u32[]{:S(2)}, u32[]{:S(2)}) collective-permute-start(bf16[144,384]{1,0:T(8,128)(2,1)S(1)} %attend.8), channel_id=1, source_target_pairs={{0,64},{8,200},{16,80},{24,216},{32,96},{40,232},{48,112},{56,248}... | collective-permute-start | bytes 331784 | tf_op jit(solution)/shard_map/ppermute | solution.py:39
  66.9 9.2 %collective-permute-start.9 = (bf16[144,384]{1,0:T(8,128)(2,1)S(1)}, bf16[144,384]{1,0:T(8,128)(2,1)S(1)}, u32[]{:S(2)}, u32[]{:S(2)}) collective-permute-start(bf16[144,384]{1,0:T(8,128)(2,1)S(1)} %attend.11), channel_id=1, source_target_pairs={{0,64},{8,200},{16,80},{24,216},{32,96},{40,232},{48,112},{56,248}... | collective-permute-start | bytes 331784 | tf_op jit(solution)/shard_map/ppermute | solution.py:39
  74.9 1.4 %collective-permute-start.13 = (bf16[144,384]{1,0:T(8,128)(2,1)S(1)}, bf16[144,384]{1,0:T(8,128)(2,1)S(1)}, u32[]{:S(2)}, u32[]{:S(2)}) collective-permute-start(bf16[144,384]{1,0:T(8,128)(2,1)S(1)} %merge.5), channel_id=1, source_target_pairs={{0,8},{8,0},{16,24},{24,16},{32,40},{40,32},{48,56},{56,48},{64,72... | collective-permute-start | bytes 331784 | tf_op jit(solution)/shard_map/ppermute | solution.py:31
  75.0 7.8 %copy-start.2 = (bf16[384,3072]{1,0:T(8,128)(2,1)S(1)}, bf16[384,3072]{1,0:T(8,128)(2,1)}, u32[]{:S(2)}) copy-start(bf16[384,3072]{1,0:T(8,128)(2,1)} %refs_3_.1) | copy-start | bytes 7077892
  76.9 5.8 %collective-permute-start.14 = (bf16[80,384]{1,0:T(8,128)(2,1)S(1)}, bf16[80,384]{1,0:T(8,128)(2,1)S(1)}, u32[]{:S(2)}, u32[]{:S(2)}) collective-permute-start(bf16[80,384]{1,0:T(8,128)(2,1)S(1)} %merge.7), channel_id=1, source_target_pairs={{0,16},{8,24},{16,0},{24,8},{32,48},{40,56},{48,32},{56,40},{64,80... | collective-permute-start | bytes 184328 | tf_op jit(solution)/shard_map/ppermute | solution.py:31

commit v4 on v3

--- a/solution.py
+++ b/solution.py
@@ -61,94 +61,90 @@
 
 def attend_kernel(count, *refs):
     asked, (key_a, key_b, value_a, value_b), rest = refs[:count], refs[count : count + 4], refs[count + 4 :]
-    outs, held, weights = rest[:count], rest[count : count + AHEAD + 1], rest[count + AHEAD + 1 :]
+    outs, turned, rest = rest[:count], rest[count], rest[count + 1 :]
     heads = asked[0].shape[1] // HD
     half = key_a.shape[0]
+    groups = 2 * half // GROUP
+    held, weights = rest[:groups], rest[groups:]
     across = sum(ref.shape[0] for ref in asked)
-    steps = [(head, at) for head in range(heads) for at in range(0, 2 * half, GROUP)]
     row = lax.broadcasted_iota(jnp.int32, (TAIL, across), 0)
 
     def columns(head):
-        return slice(head * HD, (head + 1) * HD)
-
-    def turned_queries(head):
-        return jnp.transpose(jnp.concatenate([ref[:, columns(head)] for ref in asked], axis=0))
-
-    queries = [turned_queries(head) for head in range(heads)]
-
-    def score(step, part, peak):
-        head, at = steps[step]
-        keys, place = (key_a, at + part) if at < half else (key_b, at + part - half)
+        return pl.ds(pl.multiple_of(head * HD, HD), HD)
+
+    def score(head, group, part, peak):
+        at = group * GROUP + part
+        keys, place = (key_a, at) if at < half else (key_b, at - half)
         block = LOG2E * jnp.dot(
-            keys[place : place + BLOCK, columns(head)], queries[head], preferred_element_type=jnp.float32
+            keys[place : place + BLOCK, columns(head)], turned[head], preferred_element_type=jnp.float32
         )
-        held[step % len(held)][part : part + BLOCK, :] = block
+        held[group][part : part + BLOCK, :] = block
         top = jnp.max(block.reshape(BLOCK // 8, 8, across), axis=0)
         return top if peak is None else jnp.maximum(peak, top)
 
-    def weigh(step, start, peak, total):
+    def weigh(group, start, peak, total):
         for part in range(start, start + BLOCK, PART):
-            block = held[step % len(held)][part : part + PART, :].reshape(PART // 8, 8, across)
+            block = held[group][part : part + PART, :].reshape(PART // 8, 8, across)
             block = jnp.exp2(block - peak[None])
             total = total + jnp.sum(block, axis=0)
             block = block.reshape(PART, across).astype(jnp.bfloat16)
-            weights[step % 2][part : part + PART, :] = block
+            weights[group % 2][part : part + PART, :] = block
         return total
 
-    def weighted(step):
-        head, at = steps[step]
+    def weighted(head, group):
+        at = group * GROUP
         values, place = (value_a, at) if at < half else (value_b, at - half)
         return jnp.dot(
-            values[columns(head), place : place + GROUP],
-            weights[step % 2][...],
-            preferred_element_type=jnp.float32,
+            values[columns(head), place : place + GROUP], weights[group % 2][...], preferred_element_type=jnp.float32
         )
 
-    stats = jnp.zeros((TAIL, across), jnp.float32)
-    numerator = None
-
-    def add_values(step, rescale, top, total):
-        nonlocal numerator, stats
-        head, at = steps[step]
-        here = weighted(step)
-        numerator = here if at == 0 else numerator * rescale + here
-        if at + GROUP == 2 * half:
-            total = jnp.sum(total, axis=0, keepdims=True)
-            partial = jnp.transpose(numerator / total).astype(jnp.bfloat16)
-            place = 0
-            for ref, out in zip(asked, outs):
-                out[: ref.shape[0], columns(head)] = partial[place : place + ref.shape[0]]
-                place += ref.shape[0]
-            for index, part in enumerate(parts_of(top + LOG2E * jnp.log(total))):
-                stats = jnp.where(row == head * 3 + index, part, stats)
-
-    peaks = [None] * len(steps)
-
-    def score_ahead(step, part):
-        if step < len(steps):
-            peaks[step] = score(step, part, peaks[step])
-
-    for step in range(AHEAD):
+    for head in range(heads):
+        block = jnp.concatenate([ref[:, head * HD : (head + 1) * HD] for ref in asked], axis=0)
+        turned[head] = jnp.transpose(block)
+
+    def one_head(head, carry):
+        *peaks, stats = carry
+        peaks = peaks + [None] * groups
+        after = jnp.minimum(head + 1, heads - 1)
+        top = total = numerator = pending = None
+
+        def add_values(numerator, group, rescale):
+            here = weighted(head, group)
+            return here if numerator is None else numerator * rescale + here
+
+        for group in range(groups):
+            rescale, highest = None, jnp.max(peaks[group], axis=0, keepdims=True)
+            if group:
+                highest = jnp.maximum(top, highest)
+                rescale = jnp.exp2(top - highest)
+                total = total * rescale
+            else:
+                total = jnp.zeros((8, across), jnp.float32)
+            top = highest
+            wide = jnp.broadcast_to(top, (8, across))
+            then = group + AHEAD
+            for part in range(0, GROUP, BLOCK):
+                peaks[then] = score(head if then < groups else after, then % groups, part, peaks[then])
+                total = weigh(group, part, wide, total)
+                if part == 0 and pending:
+                    numerator = add_values(numerator, *pending)
+            pending = (group, rescale)
+        numerator = add_values(numerator, *pending)
+        total = jnp.sum(total, axis=0, keepdims=True)
+        partial = jnp.transpose(numerator / total).astype(jnp.bfloat16)
+        place = 0
+        for ref, out in zip(asked, outs):
+            out[: ref.shape[0], columns(head)] = partial[place : place + ref.shape[0]]
+            place += ref.shape[0]
+        for index, part in enumerate(parts_of(top + LOG2E * jnp.log(total))):
+            stats = jnp.where(row == head * 3 + index, part, stats)
+        return (*peaks[groups:], stats)
+
+    first = [None] * AHEAD
+    for group in range(AHEAD):
         for part in range(0, GROUP, BLOCK):
-            score_ahead(step, part)
-    pending = top = total = None
-    for step, (head, at) in enumerate(steps):
-        rescale, highest = None, jnp.max(peaks[step], axis=0, keepdims=True)
-        if at:
-            highest = jnp.maximum(top, highest)
-            rescale = jnp.exp2(top - highest)
-            total = total * rescale
-        else:
-            total = jnp.zeros((8, across), jnp.float32)
-        top = highest
-        wide = jnp.broadcast_to(top, (8, across))
-        for part in range(0, GROUP, BLOCK):
-            score_ahead(step + AHEAD, part)
-            total = weigh(step, part, wide, total)
-            if part == 0 and pending:
-                add_values(*pending)
-        pending = (step, rescale, top, total)
-    add_values(*pending)
+            first[group] = score(0, group, part, first[group])
+    *_, stats = lax.fori_loop(0, heads, one_head, (*first, jnp.zeros((TAIL, across), jnp.float32)))
     stats = stats.astype(jnp.bfloat16)
     place = 0
     for ref, out in zip(asked, outs):
@@ -250,7 +246,9 @@
     across = sum(queries.shape[0] for queries in asked)
     pairs = 2 * across * keys[0].shape[0] * (width // HD)
     out_shape = [shape(queries.shape[0] + TAIL, width) for queries in asked]
-    scratch = [pltpu.VMEM((GROUP, across), kind) for kind in (jnp.float32,) * (AHEAD + 1) + (jnp.bfloat16,) * 2]
+    groups = 2 * keys[0].shape[0] // GROUP
+    scratch = [pltpu.VMEM((width // HD, HD, across), jnp.bfloat16)]
+    scratch += [pltpu.VMEM((GROUP, across), kind) for kind in (jnp.float32,) * groups + (jnp.bfloat16,) * 2]
     kernel = functools.partial(attend_kernel, len(asked))
     operands = (*asked, *keys, *values)
     return call(kernel, "attend", out_shape, operands, 8 * pairs * HD, 8 * keys[0].size, pairs, 32, scratch)

time: 95.1 us -> 95.2 us (level)
  Pallas kernels: 24.1 us -> 27.6 us
  waiting for transfers between devices: 21 us -> 18.3 us
    pallas_call x15, Pallas kernels: 24.1 us -> 27.6 us  [call(): pl.pallas_call(kernel, out_shape=out_shape, in_specs=[vmem()] * len(opera...]
    ppermute x9, waiting for transfers between devices: 10.3 us -> 7.79 us  [carry(): return lax.ppermute(value, 'ctx', pairs)]
  transfers between devices with their start and end apart: 15 -> 15, of which waited for: 7 -> 6; matrix products, arithmetic and copies ran while one was open for 0% -> 0% of each run, Pallas kernels for 24% -> 28%
where the time goes in v4:
time: 95.2 us; the launch traced here: 94.8 us
  Pallas kernels  27.6 us (29%)
  blocking collectives  24.5 us (26%)
  starting transfers between devices  22.5 us (24%)
  waiting for transfers between devices  18.3 us (19%)
    pallas_call x15, Pallas kernels, call(): pl.pallas_call(kernel, out_shape=out_shape, in_specs=[vmem()] * len(opera...  27.6 us
    all_to_all x2, blocking collectives, exchange(): return lax.all_to_all(value, 'head', 0, 0)  24.5 us
    ppermute x9, starting transfers between devices, carry(): return lax.ppermute(value, 'ctx', pairs)  20.1 us
    ppermute x6, waiting for transfers between devices, move(): return lax.ppermute(value, 'ctx', pairs)  10.5 us
    ppermute x9, waiting for transfers between devices, carry(): return lax.ppermute(value, 'ctx', pairs)  7.79 us
    ppermute x6, starting transfers between devices, move(): return lax.ppermute(value, 'ctx', pairs)  2.47 us
  transfers between devices with their start and end apart: 15, of which 6 were waited for; matrix products, arithmetic and copies ran while one was open for 0% of the time, Pallas kernels for 28%

profile of v4, /device:TPU:4, one launch (start us, length us, event | category | flops | bytes accessed | tf_op | source)
XLA Modules:
  0.0 94.8 jit_solution(13491072331926979525)
XLA Ops:
  0.5 0.8 copy-done.4
  1.3 14.0 %all_to_all.10 = bf16[8,8,3072]{2,1,0:T(8,128)(2,1)S(1)} all-to-all(bf16[8,8,3072]{2,1,0:T(8,128)(2,1)S(1)} %repeat.1), channel_id=1, replica_groups=mesh['ctx'=32,'head'=8] {'head'}, dimensions={0} | all-to-all | bytes 786432 | tf_op jit(solution)/shard_map/all_to_all | solution.py:43
  15.8 0.9 collective-permute-start
  17.2 4.3 %collective-permute-done = bf16[64,384]{1,0:T(8,128)(2,1)S(1)} collective-permute-done((bf16[64,384]{1,0:T(8,128)(2,1)S(1)}, bf16[64,384]{1,0:T(8,128)(2,1)S(1)}, u32[]{:S(2)}, u32[]{:S(2)}) %collective-permute-start) | collective-permute-done | bytes 49184 | tf_op jit(solution)/shard_map/ppermute | solution.py:31
  21.6 1.3 %collective-permute-done.2 = bf16[128,384]{1,0:T(8,128)(2,1)S(1)} collective-permute-done((bf16[128,384]{1,0:T(8,128)(2,1)S(1)}, bf16[128,384]{1,0:T(8,128)(2,1)S(1)}, u32[]{:S(2)}, u32[]{:S(2)}) %collective-permute-start.2) | collective-permute-done | bytes 98336 | tf_op jit(solution)/shard_map/ppermute | solution.py:31
  23.0 5.9 %collective-permute-start.4 = (bf16[256,384]{1,0:T(8,128)(2,1)S(1)}, bf16[256,384]{1,0:T(8,128)(2,1)S(1)}, u32[]{:S(2)}, u32[]{:S(2)}) collective-permute-start(bf16[256,384]{1,0:T(8,128)(2,1)S(1)} %pad_maximum_fusion), channel_id=1, source_target_pairs={{0,224},{8,40},{16,240},{24,56},{32,0},{40,72},{48,16},{56,88},{64... | collective-permute-start | bytes 589832 | tf_op jit(solution)/shard_map/ppermute | solution.py:39
  29.4 3.5 %attend.6.refs_0_ = bf16[144,384]{1,0:T(8,128)(2,1)S(1)} custom-call(bf16[128,384]{1,0:T(8,128)(2,1)S(1)} %constant_dynamic-update-slice_fusion.refs_0_, bf16[2048,384]{1,0:T(8,128)(2,1)S(1)} %copy-done, bf16[2048,384]{1,0:T(8,128)(2,1)S(1)} %collective-permute-done.1.refs_2_, bf16[384,2048]{1,0:T(8,128)(2,1)S(1)} %turn.2.refs_3_, ...), custom_call_target="tpu_custom_call" | custom-call | flops 1610612736 | bytes 6291456 | tf_op jit(solution)/shard_map/attend/pallas_call | solution.py:218
  32.9 2.9 %collective-permute-start.5 = (bf16[256,384]{1,0:T(8,128)(2,1)S(1)}, bf16[256,384]{1,0:T(8,128)(2,1)S(1)}, u32[]{:S(2)}, u32[]{:S(2)}) collective-permute-start(bf16[256,384]{1,0:T(8,128)(2,1)S(1)} %collective-permute-done.4.refs_0_), channel_id=1, source_target_pairs={{0,224},{8,40},{16,240},{24,56},{32,0},{40,72},{48,16},{56,88},{64... | collective-permute-start | bytes 589832 | tf_op jit(solution)/shard_map/ppermute | solution.py:39
  35.8 4.9 %attend.7 = bf16[272,384]{1,0:T(8,128)(2,1)S(1)} custom-call(bf16[256,384]{1,0:T(8,128)(2,1)S(1)} %collective-permute-done.4.refs_0_, bf16[2048,384]{1,0:T(8,128)(2,1)S(1)} %copy-done, bf16[2048,384]{1,0:T(8,128)(2,1)S(1)} %collective-permute-done.1.refs_2_, bf16[384,2048]{1,0:T(8,128)(2,1)S(1)} %turn.2.refs_3_, bf16[384,2048]{1,0:T(8,128)(2,1)S(1)} %turn.3.refs_4_), custom_call_target="tpu_custom_call" | custom-call | flops 3221225472 | bytes 6291456 | tf_op jit(solution)/shard_map/attend/pallas_call | solution.py:218
  40.8 1.9 %collective-permute-start.6 = (bf16[256,384]{1,0:T(8,128)(2,1)S(1)}, bf16[256,384]{1,0:T(8,128)(2,1)S(1)}, u32[]{:S(2)}, u32[]{:S(2)}) collective-permute-start(bf16[256,384]{1,0:T(8,128)(2,1)S(1)} %collective-permute-done.5), channel_id=1, source_target_pairs={{0,224},{8,40},{16,240},{24,56},{32,0},{40,72},{48,16},{56,88},{64... | collective-permute-start | bytes 589832 | tf_op jit(solution)/shard_map/ppermute | solution.py:39
  42.9 1.5 %collective-permute-start.8 = (bf16[128,384]{1,0:T(8,128)(2,1)S(1)}, bf16[128,384]{1,0:T(8,128)(2,1)S(1)}, u32[]{:S(2)}, u32[]{:S(2)}) collective-permute-start(bf16[128,384]{1,0:T(8,128)(2,1)S(1)} %get-tuple-element.47), channel_id=1, source_target_pairs={{0,192},{8,72},{16,208},{24,88},{32,224},{40,104},{48,240},{56,120... | collective-permute-start | bytes 294920 | tf_op jit(solution)/shard_map/ppermute | solution.py:39
  44.4 3.5 %attend.8 = bf16[144,384]{1,0:T(8,128)(2,1)S(1)} custom-call(bf16[128,384]{1,0:T(8,128)(2,1)S(1)} %get-tuple-element.48.refs_0_, bf16[2048,384]{1,0:T(8,128)(2,1)S(1)} %copy-done, bf16[2048,384]{1,0:T(8,128)(2,1)S(1)} %collective-permute-done.1.refs_2_, bf16[384,2048]{1,0:T(8,128)(2,1)S(1)} %turn.2.refs_3_, bf16[384,2048]{1,0:T(8,128)(2,1)S(1)} %turn.3.refs_4_), custom_call_target="tpu_custom_call" | custom-call | flops 1610612736 | bytes 6291456 | tf_op jit(solution)/shard_map/attend/pallas_call | solution.py:218
  48.0 1.8 %collective-permute-done.7.refs_2_.refs_1_ = bf16[272,384]{1,0:T(8,128)(2,1)S(1)} collective-permute-done((bf16[272,384]{1,0:T(8,128)(2,1)S(1)}, bf16[272,384]{1,0:T(8,128)(2,1)S(1)}, u32[]{:S(2)}, u32[]{:S(2)}) %collective-permute-start.7) | collective-permute-done | bytes 208928 | tf_op jit(solution)/shard_map/ppermute | solution.py:39
  49.7 5.0 %attend.9 = bf16[272,384]{1,0:T(8,128)(2,1)S(1)} custom-call(bf16[256,384]{1,0:T(8,128)(2,1)S(1)} %collective-permute-done.6.refs_0_, bf16[2048,384]{1,0:T(8,128)(2,1)S(1)} %copy-done, bf16[2048,384]{1,0:T(8,128)(2,1)S(1)} %collective-permute-done.1.refs_2_, bf16[384,2048]{1,0:T(8,128)(2,1)S(1)} %turn.2.refs_3_, bf16[384,2048]{1,0:T(8,128)(2,1)S(1)} %turn.3.refs_4_), custom_call_target="tpu_custom_call" | custom-call | flops 3221225472 | bytes 6291456 | tf_op jit(solution)/shard_map/attend/pallas_call | solution.py:218
  54.7 0.8 collective-permute-start.11
  55.5 3.5 %attend.10 = bf16[144,384]{1,0:T(8,128)(2,1)S(1)} custom-call(bf16[128,384]{1,0:T(8,128)(2,1)S(1)} %collective-permute-done.8.refs_0_, bf16[2048,384]{1,0:T(8,128)(2,1)S(1)} %copy-done, bf16[2048,384]{1,0:T(8,128)(2,1)S(1)} %collective-permute-done.1.refs_2_, bf16[384,2048]{1,0:T(8,128)(2,1)S(1)} %turn.2.refs_3_, bf16[384,2048]{1,0:T(8,128)(2,1)S(1)} %turn.3.refs_4_), custom_call_target="tpu_custom_call" | custom-call | flops 1610612736 | bytes 6291456 | tf_op jit(solution)/shard_map/attend/pallas_call | solution.py:218
  59.0 2.7 %collective-permute-start.10 = (bf16[144,384]{1,0:T(8,128)(2,1)S(1)}, bf16[144,384]{1,0:T(8,128)(2,1)S(1)}, u32[]{:S(2)}, u32[]{:S(2)}) collective-permute-start(bf16[144,384]{1,0:T(8,128)(2,1)S(1)} %attend.10), channel_id=1, source_target_pairs={{0,128},{8,136},{16,144},{24,152},{32,160},{40,168},{48,176},{56,1... | collective-permute-start | bytes 331784 | tf_op jit(solution)/shard_map/ppermute | solution.py:39
  61.7 4.1 %collective-permute-start.12 = (bf16[144,384]{1,0:T(8,128)(2,1)S(1)}, bf16[144,384]{1,0:T(8,128)(2,1)S(1)}, u32[]{:S(2)}, u32[]{:S(2)}) collective-permute-start(bf16[144,384]{1,0:T(8,128)(2,1)S(1)} %attend.8), channel_id=1, source_target_pairs={{0,64},{8,200},{16,80},{24,216},{32,96},{40,232},{48,112},{56,248}... | collective-permute-start | bytes 331784 | tf_op jit(solution)/shard_map/ppermute | solution.py:39
  65.8 3.5 %attend.11 = bf16[144,384]{1,0:T(8,128)(2,1)S(1)} custom-call(bf16[128,384]{1,0:T(8,128)(2,1)S(1)} %slice.11.refs_0_, bf16[2048,384]{1,0:T(8,128)(2,1)S(1)} %copy-done, bf16[2048,384]{1,0:T(8,128)(2,1)S(1)} %collective-permute-done.1.refs_2_, bf16[384,2048]{1,0:T(8,128)(2,1)S(1)} %turn.2.refs_3_, bf16[384,2048]{1,0:T(8,128)(2,1)S(1)} %turn.3.refs_4_), custom_call_target="tpu_custom_call" | custom-call | flops 1610612736 | bytes 6291456 | tf_op jit(solution)/shard_map/attend/pallas_call | solution.py:218
  69.4 4.8 %collective-permute-done.12.refs_0_ = bf16[144,384]{1,0:T(8,128)(2,1)S(1)} collective-permute-done((bf16[144,384]{1,0:T(8,128)(2,1)S(1)}, bf16[144,384]{1,0:T(8,128)(2,1)S(1)}, u32[]{:S(2)}, u32[]{:S(2)}) %collective-permute-start.12) | collective-permute-done | bytes 110624 | tf_op jit(solution)/shard_map/ppermute | solution.py:39
  75.2 1.2 %collective-permute-done.9.refs_1_ = bf16[144,384]{1,0:T(8,128)(2,1)S(1)} collective-permute-done((bf16[144,384]{1,0:T(8,128)(2,1)S(1)}, bf16[144,384]{1,0:T(8,128)(2,1)S(1)}, u32[]{:S(2)}, u32[]{:S(2)}) %collective-permute-start.9) | collective-permute-done | bytes 110624 | tf_op jit(solution)/shard_map/ppermute | solution.py:39
  77.0 0.9 collective-permute-start.14
  77.9 4.9 %collective-permute-done.14.refs_2_ = bf16[80,384]{1,0:T(8,128)(2,1)S(1)} collective-permute-done((bf16[80,384]{1,0:T(8,128)(2,1)S(1)}, bf16[80,384]{1,0:T(8,128)(2,1)S(1)}, u32[]{:S(2)}, u32[]{:S(2)}) %collective-permute-start.14) | collective-permute-done | bytes 61472 | tf_op jit(solution)/shard_map/ppermute | solution.py:31
  83.6 10.5 %all_to_all.11 = bf16[8,8,3072]{2,1,0:T(8,128)(2,1)S(1)} all-to-all(bf16[8,8,3072]{2,1,0:T(8,128)(2,1)S(1)} %bitcast.2), channel_id=1, replica_groups=mesh['ctx'=32,'head'=8] {'head'}, dimensions={0} | all-to-all | bytes 786432 | tf_op jit(solution)/shard_map/all_to_all | solution.py:43
  (39 shorter events, 5.4 us)
Async XLA Ops:
  0.0 22.9 %collective-permute-start.3 = (bf16[2048,384]{1,0:T(8,128)(2,1)}, bf16[2048,384]{1,0:T(8,128)(2,1)S(1)}, u32[]{:S(2)}, u32[]{:S(2)}) collective-permute-start(bf16[2048,384]{1,0:T(8,128)(2,1)} %value.2), channel_id=1, source_target_pairs={{0,8},{8,0},{16,24},{24,16},{32,40},{40,32},{48,56},{56,48},{64,72... | collective-permute-start | bytes 4718600 | tf_op jit(solution)/shard_map/ppermute | solution.py:31
  0.0 29.4 %collective-permute-start.1 = (bf16[2048,384]{1,0:T(8,128)(2,1)}, bf16[2048,384]{1,0:T(8,128)(2,1)S(1)}, u32[]{:S(2)}, u32[]{:S(2)}) collective-permute-start(bf16[2048,384]{1,0:T(8,128)(2,1)} %refs_1_.11), channel_id=1, source_target_pairs={{0,8},{8,0},{16,24},{24,16},{32,40},{40,32},{48,56},{56,48},{64,72... | collective-permute-start | bytes 4718600 | tf_op jit(solution)/shard_map/ppermute | solution.py:31
  0.5 0.8 copy-start.4
  1.3 14.0 %copy-start.1 = (bf16[3072,384]{1,0:T(8,128)(2,1)S(1)}, bf16[3072,384]{1,0:T(8,128)(2,1)}, u32[]{:S(2)}) copy-start(bf16[3072,384]{1,0:T(8,128)(2,1)} %weight.1) | copy-start | bytes 7077892
  15.3 1.4 %copy-start.3 = (bf16[2048,384]{1,0:T(8,128)(2,1)S(1)}, bf16[2048,384]{1,0:T(8,128)(2,1)}, u32[]{:S(2)}) copy-start(bf16[2048,384]{1,0:T(8,128)(2,1)} %value.2) | copy-start | bytes 4718596
  15.8 5.7 %collective-permute-start = (bf16[64,384]{1,0:T(8,128)(2,1)S(1)}, bf16[64,384]{1,0:T(8,128)(2,1)S(1)}, u32[]{:S(2)}, u32[]{:S(2)}) collective-permute-start(bf16[64,384]{1,0:T(8,128)(2,1)S(1)} %project.1), channel_id=1, source_target_pairs={{0,16},{8,24},{16,0},{24,8},{32,48},{40,56},{48,32},{56,40},{64,80... | collective-permute-start | bytes 147464 | tf_op jit(solution)/shard_map/ppermute | solution.py:31
  21.5 1.4 %collective-permute-start.2 = (bf16[128,384]{1,0:T(8,128)(2,1)S(1)}, bf16[128,384]{1,0:T(8,128)(2,1)S(1)}, u32[]{:S(2)}, u32[]{:S(2)}) collective-permute-start(bf16[128,384]{1,0:T(8,128)(2,1)S(1)} %constant_dynamic-update-slice_fusion.refs_0_), channel_id=1, source_target_pairs={{0,8},{8,0},{16,24},{24,16},{32,40},{40,32},{48,56},{56,48},{64,72... | collective-permute-start | bytes 294920 | tf_op jit(solution)/shard_map/ppermute | solution.py:31
  23.0 6.4 %copy-start = (bf16[2048,384]{1,0:T(8,128)(2,1)S(1)}, bf16[2048,384]{1,0:T(8,128)(2,1)}, u32[]{:S(2)}) copy-start(bf16[2048,384]{1,0:T(8,128)(2,1)} %refs_1_.11) | copy-start | bytes 4718596
  23.0 9.9 %collective-permute-start.4 = (bf16[256,384]{1,0:T(8,128)(2,1)S(1)}, bf16[256,384]{1,0:T(8,128)(2,1)S(1)}, u32[]{:S(2)}, u32[]{:S(2)}) collective-permute-start(bf16[256,384]{1,0:T(8,128)(2,1)S(1)} %pad_maximum_fusion), channel_id=1, source_target_pairs={{0,224},{8,40},{16,240},{24,56},{32,0},{40,72},{48,16},{56,88},{64... | collective-permute-start | bytes 589832 | tf_op jit(solution)/shard_map/ppermute | solution.py:39
  32.9 7.8 %collective-permute-start.5 = (bf16[256,384]{1,0:T(8,128)(2,1)S(1)}, bf16[256,384]{1,0:T(8,128)(2,1)S(1)}, u32[]{:S(2)}, u32[]{:S(2)}) collective-permute-start(bf16[256,384]{1,0:T(8,128)(2,1)S(1)} %collective-permute-done.4.refs_0_), channel_id=1, source_target_pairs={{0,224},{8,40},{16,240},{24,56},{32,0},{40,72},{48,16},{56,88},{64... | collective-permute-start | bytes 589832 | tf_op jit(solution)/shard_map/ppermute | solution.py:39
  40.8 7.2 %collective-permute-start.6 = (bf16[256,384]{1,0:T(8,128)(2,1)S(1)}, bf16[256,384]{1,0:T(8,128)(2,1)S(1)}, u32[]{:S(2)}, u32[]{:S(2)}) collective-permute-start(bf16[256,384]{1,0:T(8,128)(2,1)S(1)} %collective-permute-done.5), channel_id=1, source_target_pairs={{0,224},{8,40},{16,240},{24,56},{32,0},{40,72},{48,16},{56,88},{64... | collective-permute-start | bytes 589832 | tf_op jit(solution)/shard_map/ppermute | solution.py:39
  42.7 7.1 %collective-permute-start.7 = (bf16[272,384]{1,0:T(8,128)(2,1)S(1)}, bf16[272,384]{1,0:T(8,128)(2,1)S(1)}, u32[]{:S(2)}, u32[]{:S(2)}) collective-permute-start(bf16[272,384]{1,0:T(8,128)(2,1)S(1)} %attend.7), channel_id=1, source_target_pairs={{0,32},{8,232},{16,48},{24,248},{32,64},{40,8},{48,80},{56,24},{64... | collective-permute-start | bytes 626696 | tf_op jit(solution)/shard_map/ppermute | solution.py:39
  42.9 11.8 %collective-permute-start.8 = (bf16[128,384]{1,0:T(8,128)(2,1)S(1)}, bf16[128,384]{1,0:T(8,128)(2,1)S(1)}, u32[]{:S(2)}, u32[]{:S(2)}) collective-permute-start(bf16[128,384]{1,0:T(8,128)(2,1)S(1)} %get-tuple-element.47), channel_id=1, source_target_pairs={{0,192},{8,72},{16,208},{24,88},{32,224},{40,104},{48,240},{56,120... | collective-permute-start | bytes 294920 | tf_op jit(solution)/shard_map/ppermute | solution.py:39
  54.7 19.5 %collective-permute-start.11 = (bf16[272,384]{1,0:T(8,128)(2,1)S(1)}, bf16[272,384]{1,0:T(8,128)(2,1)S(1)}, u32[]{:S(2)}, u32[]{:S(2)}) collective-permute-start(bf16[272,384]{1,0:T(8,128)(2,1)S(1)} %attend.9), channel_id=1, source_target_pairs={{0,96},{8,168},{16,112},{24,184},{32,128},{40,200},{48,144},{56,21... | collective-permute-start | bytes 626696 | tf_op jit(solution)/shard_map/ppermute | solution.py:39
  59.0 15.7 %collective-permute-start.10 = (bf16[144,384]{1,0:T(8,128)(2,1)S(1)}, bf16[144,384]{1,0:T(8,128)(2,1)S(1)}, u32[]{:S(2)}, u32[]{:S(2)}) collective-permute-start(bf16[144,384]{1,0:T(8,128)(2,1)S(1)} %attend.10), channel_id=1, source_target_pairs={{0,128},{8,136},{16,144},{24,152},{32,160},{40,168},{48,176},{56,1... | collective-permute-start | bytes 331784 | tf_op jit(solution)/shard_map/ppermute | solution.py:39
  61.7 12.5 %collective-permute-start.12 = (bf16[144,384]{1,0:T(8,128)(2,1)S(1)}, bf16[144,384]{1,0:T(8,128)(2,1)S(1)}, u32[]{:S(2)}, u32[]{:S(2)}) collective-permute-start(bf16[144,384]{1,0:T(8,128)(2,1)S(1)} %attend.8), channel_id=1, source_target_pairs={{0,64},{8,200},{16,80},{24,216},{32,96},{40,232},{48,112},{56,248}... | collective-permute-start | bytes 331784 | tf_op jit(solution)/shard_map/ppermute | solution.py:39
  69.3 7.0 %collective-permute-start.9 = (bf16[144,384]{1,0:T(8,128)(2,1)S(1)}, bf16[144,384]{1,0:T(8,128)(2,1)S(1)}, u32[]{:S(2)}, u32[]{:S(2)}) collective-permute-start(bf16[144,384]{1,0:T(8,128)(2,1)S(1)} %attend.11), channel_id=1, source_target_pairs={{0,64},{8,200},{16,80},{24,216},{32,96},{40,232},{48,112},{56,248}... | collective-permute-start | bytes 331784 | tf_op jit(solution)/shard_map/ppermute | solution.py:39
  74.6 1.8 %collective-permute-start.13 = (bf16[144,384]{1,0:T(8,128)(2,1)S(1)}, bf16[144,384]{1,0:T(8,128)(2,1)S(1)}, u32[]{:S(2)}, u32[]{:S(2)}) collective-permute-start(bf16[144,384]{1,0:T(8,128)(2,1)S(1)} %merge.5), channel_id=1, source_target_pairs={{0,8},{8,0},{16,24},{24,16},{32,40},{40,32},{48,56},{56,48},{64,72... | collective-permute-start | bytes 331784 | tf_op jit(solution)/shard_map/ppermute | solution.py:31
  74.7 8.1 %copy-start.2 = (bf16[384,3072]{1,0:T(8,128)(2,1)S(1)}, bf16[384,3072]{1,0:T(8,128)(2,1)}, u32[]{:S(2)}) copy-start(bf16[384,3072]{1,0:T(8,128)(2,1)} %refs_3_.1) | copy-start | bytes 7077892
  77.0 5.8 %collective-permute-start.14 = (bf16[80,384]{1,0:T(8,128)(2,1)S(1)}, bf16[80,384]{1,0:T(8,128)(2,1)S(1)}, u32[]{:S(2)}, u32[]{:S(2)}) collective-permute-start(bf16[80,384]{1,0:T(8,128)(2,1)S(1)} %merge.7), channel_id=1, source_target_pairs={{0,16},{8,24},{16,0},{24,8},{32,48},{40,56},{48,32},{56,40},{64,80... | collective-permute-start | bytes 184328 | tf_op jit(solution)/shard_map/ppermute | solution.py:31

commit v5 on v3

--- a/solution.py
+++ b/solution.py
@@ -35,7 +35,7 @@
     pairs = []
     for source in range(Z * 4):
         z, core = source // 4, source % 2
-        pairs.append((source, (z + (steps if core else -steps)) % Z * 4 + source % 4))
+        pairs.append((source, (z + (-steps if core else steps)) % Z * 4 + source % 4))
     return lax.ppermute(value, "ctx", pairs)
 
 
@@ -306,7 +306,7 @@
     part_others, third, back_near = tied(part_others, third, back_near)
     back_others = carry(part_others, -2)
     part, = attend((third,), keys, values)
-    part, second, far = tied(part, second, far)
+    part, second, far, back_others = tied(part, second, far, back_others)
     back_third = carry(part, -3)
     part_far, = attend((far,), keys, values)
     part_far, second = tied(part_far, second)

time: 95.1 us -> 94.4 us (level)
  the two profiles are of different devices: /device:TPU:4 before, /device:TPU:64 now
where the time goes in v5:
time: 94.4 us; the launch traced here: 94.1 us
  starting transfers between devices  25.4 us (27%)
  blocking collectives  24.8 us (26%)
  Pallas kernels  24.1 us (26%)
  waiting for transfers between devices  18.1 us (19%)
    all_to_all x2, blocking collectives, exchange(): return lax.all_to_all(value, 'head', 0, 0)  24.8 us
    pallas_call x15, Pallas kernels, call(): pl.pallas_call(kernel, out_shape=out_shape, in_specs=[vmem()] * len(opera...  24.1 us
    ppermute x9, starting transfers between devices, carry(): return lax.ppermute(value, 'ctx', pairs)  19 us
    ppermute x9, waiting for transfers between devices, carry(): return lax.ppermute(value, 'ctx', pairs)  11.5 us
    ppermute x6, waiting for transfers between devices, move(): return lax.ppermute(value, 'ctx', pairs)  6.66 us
    ppermute x6, starting transfers between devices, move(): return lax.ppermute(value, 'ctx', pairs)  6.35 us
  transfers between devices with their start and end apart: 15, of which 8 were waited for; matrix products, arithmetic and copies ran while one was open for 0% of the time, Pallas kernels for 24%

profile of v5, /device:TPU:64, one launch (start us, length us, event | category | flops | bytes accessed | tf_op | source)
XLA Modules:
  0.0 94.1 jit_solution(9774140355094083641)
XLA Ops:
  0.5 0.8 copy-done.4
  1.3 14.3 %all_to_all.10 = bf16[8,8,3072]{2,1,0:T(8,128)(2,1)S(1)} all-to-all(bf16[8,8,3072]{2,1,0:T(8,128)(2,1)S(1)} %repeat.1), channel_id=1, replica_groups=mesh['ctx'=32,'head'=8] {'head'}, dimensions={0} | all-to-all | bytes 786432 | tf_op jit(solution)/shard_map/all_to_all | solution.py:43
  16.1 2.8 %collective-permute-start = (bf16[64,384]{1,0:T(8,128)(2,1)S(1)}, bf16[64,384]{1,0:T(8,128)(2,1)S(1)}, u32[]{:S(2)}, u32[]{:S(2)}) collective-permute-start(bf16[64,384]{1,0:T(8,128)(2,1)S(1)} %project.1), channel_id=1, source_target_pairs={{0,16},{8,24},{16,0},{24,8},{32,48},{40,56},{48,32},{56,40},{64,80... | collective-permute-start | bytes 147464 | tf_op jit(solution)/shard_map/ppermute | solution.py:31
  19.4 2.4 %collective-permute-done = bf16[64,384]{1,0:T(8,128)(2,1)S(1)} collective-permute-done((bf16[64,384]{1,0:T(8,128)(2,1)S(1)}, bf16[64,384]{1,0:T(8,128)(2,1)S(1)}, u32[]{:S(2)}, u32[]{:S(2)}) %collective-permute-start) | collective-permute-done | bytes 49184 | tf_op jit(solution)/shard_map/ppermute | solution.py:31
  21.9 1.3 %collective-permute-done.2 = bf16[128,384]{1,0:T(8,128)(2,1)S(1)} collective-permute-done((bf16[128,384]{1,0:T(8,128)(2,1)S(1)}, bf16[128,384]{1,0:T(8,128)(2,1)S(1)}, u32[]{:S(2)}, u32[]{:S(2)}) %collective-permute-start.2) | collective-permute-done | bytes 98336 | tf_op jit(solution)/shard_map/ppermute | solution.py:31
  23.3 2.0 %collective-permute-start.4 = (bf16[256,384]{1,0:T(8,128)(2,1)S(1)}, bf16[256,384]{1,0:T(8,128)(2,1)S(1)}, u32[]{:S(2)}, u32[]{:S(2)}) collective-permute-start(bf16[256,384]{1,0:T(8,128)(2,1)S(1)} %pad_maximum_fusion), channel_id=1, source_target_pairs={{0,32},{8,232},{16,48},{24,248},{32,64},{40,8},{48,80},{56,24},{64... | collective-permute-start | bytes 589832 | tf_op jit(solution)/shard_map/ppermute | solution.py:39
  25.7 2.8 %attend.6.refs_0_ = bf16[144,384]{1,0:T(8,128)(2,1)S(1)} custom-call(bf16[128,384]{1,0:T(8,128)(2,1)S(1)} %constant_dynamic-update-slice_fusion.refs_0_, bf16[2048,384]{1,0:T(8,128)(2,1)S(1)} %copy-done, bf16[2048,384]{1,0:T(8,128)(2,1)S(1)} %collective-permute-done.1.refs_2_, bf16[384,2048]{1,0:T(8,128)(2,1)S(1)} %turn.2.refs_3_, ...), custom_call_target="tpu_custom_call" | custom-call | flops 1610612736 | bytes 6291456 | tf_op jit(solution)/shard_map/attend/pallas_call | solution.py:222
  29.0 3.0 %collective-permute-start.5 = (bf16[256,384]{1,0:T(8,128)(2,1)S(1)}, bf16[256,384]{1,0:T(8,128)(2,1)S(1)}, u32[]{:S(2)}, u32[]{:S(2)}) collective-permute-start(bf16[256,384]{1,0:T(8,128)(2,1)S(1)} %collective-permute-done.4.refs_0_), channel_id=1, source_target_pairs={{0,32},{8,232},{16,48},{24,248},{32,64},{40,8},{48,80},{56,24},{64... | collective-permute-start | bytes 589832 | tf_op jit(solution)/shard_map/ppermute | solution.py:39
  32.0 4.6 %attend.7 = bf16[272,384]{1,0:T(8,128)(2,1)S(1)} custom-call(bf16[256,384]{1,0:T(8,128)(2,1)S(1)} %collective-permute-done.4.refs_0_, bf16[2048,384]{1,0:T(8,128)(2,1)S(1)} %copy-done, bf16[2048,384]{1,0:T(8,128)(2,1)S(1)} %collective-permute-done.1.refs_2_, bf16[384,2048]{1,0:T(8,128)(2,1)S(1)} %turn.2.refs_3_, bf16[384,2048]{1,0:T(8,128)(2,1)S(1)} %turn.3.refs_4_), custom_call_target="tpu_custom_call" | custom-call | flops 3221225472 | bytes 6291456 | tf_op jit(solution)/shard_map/attend/pallas_call | solution.py:222
  36.5 3.4 %collective-permute-start.6 = (bf16[256,384]{1,0:T(8,128)(2,1)S(1)}, bf16[256,384]{1,0:T(8,128)(2,1)S(1)}, u32[]{:S(2)}, u32[]{:S(2)}) collective-permute-start(bf16[256,384]{1,0:T(8,128)(2,1)S(1)} %collective-permute-done.5), channel_id=1, source_target_pairs={{0,32},{8,232},{16,48},{24,248},{32,64},{40,8},{48,80},{56,24},{64... | collective-permute-start | bytes 589832 | tf_op jit(solution)/shard_map/ppermute | solution.py:39
  39.9 5.0 %collective-permute-start.8 = (bf16[128,384]{1,0:T(8,128)(2,1)S(1)}, bf16[128,384]{1,0:T(8,128)(2,1)S(1)}, u32[]{:S(2)}, u32[]{:S(2)}) collective-permute-start(bf16[128,384]{1,0:T(8,128)(2,1)S(1)} %get-tuple-element.49), channel_id=1, source_target_pairs={{0,64},{8,200},{16,80},{24,216},{32,96},{40,232},{48,112},{56,248}... | collective-permute-start | bytes 294920 | tf_op jit(solution)/shard_map/ppermute | solution.py:39
  45.0 2.8 %attend.8 = bf16[144,384]{1,0:T(8,128)(2,1)S(1)} custom-call(bf16[128,384]{1,0:T(8,128)(2,1)S(1)} %get-tuple-element.50.refs_0_, bf16[2048,384]{1,0:T(8,128)(2,1)S(1)} %copy-done, bf16[2048,384]{1,0:T(8,128)(2,1)S(1)} %collective-permute-done.1.refs_2_, bf16[384,2048]{1,0:T(8,128)(2,1)S(1)} %turn.2.refs_3_, bf16[384,2048]{1,0:T(8,128)(2,1)S(1)} %turn.3.refs_4_), custom_call_target="tpu_custom_call" | custom-call | flops 1610612736 | bytes 6291456 | tf_op jit(solution)/shard_map/attend/pallas_call | solution.py:222
  48.3 4.6 %attend.9 = bf16[272,384]{1,0:T(8,128)(2,1)S(1)} custom-call(bf16[256,384]{1,0:T(8,128)(2,1)S(1)} %collective-permute-done.6.refs_0_, bf16[2048,384]{1,0:T(8,128)(2,1)S(1)} %copy-done, bf16[2048,384]{1,0:T(8,128)(2,1)S(1)} %collective-permute-done.1.refs_2_, bf16[384,2048]{1,0:T(8,128)(2,1)S(1)} %turn.2.refs_3_, bf16[384,2048]{1,0:T(8,128)(2,1)S(1)} %turn.3.refs_4_), custom_call_target="tpu_custom_call" | custom-call | flops 3221225472 | bytes 6291456 | tf_op jit(solution)/shard_map/attend/pallas_call | solution.py:222
  53.0 3.2 %collective-permute-done.9.refs_0_ = bf16[144,384]{1,0:T(8,128)(2,1)S(1)} collective-permute-done((bf16[144,384]{1,0:T(8,128)(2,1)S(1)}, bf16[144,384]{1,0:T(8,128)(2,1)S(1)}, u32[]{:S(2)}, u32[]{:S(2)}) %collective-permute-start.9) | collective-permute-done | bytes 110624 | tf_op jit(solution)/shard_map/ppermute | solution.py:39
  56.1 1.4 %collective-permute-start.12 = (bf16[272,384]{1,0:T(8,128)(2,1)S(1)}, bf16[272,384]{1,0:T(8,128)(2,1)S(1)}, u32[]{:S(2)}, u32[]{:S(2)}) collective-permute-start(bf16[272,384]{1,0:T(8,128)(2,1)S(1)} %attend.9), channel_id=1, source_target_pairs={{0,160},{8,104},{16,176},{24,120},{32,192},{40,136},{48,208},{56,1... | collective-permute-start | bytes 626696 | tf_op jit(solution)/shard_map/ppermute | solution.py:39
  57.6 2.8 %attend.10 = bf16[144,384]{1,0:T(8,128)(2,1)S(1)} custom-call(bf16[128,384]{1,0:T(8,128)(2,1)S(1)} %collective-permute-done.8.refs_0_, bf16[2048,384]{1,0:T(8,128)(2,1)S(1)} %copy-done, bf16[2048,384]{1,0:T(8,128)(2,1)S(1)} %collective-permute-done.1.refs_2_, bf16[384,2048]{1,0:T(8,128)(2,1)S(1)} %turn.2.refs_3_, bf16[384,2048]{1,0:T(8,128)(2,1)S(1)} %turn.3.refs_4_), custom_call_target="tpu_custom_call" | custom-call | flops 1610612736 | bytes 6291456 | tf_op jit(solution)/shard_map/attend/pallas_call | solution.py:222
  60.4 3.5 %collective-permute-start.11 = (bf16[144,384]{1,0:T(8,128)(2,1)S(1)}, bf16[144,384]{1,0:T(8,128)(2,1)S(1)}, u32[]{:S(2)}, u32[]{:S(2)}) collective-permute-start(bf16[144,384]{1,0:T(8,128)(2,1)S(1)} %attend.10), channel_id=1, source_target_pairs={{0,128},{8,136},{16,144},{24,152},{32,160},{40,168},{48,176},{56,1... | collective-permute-start | bytes 331784 | tf_op jit(solution)/shard_map/ppermute | solution.py:39
  64.0 2.8 %attend.11 = bf16[144,384]{1,0:T(8,128)(2,1)S(1)} custom-call(bf16[128,384]{1,0:T(8,128)(2,1)S(1)} %slice.11.refs_0_, bf16[2048,384]{1,0:T(8,128)(2,1)S(1)} %copy-done, bf16[2048,384]{1,0:T(8,128)(2,1)S(1)} %collective-permute-done.1.refs_2_, bf16[384,2048]{1,0:T(8,128)(2,1)S(1)} %turn.2.refs_3_, bf16[384,2048]{1,0:T(8,128)(2,1)S(1)} %turn.3.refs_4_), custom_call_target="tpu_custom_call" | custom-call | flops 1610612736 | bytes 6291456 | tf_op jit(solution)/shard_map/attend/pallas_call | solution.py:222
  67.0 2.8 %collective-permute-done.12.refs_3_.refs_2_ = bf16[272,384]{1,0:T(8,128)(2,1)S(1)} collective-permute-done((bf16[272,384]{1,0:T(8,128)(2,1)S(1)}, bf16[272,384]{1,0:T(8,128)(2,1)S(1)}, u32[]{:S(2)}, u32[]{:S(2)}) %collective-permute-start.12) | collective-permute-done | bytes 208928 | tf_op jit(solution)/shard_map/ppermute | solution.py:39
  70.2 1.0 %collective-permute-done.11.refs_1_ = bf16[144,384]{1,0:T(8,128)(2,1)S(1)} collective-permute-done((bf16[144,384]{1,0:T(8,128)(2,1)S(1)}, bf16[144,384]{1,0:T(8,128)(2,1)S(1)}, u32[]{:S(2)}, u32[]{:S(2)}) %collective-permute-start.11) | collective-permute-done | bytes 110624 | tf_op jit(solution)/shard_map/ppermute | solution.py:39
  71.6 4.1 %collective-permute-done.10.refs_1_ = bf16[144,384]{1,0:T(8,128)(2,1)S(1)} collective-permute-done((bf16[144,384]{1,0:T(8,128)(2,1)S(1)}, bf16[144,384]{1,0:T(8,128)(2,1)S(1)}, u32[]{:S(2)}, u32[]{:S(2)}) %collective-permute-start.10) | collective-permute-done | bytes 110624 | tf_op jit(solution)/shard_map/ppermute | solution.py:39
  76.4 2.8 %collective-permute-start.14 = (bf16[80,384]{1,0:T(8,128)(2,1)S(1)}, bf16[80,384]{1,0:T(8,128)(2,1)S(1)}, u32[]{:S(2)}, u32[]{:S(2)}) collective-permute-start(bf16[80,384]{1,0:T(8,128)(2,1)S(1)} %merge.7), channel_id=1, source_target_pairs={{0,16},{8,24},{16,0},{24,8},{32,48},{40,56},{48,32},{56,40},{64,80... | collective-permute-start | bytes 184328 | tf_op jit(solution)/shard_map/ppermute | solution.py:31
  79.2 3.0 %collective-permute-done.14.refs_2_ = bf16[80,384]{1,0:T(8,128)(2,1)S(1)} collective-permute-done((bf16[80,384]{1,0:T(8,128)(2,1)S(1)}, bf16[80,384]{1,0:T(8,128)(2,1)S(1)}, u32[]{:S(2)}, u32[]{:S(2)}) %collective-permute-start.14) | collective-permute-done | bytes 61472 | tf_op jit(solution)/shard_map/ppermute | solution.py:31
  82.9 10.5 %all_to_all.11 = bf16[8,8,3072]{2,1,0:T(8,128)(2,1)S(1)} all-to-all(bf16[8,8,3072]{2,1,0:T(8,128)(2,1)S(1)} %bitcast.2), channel_id=1, replica_groups=mesh['ctx'=32,'head'=8] {'head'}, dimensions={0} | all-to-all | bytes 786432 | tf_op jit(solution)/shard_map/all_to_all | solution.py:43
  (39 shorter events, 6.2 us)
Async XLA Ops:
  0.0 23.2 %collective-permute-start.3 = (bf16[2048,384]{1,0:T(8,128)(2,1)}, bf16[2048,384]{1,0:T(8,128)(2,1)S(1)}, u32[]{:S(2)}, u32[]{:S(2)}) collective-permute-start(bf16[2048,384]{1,0:T(8,128)(2,1)} %value.2), channel_id=1, source_target_pairs={{0,8},{8,0},{16,24},{24,16},{32,40},{40,32},{48,56},{56,48},{64,72... | collective-permute-start | bytes 4718600 | tf_op jit(solution)/shard_map/ppermute | solution.py:31
  0.0 25.7 %collective-permute-start.1 = (bf16[2048,384]{1,0:T(8,128)(2,1)}, bf16[2048,384]{1,0:T(8,128)(2,1)S(1)}, u32[]{:S(2)}, u32[]{:S(2)}) collective-permute-start(bf16[2048,384]{1,0:T(8,128)(2,1)} %refs_1_.11), channel_id=1, source_target_pairs={{0,8},{8,0},{16,24},{24,16},{32,40},{40,32},{48,56},{56,48},{64,72... | collective-permute-start | bytes 4718600 | tf_op jit(solution)/shard_map/ppermute | solution.py:31
  0.5 0.8 copy-start.4
  1.3 14.3 %copy-start.1 = (bf16[3072,384]{1,0:T(8,128)(2,1)S(1)}, bf16[3072,384]{1,0:T(8,128)(2,1)}, u32[]{:S(2)}) copy-start(bf16[3072,384]{1,0:T(8,128)(2,1)} %weight.1) | copy-start | bytes 7077892
  15.6 3.3 %copy-start.3 = (bf16[2048,384]{1,0:T(8,128)(2,1)S(1)}, bf16[2048,384]{1,0:T(8,128)(2,1)}, u32[]{:S(2)}) copy-start(bf16[2048,384]{1,0:T(8,128)(2,1)} %value.2) | copy-start | bytes 4718596
  16.1 5.7 %collective-permute-start = (bf16[64,384]{1,0:T(8,128)(2,1)S(1)}, bf16[64,384]{1,0:T(8,128)(2,1)S(1)}, u32[]{:S(2)}, u32[]{:S(2)}) collective-permute-start(bf16[64,384]{1,0:T(8,128)(2,1)S(1)} %project.1), channel_id=1, source_target_pairs={{0,16},{8,24},{16,0},{24,8},{32,48},{40,56},{48,32},{56,40},{64,80... | collective-permute-start | bytes 147464 | tf_op jit(solution)/shard_map/ppermute | solution.py:31
  21.8 1.4 %collective-permute-start.2 = (bf16[128,384]{1,0:T(8,128)(2,1)S(1)}, bf16[128,384]{1,0:T(8,128)(2,1)S(1)}, u32[]{:S(2)}, u32[]{:S(2)}) collective-permute-start(bf16[128,384]{1,0:T(8,128)(2,1)S(1)} %constant_dynamic-update-slice_fusion.refs_0_), channel_id=1, source_target_pairs={{0,8},{8,0},{16,24},{24,16},{32,40},{40,32},{48,56},{56,48},{64,72... | collective-permute-start | bytes 294920 | tf_op jit(solution)/shard_map/ppermute | solution.py:31
  23.3 2.5 %copy-start = (bf16[2048,384]{1,0:T(8,128)(2,1)S(1)}, bf16[2048,384]{1,0:T(8,128)(2,1)}, u32[]{:S(2)}) copy-start(bf16[2048,384]{1,0:T(8,128)(2,1)} %refs_1_.11) | copy-start | bytes 4718596
  23.3 5.7 %collective-permute-start.4 = (bf16[256,384]{1,0:T(8,128)(2,1)S(1)}, bf16[256,384]{1,0:T(8,128)(2,1)S(1)}, u32[]{:S(2)}, u32[]{:S(2)}) collective-permute-start(bf16[256,384]{1,0:T(8,128)(2,1)S(1)} %pad_maximum_fusion), channel_id=1, source_target_pairs={{0,32},{8,232},{16,48},{24,248},{32,64},{40,8},{48,80},{56,24},{64... | collective-permute-start | bytes 589832 | tf_op jit(solution)/shard_map/ppermute | solution.py:39
  29.0 7.5 %collective-permute-start.5 = (bf16[256,384]{1,0:T(8,128)(2,1)S(1)}, bf16[256,384]{1,0:T(8,128)(2,1)S(1)}, u32[]{:S(2)}, u32[]{:S(2)}) collective-permute-start(bf16[256,384]{1,0:T(8,128)(2,1)S(1)} %collective-permute-done.4.refs_0_), channel_id=1, source_target_pairs={{0,32},{8,232},{16,48},{24,248},{32,64},{40,8},{48,80},{56,24},{64... | collective-permute-start | bytes 589832 | tf_op jit(solution)/shard_map/ppermute | solution.py:39
  36.5 11.2 %collective-permute-start.6 = (bf16[256,384]{1,0:T(8,128)(2,1)S(1)}, bf16[256,384]{1,0:T(8,128)(2,1)S(1)}, u32[]{:S(2)}, u32[]{:S(2)}) collective-permute-start(bf16[256,384]{1,0:T(8,128)(2,1)S(1)} %collective-permute-done.5), channel_id=1, source_target_pairs={{0,32},{8,232},{16,48},{24,248},{32,64},{40,8},{48,80},{56,24},{64... | collective-permute-start | bytes 589832 | tf_op jit(solution)/shard_map/ppermute | solution.py:39
  39.9 7.9 %collective-permute-start.7 = (bf16[272,384]{1,0:T(8,128)(2,1)S(1)}, bf16[272,384]{1,0:T(8,128)(2,1)S(1)}, u32[]{:S(2)}, u32[]{:S(2)}) collective-permute-start(bf16[272,384]{1,0:T(8,128)(2,1)S(1)} %attend.7), channel_id=1, source_target_pairs={{0,224},{8,40},{16,240},{24,56},{32,0},{40,72},{48,16},{56,88},{64... | collective-permute-start | bytes 626696 | tf_op jit(solution)/shard_map/ppermute | solution.py:39
  39.9 13.0 %collective-permute-start.8 = (bf16[128,384]{1,0:T(8,128)(2,1)S(1)}, bf16[128,384]{1,0:T(8,128)(2,1)S(1)}, u32[]{:S(2)}, u32[]{:S(2)}) collective-permute-start(bf16[128,384]{1,0:T(8,128)(2,1)S(1)} %get-tuple-element.49), channel_id=1, source_target_pairs={{0,64},{8,200},{16,80},{24,216},{32,96},{40,232},{48,112},{56,248}... | collective-permute-start | bytes 294920 | tf_op jit(solution)/shard_map/ppermute | solution.py:39
  47.8 8.3 %collective-permute-start.9 = (bf16[144,384]{1,0:T(8,128)(2,1)S(1)}, bf16[144,384]{1,0:T(8,128)(2,1)S(1)}, u32[]{:S(2)}, u32[]{:S(2)}) collective-permute-start(bf16[144,384]{1,0:T(8,128)(2,1)S(1)} %attend.8), channel_id=1, source_target_pairs={{0,192},{8,72},{16,208},{24,88},{32,224},{40,104},{48,240},{56,120... | collective-permute-start | bytes 331784 | tf_op jit(solution)/shard_map/ppermute | solution.py:39
  56.1 13.6 %collective-permute-start.12 = (bf16[272,384]{1,0:T(8,128)(2,1)S(1)}, bf16[272,384]{1,0:T(8,128)(2,1)S(1)}, u32[]{:S(2)}, u32[]{:S(2)}) collective-permute-start(bf16[272,384]{1,0:T(8,128)(2,1)S(1)} %attend.9), channel_id=1, source_target_pairs={{0,160},{8,104},{16,176},{24,120},{32,192},{40,136},{48,208},{56,1... | collective-permute-start | bytes 626696 | tf_op jit(solution)/shard_map/ppermute | solution.py:39
  60.4 10.8 %collective-permute-start.11 = (bf16[144,384]{1,0:T(8,128)(2,1)S(1)}, bf16[144,384]{1,0:T(8,128)(2,1)S(1)}, u32[]{:S(2)}, u32[]{:S(2)}) collective-permute-start(bf16[144,384]{1,0:T(8,128)(2,1)S(1)} %attend.10), channel_id=1, source_target_pairs={{0,128},{8,136},{16,144},{24,152},{32,160},{40,168},{48,176},{56,1... | collective-permute-start | bytes 331784 | tf_op jit(solution)/shard_map/ppermute | solution.py:39
  66.8 8.9 %collective-permute-start.10 = (bf16[144,384]{1,0:T(8,128)(2,1)S(1)}, bf16[144,384]{1,0:T(8,128)(2,1)S(1)}, u32[]{:S(2)}, u32[]{:S(2)}) collective-permute-start(bf16[144,384]{1,0:T(8,128)(2,1)S(1)} %attend.11), channel_id=1, source_target_pairs={{0,192},{8,72},{16,208},{24,88},{32,224},{40,104},{48,240},{56,120... | collective-permute-start | bytes 331784 | tf_op jit(solution)/shard_map/ppermute | solution.py:39
  70.1 5.6 %collective-permute-start.13 = (bf16[144,384]{1,0:T(8,128)(2,1)S(1)}, bf16[144,384]{1,0:T(8,128)(2,1)S(1)}, u32[]{:S(2)}, u32[]{:S(2)}) collective-permute-start(bf16[144,384]{1,0:T(8,128)(2,1)S(1)} %merge.5), channel_id=1, source_target_pairs={{0,8},{8,0},{16,24},{24,16},{32,40},{40,32},{48,56},{56,48},{64,72... | collective-permute-start | bytes 331784 | tf_op jit(solution)/shard_map/ppermute | solution.py:31
  71.2 11.0 %copy-start.2 = (bf16[384,3072]{1,0:T(8,128)(2,1)S(1)}, bf16[384,3072]{1,0:T(8,128)(2,1)}, u32[]{:S(2)}) copy-start(bf16[384,3072]{1,0:T(8,128)(2,1)} %refs_3_.1) | copy-start | bytes 7077892
  76.4 5.8 %collective-permute-start.14 = (bf16[80,384]{1,0:T(8,128)(2,1)S(1)}, bf16[80,384]{1,0:T(8,128)(2,1)S(1)}, u32[]{:S(2)}, u32[]{:S(2)}) collective-permute-start(bf16[80,384]{1,0:T(8,128)(2,1)S(1)} %merge.7), channel_id=1, source_target_pairs={{0,16},{8,24},{16,0},{24,8},{32,48},{40,56},{48,32},{56,40},{64,80... | collective-permute-start | bytes 184328 | tf_op jit(solution)/shard_map/ppermute | solution.py:31

commit v6 on v5

--- a/solution.py
+++ b/solution.py
@@ -79,7 +79,7 @@
     def score(step, part, peak):
         head, at = steps[step]
         keys, place = (key_a, at + part) if at < half else (key_b, at + part - half)
-        block = LOG2E * jnp.dot(
+        block = jnp.dot(
             keys[place : place + BLOCK, columns(head)], queries[head], preferred_element_type=jnp.float32
         )
         held[step % len(held)][part : part + BLOCK, :] = block
@@ -89,7 +89,7 @@
     def weigh(step, start, peak, total):
         for part in range(start, start + BLOCK, PART):
             block = held[step % len(held)][part : part + PART, :].reshape(PART // 8, 8, across)
-            block = jnp.exp2(block - peak[None])
+            block = jnp.exp2(LOG2E * block - peak[None])
             total = total + jnp.sum(block, axis=0)
             block = block.reshape(PART, across).astype(jnp.bfloat16)
             weights[step % 2][part : part + PART, :] = block
@@ -133,7 +133,7 @@
             score_ahead(step, part)
     pending = top = total = None
     for step, (head, at) in enumerate(steps):
-        rescale, highest = None, jnp.max(peaks[step], axis=0, keepdims=True)
+        rescale, highest = None, LOG2E * jnp.max(peaks[step], axis=0, keepdims=True)
         if at:
             highest = jnp.maximum(top, highest)
             rescale = jnp.exp2(top - highest)

time: 94.4 us -> 94 us (level)
  the two profiles are of different devices: /device:TPU:64 before, /device:TPU:4 now
where the time goes in v6:
time: 94 us; the launch traced here: 93.1 us
  waiting for transfers between devices  24.9 us (26%)
  blocking collectives  24.5 us (26%)
  Pallas kernels  23.5 us (25%)
  starting transfers between devices  18.5 us (20%)
    all_to_all x2, blocking collectives, exchange(): return lax.all_to_all(value, 'head', 0, 0)  24.5 us
    pallas_call x15, Pallas kernels, call(): pl.pallas_call(kernel, out_shape=out_shape, in_specs=[vmem()] * len(opera...  23.5 us
    ppermute x9, starting transfers between devices, carry(): return lax.ppermute(value, 'ctx', pairs)  16 us
    ppermute x9, waiting for transfers between devices, carry(): return lax.ppermute(value, 'ctx', pairs)  14.3 us
    ppermute x6, waiting for transfers between devices, move(): return lax.ppermute(value, 'ctx', pairs)  10.6 us
    ppermute x6, starting transfers between devices, move(): return lax.ppermute(value, 'ctx', pairs)  2.45 us
  transfers between devices with their start and end apart: 15, of which 9 were waited for; matrix products, arithmetic and copies ran while one was open for 0% of the time, Pallas kernels for 24%

profile of v6, /device:TPU:4, one launch (start us, length us, event | category | flops | bytes accessed | tf_op | source)
XLA Modules:
  0.0 93.1 jit_solution(7475908862917996683)
XLA Ops:
  1.3 14.0 %all_to_all.10 = bf16[8,8,3072]{2,1,0:T(8,128)(2,1)S(1)} all-to-all(bf16[8,8,3072]{2,1,0:T(8,128)(2,1)S(1)} %repeat.1), channel_id=1, replica_groups=mesh['ctx'=32,'head'=8] {'head'}, dimensions={0} | all-to-all | bytes 786432 | tf_op jit(solution)/shard_map/all_to_all | solution.py:43
  15.8 0.9 collective-permute-start
  17.2 4.3 %collective-permute-done = bf16[64,384]{1,0:T(8,128)(2,1)S(1)} collective-permute-done((bf16[64,384]{1,0:T(8,128)(2,1)S(1)}, bf16[64,384]{1,0:T(8,128)(2,1)S(1)}, u32[]{:S(2)}, u32[]{:S(2)}) %collective-permute-start) | collective-permute-done | bytes 49184 | tf_op jit(solution)/shard_map/ppermute | solution.py:31
  21.6 1.3 %collective-permute-done.2 = bf16[128,384]{1,0:T(8,128)(2,1)S(1)} collective-permute-done((bf16[128,384]{1,0:T(8,128)(2,1)S(1)}, bf16[128,384]{1,0:T(8,128)(2,1)S(1)}, u32[]{:S(2)}, u32[]{:S(2)}) %collective-permute-start.2) | collective-permute-done | bytes 98336 | tf_op jit(solution)/shard_map/ppermute | solution.py:31
  23.0 2.0 %collective-permute-start.4 = (bf16[256,384]{1,0:T(8,128)(2,1)S(1)}, bf16[256,384]{1,0:T(8,128)(2,1)S(1)}, u32[]{:S(2)}, u32[]{:S(2)}) collective-permute-start(bf16[256,384]{1,0:T(8,128)(2,1)S(1)} %pad_maximum_fusion), channel_id=1, source_target_pairs={{0,32},{8,232},{16,48},{24,248},{32,64},{40,8},{48,80},{56,24},{64... | collective-permute-start | bytes 589832 | tf_op jit(solution)/shard_map/ppermute | solution.py:39
  25.4 2.8 %attend.6.refs_0_ = bf16[144,384]{1,0:T(8,128)(2,1)S(1)} custom-call(bf16[128,384]{1,0:T(8,128)(2,1)S(1)} %constant_dynamic-update-slice_fusion.refs_0_, bf16[2048,384]{1,0:T(8,128)(2,1)S(1)} %copy-done, bf16[2048,384]{1,0:T(8,128)(2,1)S(1)} %collective-permute-done.1.refs_2_, bf16[384,2048]{1,0:T(8,128)(2,1)S(1)} %turn.2.refs_3_, ...), custom_call_target="tpu_custom_call" | custom-call | flops 1610612736 | bytes 6291456 | tf_op jit(solution)/shard_map/attend/pallas_call | solution.py:222
  28.3 4.3 %collective-permute-done.4.refs_0_ = bf16[256,384]{1,0:T(8,128)(2,1)S(1)} collective-permute-done((bf16[256,384]{1,0:T(8,128)(2,1)S(1)}, bf16[256,384]{1,0:T(8,128)(2,1)S(1)}, u32[]{:S(2)}, u32[]{:S(2)}) %collective-permute-start.4) | collective-permute-done | bytes 196640 | tf_op jit(solution)/shard_map/ppermute | solution.py:39
  32.6 4.3 %attend.7 = bf16[272,384]{1,0:T(8,128)(2,1)S(1)} custom-call(bf16[256,384]{1,0:T(8,128)(2,1)S(1)} %collective-permute-done.4.refs_0_, bf16[2048,384]{1,0:T(8,128)(2,1)S(1)} %copy-done, bf16[2048,384]{1,0:T(8,128)(2,1)S(1)} %collective-permute-done.1.refs_2_, bf16[384,2048]{1,0:T(8,128)(2,1)S(1)} %turn.2.refs_3_, bf16[384,2048]{1,0:T(8,128)(2,1)S(1)} %turn.3.refs_4_), custom_call_target="tpu_custom_call" | custom-call | flops 3221225472 | bytes 6291456 | tf_op jit(solution)/shard_map/attend/pallas_call | solution.py:222
  36.8 2.6 %collective-permute-done.5 = bf16[256,384]{1,0:T(8,128)(2,1)S(1)} collective-permute-done((bf16[256,384]{1,0:T(8,128)(2,1)S(1)}, bf16[256,384]{1,0:T(8,128)(2,1)S(1)}, u32[]{:S(2)}, u32[]{:S(2)}) %collective-permute-start.5) | collective-permute-done | bytes 196640 | tf_op jit(solution)/shard_map/ppermute | solution.py:39
  39.4 3.2 %collective-permute-start.7 = (bf16[272,384]{1,0:T(8,128)(2,1)S(1)}, bf16[272,384]{1,0:T(8,128)(2,1)S(1)}, u32[]{:S(2)}, u32[]{:S(2)}) collective-permute-start(bf16[272,384]{1,0:T(8,128)(2,1)S(1)} %attend.7), channel_id=1, source_target_pairs={{0,224},{8,40},{16,240},{24,56},{32,0},{40,72},{48,16},{56,88},{64... | collective-permute-start | bytes 626696 | tf_op jit(solution)/shard_map/ppermute | solution.py:39
  42.9 2.8 %attend.8 = bf16[144,384]{1,0:T(8,128)(2,1)S(1)} custom-call(bf16[128,384]{1,0:T(8,128)(2,1)S(1)} %get-tuple-element.50.refs_0_, bf16[2048,384]{1,0:T(8,128)(2,1)S(1)} %copy-done, bf16[2048,384]{1,0:T(8,128)(2,1)S(1)} %collective-permute-done.1.refs_2_, bf16[384,2048]{1,0:T(8,128)(2,1)S(1)} %turn.2.refs_3_, bf16[384,2048]{1,0:T(8,128)(2,1)S(1)} %turn.3.refs_4_), custom_call_target="tpu_custom_call" | custom-call | flops 1610612736 | bytes 6291456 | tf_op jit(solution)/shard_map/attend/pallas_call | solution.py:222
  45.7 2.7 %collective-permute-done.6.refs_0_ = bf16[256,384]{1,0:T(8,128)(2,1)S(1)} collective-permute-done((bf16[256,384]{1,0:T(8,128)(2,1)S(1)}, bf16[256,384]{1,0:T(8,128)(2,1)S(1)}, u32[]{:S(2)}, u32[]{:S(2)}) %collective-permute-start.6) | collective-permute-done | bytes 196640 | tf_op jit(solution)/shard_map/ppermute | solution.py:39
  48.4 1.6 %collective-permute-start.9 = (bf16[144,384]{1,0:T(8,128)(2,1)S(1)}, bf16[144,384]{1,0:T(8,128)(2,1)S(1)}, u32[]{:S(2)}, u32[]{:S(2)}) collective-permute-start(bf16[144,384]{1,0:T(8,128)(2,1)S(1)} %attend.8), channel_id=1, source_target_pairs={{0,192},{8,72},{16,208},{24,88},{32,224},{40,104},{48,240},{56,120... | collective-permute-start | bytes 331784 | tf_op jit(solution)/shard_map/ppermute | solution.py:39
  50.0 4.3 %attend.9 = bf16[272,384]{1,0:T(8,128)(2,1)S(1)} custom-call(bf16[256,384]{1,0:T(8,128)(2,1)S(1)} %collective-permute-done.6.refs_0_, bf16[2048,384]{1,0:T(8,128)(2,1)S(1)} %copy-done, bf16[2048,384]{1,0:T(8,128)(2,1)S(1)} %collective-permute-done.1.refs_2_, bf16[384,2048]{1,0:T(8,128)(2,1)S(1)} %turn.2.refs_3_, bf16[384,2048]{1,0:T(8,128)(2,1)S(1)} %turn.3.refs_4_), custom_call_target="tpu_custom_call" | custom-call | flops 3221225472 | bytes 6291456 | tf_op jit(solution)/shard_map/attend/pallas_call | solution.py:222
  54.3 1.1 %collective-permute-done.9.refs_0_ = bf16[144,384]{1,0:T(8,128)(2,1)S(1)} collective-permute-done((bf16[144,384]{1,0:T(8,128)(2,1)S(1)}, bf16[144,384]{1,0:T(8,128)(2,1)S(1)}, u32[]{:S(2)}, u32[]{:S(2)}) %collective-permute-start.9) | collective-permute-done | bytes 110624 | tf_op jit(solution)/shard_map/ppermute | solution.py:39
  55.3 3.5 %collective-permute-start.12 = (bf16[272,384]{1,0:T(8,128)(2,1)S(1)}, bf16[272,384]{1,0:T(8,128)(2,1)S(1)}, u32[]{:S(2)}, u32[]{:S(2)}) collective-permute-start(bf16[272,384]{1,0:T(8,128)(2,1)S(1)} %attend.9), channel_id=1, source_target_pairs={{0,160},{8,104},{16,176},{24,120},{32,192},{40,136},{48,208},{56,1... | collective-permute-start | bytes 626696 | tf_op jit(solution)/shard_map/ppermute | solution.py:39
  58.9 2.8 %attend.10 = bf16[144,384]{1,0:T(8,128)(2,1)S(1)} custom-call(bf16[128,384]{1,0:T(8,128)(2,1)S(1)} %collective-permute-done.8.refs_0_, bf16[2048,384]{1,0:T(8,128)(2,1)S(1)} %copy-done, bf16[2048,384]{1,0:T(8,128)(2,1)S(1)} %collective-permute-done.1.refs_2_, bf16[384,2048]{1,0:T(8,128)(2,1)S(1)} %turn.2.refs_3_, bf16[384,2048]{1,0:T(8,128)(2,1)S(1)} %turn.3.refs_4_), custom_call_target="tpu_custom_call" | custom-call | flops 1610612736 | bytes 6291456 | tf_op jit(solution)/shard_map/attend/pallas_call | solution.py:222
  61.7 2.3 %collective-permute-start.11 = (bf16[144,384]{1,0:T(8,128)(2,1)S(1)}, bf16[144,384]{1,0:T(8,128)(2,1)S(1)}, u32[]{:S(2)}, u32[]{:S(2)}) collective-permute-start(bf16[144,384]{1,0:T(8,128)(2,1)S(1)} %attend.10), channel_id=1, source_target_pairs={{0,128},{8,136},{16,144},{24,152},{32,160},{40,168},{48,176},{56,1... | collective-permute-start | bytes 331784 | tf_op jit(solution)/shard_map/ppermute | solution.py:39
  64.0 2.8 %attend.11 = bf16[144,384]{1,0:T(8,128)(2,1)S(1)} custom-call(bf16[128,384]{1,0:T(8,128)(2,1)S(1)} %slice.11.refs_0_, bf16[2048,384]{1,0:T(8,128)(2,1)S(1)} %copy-done, bf16[2048,384]{1,0:T(8,128)(2,1)S(1)} %collective-permute-done.1.refs_2_, bf16[384,2048]{1,0:T(8,128)(2,1)S(1)} %turn.2.refs_3_, bf16[384,2048]{1,0:T(8,128)(2,1)S(1)} %turn.3.refs_4_), custom_call_target="tpu_custom_call" | custom-call | flops 1610612736 | bytes 6291456 | tf_op jit(solution)/shard_map/attend/pallas_call | solution.py:222
  66.9 3.2 %collective-permute-start.10 = (bf16[144,384]{1,0:T(8,128)(2,1)S(1)}, bf16[144,384]{1,0:T(8,128)(2,1)S(1)}, u32[]{:S(2)}, u32[]{:S(2)}) collective-permute-start(bf16[144,384]{1,0:T(8,128)(2,1)S(1)} %attend.11), channel_id=1, source_target_pairs={{0,192},{8,72},{16,208},{24,88},{32,224},{40,104},{48,240},{56,120... | collective-permute-start | bytes 331784 | tf_op jit(solution)/shard_map/ppermute | solution.py:39
  70.5 2.0 %collective-permute-done.11.refs_1_ = bf16[144,384]{1,0:T(8,128)(2,1)S(1)} collective-permute-done((bf16[144,384]{1,0:T(8,128)(2,1)S(1)}, bf16[144,384]{1,0:T(8,128)(2,1)S(1)}, u32[]{:S(2)}, u32[]{:S(2)}) %collective-permute-start.11) | collective-permute-done | bytes 110624 | tf_op jit(solution)/shard_map/ppermute | solution.py:39
  72.9 1.8 %collective-permute-done.10.refs_1_ = bf16[144,384]{1,0:T(8,128)(2,1)S(1)} collective-permute-done((bf16[144,384]{1,0:T(8,128)(2,1)S(1)}, bf16[144,384]{1,0:T(8,128)(2,1)S(1)}, u32[]{:S(2)}, u32[]{:S(2)}) %collective-permute-start.10) | collective-permute-done | bytes 110624 | tf_op jit(solution)/shard_map/ppermute | solution.py:39
  76.2 4.9 %collective-permute-done.14.refs_2_ = bf16[80,384]{1,0:T(8,128)(2,1)S(1)} collective-permute-done((bf16[80,384]{1,0:T(8,128)(2,1)S(1)}, bf16[80,384]{1,0:T(8,128)(2,1)S(1)}, u32[]{:S(2)}, u32[]{:S(2)}) %collective-permute-start.14) | collective-permute-done | bytes 61472 | tf_op jit(solution)/shard_map/ppermute | solution.py:31
  81.9 10.5 %all_to_all.11 = bf16[8,8,3072]{2,1,0:T(8,128)(2,1)S(1)} all-to-all(bf16[8,8,3072]{2,1,0:T(8,128)(2,1)S(1)} %bitcast.2), channel_id=1, replica_groups=mesh['ctx'=32,'head'=8] {'head'}, dimensions={0} | all-to-all | bytes 786432 | tf_op jit(solution)/shard_map/all_to_all | solution.py:43
  (39 shorter events, 7.0 us)
Async XLA Ops:
  0.0 22.9 %collective-permute-start.3 = (bf16[2048,384]{1,0:T(8,128)(2,1)}, bf16[2048,384]{1,0:T(8,128)(2,1)S(1)}, u32[]{:S(2)}, u32[]{:S(2)}) collective-permute-start(bf16[2048,384]{1,0:T(8,128)(2,1)} %value.2), channel_id=1, source_target_pairs={{0,8},{8,0},{16,24},{24,16},{32,40},{40,32},{48,56},{56,48},{64,72... | collective-permute-start | bytes 4718600 | tf_op jit(solution)/shard_map/ppermute | solution.py:31
  0.0 25.4 %collective-permute-start.1 = (bf16[2048,384]{1,0:T(8,128)(2,1)}, bf16[2048,384]{1,0:T(8,128)(2,1)S(1)}, u32[]{:S(2)}, u32[]{:S(2)}) collective-permute-start(bf16[2048,384]{1,0:T(8,128)(2,1)} %refs_1_.11), channel_id=1, source_target_pairs={{0,8},{8,0},{16,24},{24,16},{32,40},{40,32},{48,56},{56,48},{64,72... | collective-permute-start | bytes 4718600 | tf_op jit(solution)/shard_map/ppermute | solution.py:31
  0.5 0.8 copy-start.4
  1.3 14.0 %copy-start.1 = (bf16[3072,384]{1,0:T(8,128)(2,1)S(1)}, bf16[3072,384]{1,0:T(8,128)(2,1)}, u32[]{:S(2)}) copy-start(bf16[3072,384]{1,0:T(8,128)(2,1)} %weight.1) | copy-start | bytes 7077892
  15.3 1.4 %copy-start.3 = (bf16[2048,384]{1,0:T(8,128)(2,1)S(1)}, bf16[2048,384]{1,0:T(8,128)(2,1)}, u32[]{:S(2)}) copy-start(bf16[2048,384]{1,0:T(8,128)(2,1)} %value.2) | copy-start | bytes 4718596
  15.8 5.7 %collective-permute-start = (bf16[64,384]{1,0:T(8,128)(2,1)S(1)}, bf16[64,384]{1,0:T(8,128)(2,1)S(1)}, u32[]{:S(2)}, u32[]{:S(2)}) collective-permute-start(bf16[64,384]{1,0:T(8,128)(2,1)S(1)} %project.1), channel_id=1, source_target_pairs={{0,16},{8,24},{16,0},{24,8},{32,48},{40,56},{48,32},{56,40},{64,80... | collective-permute-start | bytes 147464 | tf_op jit(solution)/shard_map/ppermute | solution.py:31
  21.5 1.4 %collective-permute-start.2 = (bf16[128,384]{1,0:T(8,128)(2,1)S(1)}, bf16[128,384]{1,0:T(8,128)(2,1)S(1)}, u32[]{:S(2)}, u32[]{:S(2)}) collective-permute-start(bf16[128,384]{1,0:T(8,128)(2,1)S(1)} %constant_dynamic-update-slice_fusion.refs_0_), channel_id=1, source_target_pairs={{0,8},{8,0},{16,24},{24,16},{32,40},{40,32},{48,56},{56,48},{64,72... | collective-permute-start | bytes 294920 | tf_op jit(solution)/shard_map/ppermute | solution.py:31
  23.0 2.5 %copy-start = (bf16[2048,384]{1,0:T(8,128)(2,1)S(1)}, bf16[2048,384]{1,0:T(8,128)(2,1)}, u32[]{:S(2)}) copy-start(bf16[2048,384]{1,0:T(8,128)(2,1)} %refs_1_.11) | copy-start | bytes 4718596
  23.0 9.6 %collective-permute-start.4 = (bf16[256,384]{1,0:T(8,128)(2,1)S(1)}, bf16[256,384]{1,0:T(8,128)(2,1)S(1)}, u32[]{:S(2)}, u32[]{:S(2)}) collective-permute-start(bf16[256,384]{1,0:T(8,128)(2,1)S(1)} %pad_maximum_fusion), channel_id=1, source_target_pairs={{0,32},{8,232},{16,48},{24,248},{32,64},{40,8},{48,80},{56,24},{64... | collective-permute-start | bytes 589832 | tf_op jit(solution)/shard_map/ppermute | solution.py:39
  32.6 6.9 %collective-permute-start.5 = (bf16[256,384]{1,0:T(8,128)(2,1)S(1)}, bf16[256,384]{1,0:T(8,128)(2,1)S(1)}, u32[]{:S(2)}, u32[]{:S(2)}) collective-permute-start(bf16[256,384]{1,0:T(8,128)(2,1)S(1)} %collective-permute-done.4.refs_0_), channel_id=1, source_target_pairs={{0,32},{8,232},{16,48},{24,248},{32,64},{40,8},{48,80},{56,24},{64... | collective-permute-start | bytes 589832 | tf_op jit(solution)/shard_map/ppermute | solution.py:39
  39.4 9.0 %collective-permute-start.6 = (bf16[256,384]{1,0:T(8,128)(2,1)S(1)}, bf16[256,384]{1,0:T(8,128)(2,1)S(1)}, u32[]{:S(2)}, u32[]{:S(2)}) collective-permute-start(bf16[256,384]{1,0:T(8,128)(2,1)S(1)} %collective-permute-done.5), channel_id=1, source_target_pairs={{0,32},{8,232},{16,48},{24,248},{32,64},{40,8},{48,80},{56,24},{64... | collective-permute-start | bytes 589832 | tf_op jit(solution)/shard_map/ppermute | solution.py:39
  39.4 9.0 %collective-permute-start.7 = (bf16[272,384]{1,0:T(8,128)(2,1)S(1)}, bf16[272,384]{1,0:T(8,128)(2,1)S(1)}, u32[]{:S(2)}, u32[]{:S(2)}) collective-permute-start(bf16[272,384]{1,0:T(8,128)(2,1)S(1)} %attend.7), channel_id=1, source_target_pairs={{0,224},{8,40},{16,240},{24,56},{32,0},{40,72},{48,16},{56,88},{64... | collective-permute-start | bytes 626696 | tf_op jit(solution)/shard_map/ppermute | solution.py:39
  42.7 11.6 %collective-permute-start.8 = (bf16[128,384]{1,0:T(8,128)(2,1)S(1)}, bf16[128,384]{1,0:T(8,128)(2,1)S(1)}, u32[]{:S(2)}, u32[]{:S(2)}) collective-permute-start(bf16[128,384]{1,0:T(8,128)(2,1)S(1)} %get-tuple-element.49), channel_id=1, source_target_pairs={{0,64},{8,200},{16,80},{24,216},{32,96},{40,232},{48,112},{56,248}... | collective-permute-start | bytes 294920 | tf_op jit(solution)/shard_map/ppermute | solution.py:39
  48.4 6.9 %collective-permute-start.9 = (bf16[144,384]{1,0:T(8,128)(2,1)S(1)}, bf16[144,384]{1,0:T(8,128)(2,1)S(1)}, u32[]{:S(2)}, u32[]{:S(2)}) collective-permute-start(bf16[144,384]{1,0:T(8,128)(2,1)S(1)} %attend.8), channel_id=1, source_target_pairs={{0,192},{8,72},{16,208},{24,88},{32,224},{40,104},{48,240},{56,120... | collective-permute-start | bytes 331784 | tf_op jit(solution)/shard_map/ppermute | solution.py:39
  55.3 14.7 %collective-permute-start.12 = (bf16[272,384]{1,0:T(8,128)(2,1)S(1)}, bf16[272,384]{1,0:T(8,128)(2,1)S(1)}, u32[]{:S(2)}, u32[]{:S(2)}) collective-permute-start(bf16[272,384]{1,0:T(8,128)(2,1)S(1)} %attend.9), channel_id=1, source_target_pairs={{0,160},{8,104},{16,176},{24,120},{32,192},{40,136},{48,208},{56,1... | collective-permute-start | bytes 626696 | tf_op jit(solution)/shard_map/ppermute | solution.py:39
  61.7 10.7 %collective-permute-start.11 = (bf16[144,384]{1,0:T(8,128)(2,1)S(1)}, bf16[144,384]{1,0:T(8,128)(2,1)S(1)}, u32[]{:S(2)}, u32[]{:S(2)}) collective-permute-start(bf16[144,384]{1,0:T(8,128)(2,1)S(1)} %attend.10), channel_id=1, source_target_pairs={{0,128},{8,136},{16,144},{24,152},{32,160},{40,168},{48,176},{56,1... | collective-permute-start | bytes 331784 | tf_op jit(solution)/shard_map/ppermute | solution.py:39
  66.9 7.8 %collective-permute-start.10 = (bf16[144,384]{1,0:T(8,128)(2,1)S(1)}, bf16[144,384]{1,0:T(8,128)(2,1)S(1)}, u32[]{:S(2)}, u32[]{:S(2)}) collective-permute-start(bf16[144,384]{1,0:T(8,128)(2,1)S(1)} %attend.11), channel_id=1, source_target_pairs={{0,192},{8,72},{16,208},{24,88},{32,224},{40,104},{48,240},{56,120... | collective-permute-start | bytes 331784 | tf_op jit(solution)/shard_map/ppermute | solution.py:39
  70.4 4.3 %collective-permute-start.13 = (bf16[144,384]{1,0:T(8,128)(2,1)S(1)}, bf16[144,384]{1,0:T(8,128)(2,1)S(1)}, u32[]{:S(2)}, u32[]{:S(2)}) collective-permute-start(bf16[144,384]{1,0:T(8,128)(2,1)S(1)} %merge.5), channel_id=1, source_target_pairs={{0,8},{8,0},{16,24},{24,16},{32,40},{40,32},{48,56},{56,48},{64,72... | collective-permute-start | bytes 331784 | tf_op jit(solution)/shard_map/ppermute | solution.py:31
  72.5 8.7 %copy-start.2 = (bf16[384,3072]{1,0:T(8,128)(2,1)S(1)}, bf16[384,3072]{1,0:T(8,128)(2,1)}, u32[]{:S(2)}) copy-start(bf16[384,3072]{1,0:T(8,128)(2,1)} %refs_3_.1) | copy-start | bytes 7077892
  75.3 5.8 %collective-permute-start.14 = (bf16[80,384]{1,0:T(8,128)(2,1)S(1)}, bf16[80,384]{1,0:T(8,128)(2,1)S(1)}, u32[]{:S(2)}, u32[]{:S(2)}) collective-permute-start(bf16[80,384]{1,0:T(8,128)(2,1)S(1)} %merge.7), channel_id=1, source_target_pairs={{0,16},{8,24},{16,0},{24,8},{32,48},{40,56},{48,32},{56,40},{64,80... | collective-permute-start | bytes 184328 | tf_op jit(solution)/shard_map/ppermute | solution.py:31

commit v7 on v6

--- a/solution.py
+++ b/solution.py
@@ -303,14 +303,14 @@
     third, far = carry(second, 1), carry(second[: 2 * few], 2)
     back_near = carry(part, -1)
     part_others, = attend((second[2 * few :],), keys, values)
-    part_others, third, back_near = tied(part_others, third, back_near)
+    part_others, far, back_near = tied(part_others, far, back_near)
     back_others = carry(part_others, -2)
+    part_far, = attend((far,), keys, values)
+    part_far, third = tied(part_far, third)
+    back_far = carry(part_far, -4)
     part, = attend((third,), keys, values)
-    part, second, far, back_others = tied(part, second, far, back_others)
+    part, second, back_others = tied(part, second, back_others)
     back_third = carry(part, -3)
-    part_far, = attend((far,), keys, values)
-    part_far, second = tied(part_far, second)
-    back_far = carry(part_far, -4)
     part, = attend((second[: 2 * few],), keys, values)
     early = merge(2 * few, (part_own, 0), (back_far, 0), (back_near, 0), (back_third, 0), flops=MERGE_FLOPS)
     others = move(merge(2 * few, (back_others, 0), (back_near, 2 * few), (back_third, 2 * few)), dcore=1)

time: 94 us -> 97.2 us (1.034)
  starting transfers between devices: 18.5 us -> 20.5 us
  waiting for transfers between devices: 24.9 us -> 25.9 us
    ppermute x9, starting transfers between devices: 16 us -> 18 us  [carry(): return lax.ppermute(value, 'ctx', pairs)]
    ppermute x9, waiting for transfers between devices: 14.3 us -> 15.4 us  [carry(): return lax.ppermute(value, 'ctx', pairs)]
  transfers between devices with their start and end apart: 15 -> 15, of which waited for: 9 -> 8; matrix products, arithmetic and copies ran while one was open for 0% -> 0% of each run, Pallas kernels for 24% -> 23%
where the time goes in v7:
time: 97.2 us; the launch traced here: 96.2 us
  waiting for transfers between devices  25.9 us (27%)
  blocking collectives  24.5 us (25%)
  Pallas kernels  23.5 us (24%)
  starting transfers between devices  20.5 us (21%)
    all_to_all x2, blocking collectives, exchange(): return lax.all_to_all(value, 'head', 0, 0)  24.5 us
    pallas_call x15, Pallas kernels, call(): pl.pallas_call(kernel, out_shape=out_shape, in_specs=[vmem()] * len(opera...  23.5 us
    ppermute x9, starting transfers between devices, carry(): return lax.ppermute(value, 'ctx', pairs)  18 us
    ppermute x9, waiting for transfers between devices, carry(): return lax.ppermute(value, 'ctx', pairs)  15.4 us
    ppermute x6, waiting for transfers between devices, move(): return lax.ppermute(value, 'ctx', pairs)  10.5 us
    ppermute x6, starting transfers between devices, move(): return lax.ppermute(value, 'ctx', pairs)  2.48 us
  transfers between devices with their start and end apart: 15, of which 8 were waited for; matrix products, arithmetic and copies ran while one was open for 0% of the time, Pallas kernels for 23%

profile of v7, /device:TPU:4, one launch (start us, length us, event | category | flops | bytes accessed | tf_op | source)
XLA Modules:
  0.0 96.2 jit_solution(299068268847185109)
XLA Ops:
  1.3 14.0 %all_to_all.10 = bf16[8,8,3072]{2,1,0:T(8,128)(2,1)S(1)} all-to-all(bf16[8,8,3072]{2,1,0:T(8,128)(2,1)S(1)} %repeat.1), channel_id=1, replica_groups=mesh['ctx'=32,'head'=8] {'head'}, dimensions={0} | all-to-all | bytes 786432 | tf_op jit(solution)/shard_map/all_to_all | solution.py:43
  17.2 4.3 %collective-permute-done = bf16[64,384]{1,0:T(8,128)(2,1)S(1)} collective-permute-done((bf16[64,384]{1,0:T(8,128)(2,1)S(1)}, bf16[64,384]{1,0:T(8,128)(2,1)S(1)}, u32[]{:S(2)}, u32[]{:S(2)}) %collective-permute-start) | collective-permute-done | bytes 49184 | tf_op jit(solution)/shard_map/ppermute | solution.py:31
  21.6 1.3 %collective-permute-done.2 = bf16[128,384]{1,0:T(8,128)(2,1)S(1)} collective-permute-done((bf16[128,384]{1,0:T(8,128)(2,1)S(1)}, bf16[128,384]{1,0:T(8,128)(2,1)S(1)}, u32[]{:S(2)}, u32[]{:S(2)}) %collective-permute-start.2) | collective-permute-done | bytes 98336 | tf_op jit(solution)/shard_map/ppermute | solution.py:31
  23.0 2.0 %collective-permute-start.4 = (bf16[256,384]{1,0:T(8,128)(2,1)S(1)}, bf16[256,384]{1,0:T(8,128)(2,1)S(1)}, u32[]{:S(2)}, u32[]{:S(2)}) collective-permute-start(bf16[256,384]{1,0:T(8,128)(2,1)S(1)} %pad_maximum_fusion), channel_id=1, source_target_pairs={{0,32},{8,232},{16,48},{24,248},{32,64},{40,8},{48,80},{56,24},{64... | collective-permute-start | bytes 589832 | tf_op jit(solution)/shard_map/ppermute | solution.py:39
  25.4 2.8 %attend.6.refs_0_ = bf16[144,384]{1,0:T(8,128)(2,1)S(1)} custom-call(bf16[128,384]{1,0:T(8,128)(2,1)S(1)} %constant_dynamic-update-slice_fusion.refs_0_, bf16[2048,384]{1,0:T(8,128)(2,1)S(1)} %copy-done, bf16[2048,384]{1,0:T(8,128)(2,1)S(1)} %collective-permute-done.1.refs_2_, bf16[384,2048]{1,0:T(8,128)(2,1)S(1)} %turn.2.refs_3_, ...), custom_call_target="tpu_custom_call" | custom-call | flops 1610612736 | bytes 6291456 | tf_op jit(solution)/shard_map/attend/pallas_call | solution.py:222
  28.3 4.3 %collective-permute-done.4.refs_0_ = bf16[256,384]{1,0:T(8,128)(2,1)S(1)} collective-permute-done((bf16[256,384]{1,0:T(8,128)(2,1)S(1)}, bf16[256,384]{1,0:T(8,128)(2,1)S(1)}, u32[]{:S(2)}, u32[]{:S(2)}) %collective-permute-start.4) | collective-permute-done | bytes 196640 | tf_op jit(solution)/shard_map/ppermute | solution.py:39
  32.6 4.3 %attend.7 = bf16[272,384]{1,0:T(8,128)(2,1)S(1)} custom-call(bf16[256,384]{1,0:T(8,128)(2,1)S(1)} %collective-permute-done.4.refs_0_, bf16[2048,384]{1,0:T(8,128)(2,1)S(1)} %copy-done, bf16[2048,384]{1,0:T(8,128)(2,1)S(1)} %collective-permute-done.1.refs_2_, bf16[384,2048]{1,0:T(8,128)(2,1)S(1)} %turn.2.refs_3_, bf16[384,2048]{1,0:T(8,128)(2,1)S(1)} %turn.3.refs_4_), custom_call_target="tpu_custom_call" | custom-call | flops 3221225472 | bytes 6291456 | tf_op jit(solution)/shard_map/attend/pallas_call | solution.py:222
  36.8 2.6 %collective-permute-done.5 = bf16[256,384]{1,0:T(8,128)(2,1)S(1)} collective-permute-done((bf16[256,384]{1,0:T(8,128)(2,1)S(1)}, bf16[256,384]{1,0:T(8,128)(2,1)S(1)}, u32[]{:S(2)}, u32[]{:S(2)}) %collective-permute-start.5) | collective-permute-done | bytes 196640 | tf_op jit(solution)/shard_map/ppermute | solution.py:39
  39.4 0.9 collective-permute-start.7
  40.4 1.2 %collective-permute-start.8 = (bf16[256,384]{1,0:T(8,128)(2,1)S(1)}, bf16[256,384]{1,0:T(8,128)(2,1)S(1)}, u32[]{:S(2)}, u32[]{:S(2)}) collective-permute-start(bf16[256,384]{1,0:T(8,128)(2,1)S(1)} %collective-permute-done.5), channel_id=1, source_target_pairs={{0,32},{8,232},{16,48},{24,248},{32,64},{40,8},{48,80},{56,24},{64... | collective-permute-start | bytes 589832 | tf_op jit(solution)/shard_map/ppermute | solution.py:39
  41.6 1.4 %collective-permute-start.6 = (bf16[128,384]{1,0:T(8,128)(2,1)S(1)}, bf16[128,384]{1,0:T(8,128)(2,1)S(1)}, u32[]{:S(2)}, u32[]{:S(2)}) collective-permute-start(bf16[128,384]{1,0:T(8,128)(2,1)S(1)} %get-tuple-element.47), channel_id=1, source_target_pairs={{0,64},{8,200},{16,80},{24,216},{32,96},{40,232},{48,112},{56,248}... | collective-permute-start | bytes 294920 | tf_op jit(solution)/shard_map/ppermute | solution.py:39
  42.9 2.8 %attend.8 = bf16[144,384]{1,0:T(8,128)(2,1)S(1)} custom-call(bf16[128,384]{1,0:T(8,128)(2,1)S(1)} %get-tuple-element.48.refs_0_, bf16[2048,384]{1,0:T(8,128)(2,1)S(1)} %copy-done, bf16[2048,384]{1,0:T(8,128)(2,1)S(1)} %collective-permute-done.1.refs_2_, bf16[384,2048]{1,0:T(8,128)(2,1)S(1)} %turn.2.refs_3_, bf16[384,2048]{1,0:T(8,128)(2,1)S(1)} %turn.3.refs_4_), custom_call_target="tpu_custom_call" | custom-call | flops 1610612736 | bytes 6291456 | tf_op jit(solution)/shard_map/attend/pallas_call | solution.py:222
  45.8 2.6 %collective-permute-done.6.refs_0_ = bf16[128,384]{1,0:T(8,128)(2,1)S(1)} collective-permute-done((bf16[128,384]{1,0:T(8,128)(2,1)S(1)}, bf16[128,384]{1,0:T(8,128)(2,1)S(1)}, u32[]{:S(2)}, u32[]{:S(2)}) %collective-permute-start.6) | collective-permute-done | bytes 98336 | tf_op jit(solution)/shard_map/ppermute | solution.py:39
  48.4 2.8 %attend.9 = bf16[144,384]{1,0:T(8,128)(2,1)S(1)} custom-call(bf16[128,384]{1,0:T(8,128)(2,1)S(1)} %collective-permute-done.6.refs_0_, bf16[2048,384]{1,0:T(8,128)(2,1)S(1)} %copy-done, bf16[2048,384]{1,0:T(8,128)(2,1)S(1)} %collective-permute-done.1.refs_2_, bf16[384,2048]{1,0:T(8,128)(2,1)S(1)} %turn.2.refs_3_, bf16[384,2048]{1,0:T(8,128)(2,1)S(1)} %turn.3.refs_4_), custom_call_target="tpu_custom_call" | custom-call | flops 1610612736 | bytes 6291456 | tf_op jit(solution)/shard_map/attend/pallas_call | solution.py:222
  51.2 3.1 %collective-permute-start.9 = (bf16[144,384]{1,0:T(8,128)(2,1)S(1)}, bf16[144,384]{1,0:T(8,128)(2,1)S(1)}, u32[]{:S(2)}, u32[]{:S(2)}) collective-permute-start(bf16[144,384]{1,0:T(8,128)(2,1)S(1)} %attend.8), channel_id=1, source_target_pairs={{0,192},{8,72},{16,208},{24,88},{32,224},{40,104},{48,240},{56,120... | collective-permute-start | bytes 331784 | tf_op jit(solution)/shard_map/ppermute | solution.py:39
  54.3 4.3 %attend.10 = bf16[272,384]{1,0:T(8,128)(2,1)S(1)} custom-call(bf16[256,384]{1,0:T(8,128)(2,1)S(1)} %collective-permute-done.8.refs_0_, bf16[2048,384]{1,0:T(8,128)(2,1)S(1)} %copy-done, bf16[2048,384]{1,0:T(8,128)(2,1)S(1)} %collective-permute-done.1.refs_2_, bf16[384,2048]{1,0:T(8,128)(2,1)S(1)} %turn.2.refs_3_, bf16[384,2048]{1,0:T(8,128)(2,1)S(1)} %turn.3.refs_4_), custom_call_target="tpu_custom_call" | custom-call | flops 3221225472 | bytes 6291456 | tf_op jit(solution)/shard_map/attend/pallas_call | solution.py:222
  58.6 4.2 %collective-permute-start.12 = (bf16[272,384]{1,0:T(8,128)(2,1)S(1)}, bf16[272,384]{1,0:T(8,128)(2,1)S(1)}, u32[]{:S(2)}, u32[]{:S(2)}) collective-permute-start(bf16[272,384]{1,0:T(8,128)(2,1)S(1)} %attend.10), channel_id=1, source_target_pairs={{0,160},{8,104},{16,176},{24,120},{32,192},{40,136},{48,208},{56,1... | collective-permute-start | bytes 626696 | tf_op jit(solution)/shard_map/ppermute | solution.py:39
  62.8 2.2 %collective-permute-start.11 = (bf16[144,384]{1,0:T(8,128)(2,1)S(1)}, bf16[144,384]{1,0:T(8,128)(2,1)S(1)}, u32[]{:S(2)}, u32[]{:S(2)}) collective-permute-start(bf16[144,384]{1,0:T(8,128)(2,1)S(1)} %attend.9), channel_id=1, source_target_pairs={{0,128},{8,136},{16,144},{24,152},{32,160},{40,168},{48,176},{56,1... | collective-permute-start | bytes 331784 | tf_op jit(solution)/shard_map/ppermute | solution.py:39
  65.1 2.8 %attend.11 = bf16[144,384]{1,0:T(8,128)(2,1)S(1)} custom-call(bf16[128,384]{1,0:T(8,128)(2,1)S(1)} %slice.11.refs_0_, bf16[2048,384]{1,0:T(8,128)(2,1)S(1)} %copy-done, bf16[2048,384]{1,0:T(8,128)(2,1)S(1)} %collective-permute-done.1.refs_2_, bf16[384,2048]{1,0:T(8,128)(2,1)S(1)} %turn.2.refs_3_, bf16[384,2048]{1,0:T(8,128)(2,1)S(1)} %turn.3.refs_4_), custom_call_target="tpu_custom_call" | custom-call | flops 1610612736 | bytes 6291456 | tf_op jit(solution)/shard_map/attend/pallas_call | solution.py:222
  67.9 3.1 %collective-permute-start.10 = (bf16[144,384]{1,0:T(8,128)(2,1)S(1)}, bf16[144,384]{1,0:T(8,128)(2,1)S(1)}, u32[]{:S(2)}, u32[]{:S(2)}) collective-permute-start(bf16[144,384]{1,0:T(8,128)(2,1)S(1)} %attend.11), channel_id=1, source_target_pairs={{0,192},{8,72},{16,208},{24,88},{32,224},{40,104},{48,240},{56,120... | collective-permute-start | bytes 331784 | tf_op jit(solution)/shard_map/ppermute | solution.py:39
  70.9 4.6 %collective-permute-done.12.refs_3_.refs_2_ = bf16[272,384]{1,0:T(8,128)(2,1)S(1)} collective-permute-done((bf16[272,384]{1,0:T(8,128)(2,1)S(1)}, bf16[272,384]{1,0:T(8,128)(2,1)S(1)}, u32[]{:S(2)}, u32[]{:S(2)}) %collective-permute-start.12) | collective-permute-done | bytes 208928 | tf_op jit(solution)/shard_map/ppermute | solution.py:39
  76.5 1.3 %collective-permute-done.10.refs_1_ = bf16[144,384]{1,0:T(8,128)(2,1)S(1)} collective-permute-done((bf16[144,384]{1,0:T(8,128)(2,1)S(1)}, bf16[144,384]{1,0:T(8,128)(2,1)S(1)}, u32[]{:S(2)}, u32[]{:S(2)}) %collective-permute-start.10) | collective-permute-done | bytes 110624 | tf_op jit(solution)/shard_map/ppermute | solution.py:39
  79.3 4.9 %collective-permute-done.14.refs_2_ = bf16[80,384]{1,0:T(8,128)(2,1)S(1)} collective-permute-done((bf16[80,384]{1,0:T(8,128)(2,1)S(1)}, bf16[80,384]{1,0:T(8,128)(2,1)S(1)}, u32[]{:S(2)}, u32[]{:S(2)}) %collective-permute-start.14) | collective-permute-done | bytes 61472 | tf_op jit(solution)/shard_map/ppermute | solution.py:31
  85.0 10.5 %all_to_all.11 = bf16[8,8,3072]{2,1,0:T(8,128)(2,1)S(1)} all-to-all(bf16[8,8,3072]{2,1,0:T(8,128)(2,1)S(1)} %bitcast.2), channel_id=1, replica_groups=mesh['ctx'=32,'head'=8] {'head'}, dimensions={0} | all-to-all | bytes 786432 | tf_op jit(solution)/shard_map/all_to_all | solution.py:43
  (39 shorter events, 7.7 us)
Async XLA Ops:
  0.0 22.9 %collective-permute-start.3 = (bf16[2048,384]{1,0:T(8,128)(2,1)}, bf16[2048,384]{1,0:T(8,128)(2,1)S(1)}, u32[]{:S(2)}, u32[]{:S(2)}) collective-permute-start(bf16[2048,384]{1,0:T(8,128)(2,1)} %value.2), channel_id=1, source_target_pairs={{0,8},{8,0},{16,24},{24,16},{32,40},{40,32},{48,56},{56,48},{64,72... | collective-permute-start | bytes 4718600 | tf_op jit(solution)/shard_map/ppermute | solution.py:31
  0.0 25.4 %collective-permute-start.1 = (bf16[2048,384]{1,0:T(8,128)(2,1)}, bf16[2048,384]{1,0:T(8,128)(2,1)S(1)}, u32[]{:S(2)}, u32[]{:S(2)}) collective-permute-start(bf16[2048,384]{1,0:T(8,128)(2,1)} %refs_1_.11), channel_id=1, source_target_pairs={{0,8},{8,0},{16,24},{24,16},{32,40},{40,32},{48,56},{56,48},{64,72... | collective-permute-start | bytes 4718600 | tf_op jit(solution)/shard_map/ppermute | solution.py:31
  0.5 0.8 copy-start.4
  1.3 14.0 %copy-start.1 = (bf16[3072,384]{1,0:T(8,128)(2,1)S(1)}, bf16[3072,384]{1,0:T(8,128)(2,1)}, u32[]{:S(2)}) copy-start(bf16[3072,384]{1,0:T(8,128)(2,1)} %weight.1) | copy-start | bytes 7077892
  15.3 1.4 %copy-start.3 = (bf16[2048,384]{1,0:T(8,128)(2,1)S(1)}, bf16[2048,384]{1,0:T(8,128)(2,1)}, u32[]{:S(2)}) copy-start(bf16[2048,384]{1,0:T(8,128)(2,1)} %value.2) | copy-start | bytes 4718596
  15.8 5.7 %collective-permute-start = (bf16[64,384]{1,0:T(8,128)(2,1)S(1)}, bf16[64,384]{1,0:T(8,128)(2,1)S(1)}, u32[]{:S(2)}, u32[]{:S(2)}) collective-permute-start(bf16[64,384]{1,0:T(8,128)(2,1)S(1)} %project.1), channel_id=1, source_target_pairs={{0,16},{8,24},{16,0},{24,8},{32,48},{40,56},{48,32},{56,40},{64,80... | collective-permute-start | bytes 147464 | tf_op jit(solution)/shard_map/ppermute | solution.py:31
  21.5 1.4 %collective-permute-start.2 = (bf16[128,384]{1,0:T(8,128)(2,1)S(1)}, bf16[128,384]{1,0:T(8,128)(2,1)S(1)}, u32[]{:S(2)}, u32[]{:S(2)}) collective-permute-start(bf16[128,384]{1,0:T(8,128)(2,1)S(1)} %constant_dynamic-update-slice_fusion.refs_0_), channel_id=1, source_target_pairs={{0,8},{8,0},{16,24},{24,16},{32,40},{40,32},{48,56},{56,48},{64,72... | collective-permute-start | bytes 294920 | tf_op jit(solution)/shard_map/ppermute | solution.py:31
  23.0 2.5 %copy-start = (bf16[2048,384]{1,0:T(8,128)(2,1)S(1)}, bf16[2048,384]{1,0:T(8,128)(2,1)}, u32[]{:S(2)}) copy-start(bf16[2048,384]{1,0:T(8,128)(2,1)} %refs_1_.11) | copy-start | bytes 4718596
  23.0 9.6 %collective-permute-start.4 = (bf16[256,384]{1,0:T(8,128)(2,1)S(1)}, bf16[256,384]{1,0:T(8,128)(2,1)S(1)}, u32[]{:S(2)}, u32[]{:S(2)}) collective-permute-start(bf16[256,384]{1,0:T(8,128)(2,1)S(1)} %pad_maximum_fusion), channel_id=1, source_target_pairs={{0,32},{8,232},{16,48},{24,248},{32,64},{40,8},{48,80},{56,24},{64... | collective-permute-start | bytes 589832 | tf_op jit(solution)/shard_map/ppermute | solution.py:39
  32.6 6.9 %collective-permute-start.5 = (bf16[256,384]{1,0:T(8,128)(2,1)S(1)}, bf16[256,384]{1,0:T(8,128)(2,1)S(1)}, u32[]{:S(2)}, u32[]{:S(2)}) collective-permute-start(bf16[256,384]{1,0:T(8,128)(2,1)S(1)} %collective-permute-done.4.refs_0_), channel_id=1, source_target_pairs={{0,32},{8,232},{16,48},{24,248},{32,64},{40,8},{48,80},{56,24},{64... | collective-permute-start | bytes 589832 | tf_op jit(solution)/shard_map/ppermute | solution.py:39
  39.4 9.0 %collective-permute-start.7 = (bf16[272,384]{1,0:T(8,128)(2,1)S(1)}, bf16[272,384]{1,0:T(8,128)(2,1)S(1)}, u32[]{:S(2)}, u32[]{:S(2)}) collective-permute-start(bf16[272,384]{1,0:T(8,128)(2,1)S(1)} %attend.7), channel_id=1, source_target_pairs={{0,224},{8,40},{16,240},{24,56},{32,0},{40,72},{48,16},{56,88},{64... | collective-permute-start | bytes 626696 | tf_op jit(solution)/shard_map/ppermute | solution.py:39
  40.4 10.8 %collective-permute-start.8 = (bf16[256,384]{1,0:T(8,128)(2,1)S(1)}, bf16[256,384]{1,0:T(8,128)(2,1)S(1)}, u32[]{:S(2)}, u32[]{:S(2)}) collective-permute-start(bf16[256,384]{1,0:T(8,128)(2,1)S(1)} %collective-permute-done.5), channel_id=1, source_target_pairs={{0,32},{8,232},{16,48},{24,248},{32,64},{40,8},{48,80},{56,24},{64... | collective-permute-start | bytes 589832 | tf_op jit(solution)/shard_map/ppermute | solution.py:39
  41.6 6.8 %collective-permute-start.6 = (bf16[128,384]{1,0:T(8,128)(2,1)S(1)}, bf16[128,384]{1,0:T(8,128)(2,1)S(1)}, u32[]{:S(2)}, u32[]{:S(2)}) collective-permute-start(bf16[128,384]{1,0:T(8,128)(2,1)S(1)} %get-tuple-element.47), channel_id=1, source_target_pairs={{0,64},{8,200},{16,80},{24,216},{32,96},{40,232},{48,112},{56,248}... | collective-permute-start | bytes 294920 | tf_op jit(solution)/shard_map/ppermute | solution.py:39
  51.2 7.4 %collective-permute-start.9 = (bf16[144,384]{1,0:T(8,128)(2,1)S(1)}, bf16[144,384]{1,0:T(8,128)(2,1)S(1)}, u32[]{:S(2)}, u32[]{:S(2)}) collective-permute-start(bf16[144,384]{1,0:T(8,128)(2,1)S(1)} %attend.8), channel_id=1, source_target_pairs={{0,192},{8,72},{16,208},{24,88},{32,224},{40,104},{48,240},{56,120... | collective-permute-start | bytes 331784 | tf_op jit(solution)/shard_map/ppermute | solution.py:39
  58.6 16.9 %collective-permute-start.12 = (bf16[272,384]{1,0:T(8,128)(2,1)S(1)}, bf16[272,384]{1,0:T(8,128)(2,1)S(1)}, u32[]{:S(2)}, u32[]{:S(2)}) collective-permute-start(bf16[272,384]{1,0:T(8,128)(2,1)S(1)} %attend.10), channel_id=1, source_target_pairs={{0,160},{8,104},{16,176},{24,120},{32,192},{40,136},{48,208},{56,1... | collective-permute-start | bytes 626696 | tf_op jit(solution)/shard_map/ppermute | solution.py:39
  62.8 13.2 %collective-permute-start.11 = (bf16[144,384]{1,0:T(8,128)(2,1)S(1)}, bf16[144,384]{1,0:T(8,128)(2,1)S(1)}, u32[]{:S(2)}, u32[]{:S(2)}) collective-permute-start(bf16[144,384]{1,0:T(8,128)(2,1)S(1)} %attend.9), channel_id=1, source_target_pairs={{0,128},{8,136},{16,144},{24,152},{32,160},{40,168},{48,176},{56,1... | collective-permute-start | bytes 331784 | tf_op jit(solution)/shard_map/ppermute | solution.py:39
  67.9 9.9 %collective-permute-start.10 = (bf16[144,384]{1,0:T(8,128)(2,1)S(1)}, bf16[144,384]{1,0:T(8,128)(2,1)S(1)}, u32[]{:S(2)}, u32[]{:S(2)}) collective-permute-start(bf16[144,384]{1,0:T(8,128)(2,1)S(1)} %attend.11), channel_id=1, source_target_pairs={{0,192},{8,72},{16,208},{24,88},{32,224},{40,104},{48,240},{56,120... | collective-permute-start | bytes 331784 | tf_op jit(solution)/shard_map/ppermute | solution.py:39
  75.9 1.8 %collective-permute-start.13 = (bf16[144,384]{1,0:T(8,128)(2,1)S(1)}, bf16[144,384]{1,0:T(8,128)(2,1)S(1)}, u32[]{:S(2)}, u32[]{:S(2)}) collective-permute-start(bf16[144,384]{1,0:T(8,128)(2,1)S(1)} %merge.5), channel_id=1, source_target_pairs={{0,8},{8,0},{16,24},{24,16},{32,40},{40,32},{48,56},{56,48},{64,72... | collective-permute-start | bytes 331784 | tf_op jit(solution)/shard_map/ppermute | solution.py:31
  76.0 8.2 %copy-start.2 = (bf16[384,3072]{1,0:T(8,128)(2,1)S(1)}, bf16[384,3072]{1,0:T(8,128)(2,1)}, u32[]{:S(2)}) copy-start(bf16[384,3072]{1,0:T(8,128)(2,1)} %refs_3_.1) | copy-start | bytes 7077892
  78.4 5.8 %collective-permute-start.14 = (bf16[80,384]{1,0:T(8,128)(2,1)S(1)}, bf16[80,384]{1,0:T(8,128)(2,1)S(1)}, u32[]{:S(2)}, u32[]{:S(2)}) collective-permute-start(bf16[80,384]{1,0:T(8,128)(2,1)S(1)} %merge.7), channel_id=1, source_target_pairs={{0,16},{8,24},{16,0},{24,8},{32,48},{40,56},{48,32},{56,40},{64,80... | collective-permute-start | bytes 184328 | tf_op jit(solution)/shard_map/ppermute | solution.py:31

commit v8 on v6

--- a/solution.py
+++ b/solution.py
@@ -306,12 +306,13 @@
     part_others, third, back_near = tied(part_others, third, back_near)
     back_others = carry(part_others, -2)
     part, = attend((third,), keys, values)
-    part, second, far, back_others = tied(part, second, far, back_others)
+    part, second, far = tied(part, second, far)
     back_third = carry(part, -3)
     part_far, = attend((far,), keys, values)
     part_far, second = tied(part_far, second)
     back_far = carry(part_far, -4)
     part, = attend((second[: 2 * few],), keys, values)
+    part, back_others = tied(part, back_others)
     early = merge(2 * few, (part_own, 0), (back_far, 0), (back_near, 0), (back_third, 0), flops=MERGE_FLOPS)
     others = move(merge(2 * few, (back_others, 0), (back_near, 2 * few), (back_third, 2 * few)), dcore=1)
     back_second, early, others = tied(carry(part, -2), early, others)

time: 94 us -> 96 us (1.021)
  the two profiles are of different devices: /device:TPU:4 before, /device:TPU:64 now
where the time goes in v8:
time: 96 us; the launch traced here: 95.7 us
  starting transfers between devices  28.1 us (29%)
  blocking collectives  25.4 us (26%)
  Pallas kernels  23.5 us (24%)
  waiting for transfers between devices  16.9 us (18%)
    all_to_all x2, blocking collectives, exchange(): return lax.all_to_all(value, 'head', 0, 0)  25.4 us
    pallas_call x15, Pallas kernels, call(): pl.pallas_call(kernel, out_shape=out_shape, in_specs=[vmem()] * len(opera...  23.5 us
    ppermute x9, starting transfers between devices, carry(): return lax.ppermute(value, 'ctx', pairs)  21.7 us
    ppermute x9, waiting for transfers between devices, carry(): return lax.ppermute(value, 'ctx', pairs)  10 us
    ppermute x6, waiting for transfers between devices, move(): return lax.ppermute(value, 'ctx', pairs)  6.9 us
    ppermute x6, starting transfers between devices, move(): return lax.ppermute(value, 'ctx', pairs)  6.41 us
  transfers between devices with their start and end apart: 15, of which 7 were waited for; matrix products, arithmetic and copies ran while one was open for 0% of the time, Pallas kernels for 23%

profile of v8, /device:TPU:64, one launch (start us, length us, event | category | flops | bytes accessed | tf_op | source)
XLA Modules:
  0.0 95.7 jit_solution(11967945052330874492)
XLA Ops:
  0.5 0.8 copy-done.4
  1.3 14.3 %all_to_all.10 = bf16[8,8,3072]{2,1,0:T(8,128)(2,1)S(1)} all-to-all(bf16[8,8,3072]{2,1,0:T(8,128)(2,1)S(1)} %repeat.1), channel_id=1, replica_groups=mesh['ctx'=32,'head'=8] {'head'}, dimensions={0} | all-to-all | bytes 786432 | tf_op jit(solution)/shard_map/all_to_all | solution.py:43
  16.1 2.8 %collective-permute-start = (bf16[64,384]{1,0:T(8,128)(2,1)S(1)}, bf16[64,384]{1,0:T(8,128)(2,1)S(1)}, u32[]{:S(2)}, u32[]{:S(2)}) collective-permute-start(bf16[64,384]{1,0:T(8,128)(2,1)S(1)} %project.1), channel_id=1, source_target_pairs={{0,16},{8,24},{16,0},{24,8},{32,48},{40,56},{48,32},{56,40},{64,80... | collective-permute-start | bytes 147464 | tf_op jit(solution)/shard_map/ppermute | solution.py:31
  19.4 2.4 %collective-permute-done = bf16[64,384]{1,0:T(8,128)(2,1)S(1)} collective-permute-done((bf16[64,384]{1,0:T(8,128)(2,1)S(1)}, bf16[64,384]{1,0:T(8,128)(2,1)S(1)}, u32[]{:S(2)}, u32[]{:S(2)}) %collective-permute-start) | collective-permute-done | bytes 49184 | tf_op jit(solution)/shard_map/ppermute | solution.py:31
  21.9 1.3 %collective-permute-done.2 = bf16[128,384]{1,0:T(8,128)(2,1)S(1)} collective-permute-done((bf16[128,384]{1,0:T(8,128)(2,1)S(1)}, bf16[128,384]{1,0:T(8,128)(2,1)S(1)}, u32[]{:S(2)}, u32[]{:S(2)}) %collective-permute-start.2) | collective-permute-done | bytes 98336 | tf_op jit(solution)/shard_map/ppermute | solution.py:31
  23.3 2.0 %collective-permute-start.4 = (bf16[256,384]{1,0:T(8,128)(2,1)S(1)}, bf16[256,384]{1,0:T(8,128)(2,1)S(1)}, u32[]{:S(2)}, u32[]{:S(2)}) collective-permute-start(bf16[256,384]{1,0:T(8,128)(2,1)S(1)} %pad_maximum_fusion), channel_id=1, source_target_pairs={{0,32},{8,232},{16,48},{24,248},{32,64},{40,8},{48,80},{56,24},{64... | collective-permute-start | bytes 589832 | tf_op jit(solution)/shard_map/ppermute | solution.py:39
  25.7 2.8 %attend.6.refs_0_ = bf16[144,384]{1,0:T(8,128)(2,1)S(1)} custom-call(bf16[128,384]{1,0:T(8,128)(2,1)S(1)} %constant_dynamic-update-slice_fusion.refs_0_, bf16[2048,384]{1,0:T(8,128)(2,1)S(1)} %copy-done, bf16[2048,384]{1,0:T(8,128)(2,1)S(1)} %collective-permute-done.1.refs_2_, bf16[384,2048]{1,0:T(8,128)(2,1)S(1)} %turn.2.refs_3_, ...), custom_call_target="tpu_custom_call" | custom-call | flops 1610612736 | bytes 6291456 | tf_op jit(solution)/shard_map/attend/pallas_call | solution.py:222
  29.0 2.8 %collective-permute-start.5 = (bf16[256,384]{1,0:T(8,128)(2,1)S(1)}, bf16[256,384]{1,0:T(8,128)(2,1)S(1)}, u32[]{:S(2)}, u32[]{:S(2)}) collective-permute-start(bf16[256,384]{1,0:T(8,128)(2,1)S(1)} %collective-permute-done.4.refs_0_), channel_id=1, source_target_pairs={{0,32},{8,232},{16,48},{24,248},{32,64},{40,8},{48,80},{56,24},{64... | collective-permute-start | bytes 589832 | tf_op jit(solution)/shard_map/ppermute | solution.py:39
  31.8 4.3 %attend.7 = bf16[272,384]{1,0:T(8,128)(2,1)S(1)} custom-call(bf16[256,384]{1,0:T(8,128)(2,1)S(1)} %collective-permute-done.4.refs_0_, bf16[2048,384]{1,0:T(8,128)(2,1)S(1)} %copy-done, bf16[2048,384]{1,0:T(8,128)(2,1)S(1)} %collective-permute-done.1.refs_2_, bf16[384,2048]{1,0:T(8,128)(2,1)S(1)} %turn.2.refs_3_, bf16[384,2048]{1,0:T(8,128)(2,1)S(1)} %turn.3.refs_4_), custom_call_target="tpu_custom_call" | custom-call | flops 3221225472 | bytes 6291456 | tf_op jit(solution)/shard_map/attend/pallas_call | solution.py:222
  36.7 3.2 %collective-permute-start.6 = (bf16[256,384]{1,0:T(8,128)(2,1)S(1)}, bf16[256,384]{1,0:T(8,128)(2,1)S(1)}, u32[]{:S(2)}, u32[]{:S(2)}) collective-permute-start(bf16[256,384]{1,0:T(8,128)(2,1)S(1)} %collective-permute-done.5), channel_id=1, source_target_pairs={{0,32},{8,232},{16,48},{24,248},{32,64},{40,8},{48,80},{56,24},{64... | collective-permute-start | bytes 589832 | tf_op jit(solution)/shard_map/ppermute | solution.py:39
  39.9 3.8 %collective-permute-start.8 = (bf16[128,384]{1,0:T(8,128)(2,1)S(1)}, bf16[128,384]{1,0:T(8,128)(2,1)S(1)}, u32[]{:S(2)}, u32[]{:S(2)}) collective-permute-start(bf16[128,384]{1,0:T(8,128)(2,1)S(1)} %get-tuple-element.51), channel_id=1, source_target_pairs={{0,64},{8,200},{16,80},{24,216},{32,96},{40,232},{48,112},{56,248}... | collective-permute-start | bytes 294920 | tf_op jit(solution)/shard_map/ppermute | solution.py:39
  43.7 2.8 %attend.8 = bf16[144,384]{1,0:T(8,128)(2,1)S(1)} custom-call(bf16[128,384]{1,0:T(8,128)(2,1)S(1)} %get-tuple-element.52.refs_0_, bf16[2048,384]{1,0:T(8,128)(2,1)S(1)} %copy-done, bf16[2048,384]{1,0:T(8,128)(2,1)S(1)} %collective-permute-done.1.refs_2_, bf16[384,2048]{1,0:T(8,128)(2,1)S(1)} %turn.2.refs_3_, bf16[384,2048]{1,0:T(8,128)(2,1)S(1)} %turn.3.refs_4_), custom_call_target="tpu_custom_call" | custom-call | flops 1610612736 | bytes 6291456 | tf_op jit(solution)/shard_map/attend/pallas_call | solution.py:222
  46.6 4.3 %attend.9 = bf16[272,384]{1,0:T(8,128)(2,1)S(1)} custom-call(bf16[256,384]{1,0:T(8,128)(2,1)S(1)} %collective-permute-done.6.refs_0_, bf16[2048,384]{1,0:T(8,128)(2,1)S(1)} %copy-done, bf16[2048,384]{1,0:T(8,128)(2,1)S(1)} %collective-permute-done.1.refs_2_, bf16[384,2048]{1,0:T(8,128)(2,1)S(1)} %turn.2.refs_3_, bf16[384,2048]{1,0:T(8,128)(2,1)S(1)} %turn.3.refs_4_), custom_call_target="tpu_custom_call" | custom-call | flops 3221225472 | bytes 6291456 | tf_op jit(solution)/shard_map/attend/pallas_call | solution.py:222
  50.9 2.5 %collective-permute-start.12 = (bf16[272,384]{1,0:T(8,128)(2,1)S(1)}, bf16[272,384]{1,0:T(8,128)(2,1)S(1)}, u32[]{:S(2)}, u32[]{:S(2)}) collective-permute-start(bf16[272,384]{1,0:T(8,128)(2,1)S(1)} %attend.9), channel_id=1, source_target_pairs={{0,160},{8,104},{16,176},{24,120},{32,192},{40,136},{48,208},{56,1... | collective-permute-start | bytes 626696 | tf_op jit(solution)/shard_map/ppermute | solution.py:39
  53.4 2.8 %attend.10 = bf16[144,384]{1,0:T(8,128)(2,1)S(1)} custom-call(bf16[128,384]{1,0:T(8,128)(2,1)S(1)} %collective-permute-done.8.refs_0_, bf16[2048,384]{1,0:T(8,128)(2,1)S(1)} %copy-done, bf16[2048,384]{1,0:T(8,128)(2,1)S(1)} %collective-permute-done.1.refs_2_, bf16[384,2048]{1,0:T(8,128)(2,1)S(1)} %turn.2.refs_3_, bf16[384,2048]{1,0:T(8,128)(2,1)S(1)} %turn.3.refs_4_), custom_call_target="tpu_custom_call" | custom-call | flops 1610612736 | bytes 6291456 | tf_op jit(solution)/shard_map/attend/pallas_call | solution.py:222
  56.3 1.5 %collective-permute-start.9 = (bf16[144,384]{1,0:T(8,128)(2,1)S(1)}, bf16[144,384]{1,0:T(8,128)(2,1)S(1)}, u32[]{:S(2)}, u32[]{:S(2)}) collective-permute-start(bf16[144,384]{1,0:T(8,128)(2,1)S(1)} %attend.8), channel_id=1, source_target_pairs={{0,192},{8,72},{16,208},{24,88},{32,224},{40,104},{48,240},{56,120... | collective-permute-start | bytes 331784 | tf_op jit(solution)/shard_map/ppermute | solution.py:39
  57.7 3.2 %collective-permute-start.11 = (bf16[144,384]{1,0:T(8,128)(2,1)S(1)}, bf16[144,384]{1,0:T(8,128)(2,1)S(1)}, u32[]{:S(2)}, u32[]{:S(2)}) collective-permute-start(bf16[144,384]{1,0:T(8,128)(2,1)S(1)} %attend.10), channel_id=1, source_target_pairs={{0,128},{8,136},{16,144},{24,152},{32,160},{40,168},{48,176},{56,1... | collective-permute-start | bytes 331784 | tf_op jit(solution)/shard_map/ppermute | solution.py:39
  61.0 2.8 %attend.11 = bf16[144,384]{1,0:T(8,128)(2,1)S(1)} custom-call(bf16[128,384]{1,0:T(8,128)(2,1)S(1)} %slice.11.refs_0_, bf16[2048,384]{1,0:T(8,128)(2,1)S(1)} %copy-done, bf16[2048,384]{1,0:T(8,128)(2,1)S(1)} %collective-permute-done.1.refs_2_, bf16[384,2048]{1,0:T(8,128)(2,1)S(1)} %turn.2.refs_3_, bf16[384,2048]{1,0:T(8,128)(2,1)S(1)} %turn.3.refs_4_), custom_call_target="tpu_custom_call" | custom-call | flops 1610612736 | bytes 6291456 | tf_op jit(solution)/shard_map/attend/pallas_call | solution.py:222
  63.8 2.4 %collective-permute-done.9.refs_0_ = bf16[144,384]{1,0:T(8,128)(2,1)S(1)} collective-permute-done((bf16[144,384]{1,0:T(8,128)(2,1)S(1)}, bf16[144,384]{1,0:T(8,128)(2,1)S(1)}, u32[]{:S(2)}, u32[]{:S(2)}) %collective-permute-start.9) | collective-permute-done | bytes 110624 | tf_op jit(solution)/shard_map/ppermute | solution.py:39
  66.1 2.1 %collective-permute-start.10 = (bf16[144,384]{1,0:T(8,128)(2,1)S(1)}, bf16[144,384]{1,0:T(8,128)(2,1)S(1)}, u32[]{:S(2)}, u32[]{:S(2)}) collective-permute-start(bf16[144,384]{1,0:T(8,128)(2,1)S(1)} %attend.11), channel_id=1, source_target_pairs={{0,192},{8,72},{16,208},{24,88},{32,224},{40,104},{48,240},{56,120... | collective-permute-start | bytes 331784 | tf_op jit(solution)/shard_map/ppermute | solution.py:39
  69.7 6.7 %collective-permute-done.10.refs_1_ = bf16[144,384]{1,0:T(8,128)(2,1)S(1)} collective-permute-done((bf16[144,384]{1,0:T(8,128)(2,1)S(1)}, bf16[144,384]{1,0:T(8,128)(2,1)S(1)}, u32[]{:S(2)}, u32[]{:S(2)}) %collective-permute-start.10) | collective-permute-done | bytes 110624 | tf_op jit(solution)/shard_map/ppermute | solution.py:39
  77.0 2.9 %collective-permute-start.14 = (bf16[80,384]{1,0:T(8,128)(2,1)S(1)}, bf16[80,384]{1,0:T(8,128)(2,1)S(1)}, u32[]{:S(2)}, u32[]{:S(2)}) collective-permute-start(bf16[80,384]{1,0:T(8,128)(2,1)S(1)} %merge.7), channel_id=1, source_target_pairs={{0,16},{8,24},{16,0},{24,8},{32,48},{40,56},{48,32},{56,40},{64,80... | collective-permute-start | bytes 184328 | tf_op jit(solution)/shard_map/ppermute | solution.py:31
  79.9 3.2 %collective-permute-done.14.refs_2_ = bf16[80,384]{1,0:T(8,128)(2,1)S(1)} collective-permute-done((bf16[80,384]{1,0:T(8,128)(2,1)S(1)}, bf16[80,384]{1,0:T(8,128)(2,1)S(1)}, u32[]{:S(2)}, u32[]{:S(2)}) %collective-permute-start.14) | collective-permute-done | bytes 61472 | tf_op jit(solution)/shard_map/ppermute | solution.py:31
  83.9 11.2 %all_to_all.11 = bf16[8,8,3072]{2,1,0:T(8,128)(2,1)S(1)} all-to-all(bf16[8,8,3072]{2,1,0:T(8,128)(2,1)S(1)} %bitcast.2), channel_id=1, replica_groups=mesh['ctx'=32,'head'=8] {'head'}, dimensions={0} | all-to-all | bytes 786432 | tf_op jit(solution)/shard_map/all_to_all | solution.py:43
  (39 shorter events, 6.7 us)
Async XLA Ops:
  0.0 23.2 %collective-permute-start.3 = (bf16[2048,384]{1,0:T(8,128)(2,1)}, bf16[2048,384]{1,0:T(8,128)(2,1)S(1)}, u32[]{:S(2)}, u32[]{:S(2)}) collective-permute-start(bf16[2048,384]{1,0:T(8,128)(2,1)} %value.2), channel_id=1, source_target_pairs={{0,8},{8,0},{16,24},{24,16},{32,40},{40,32},{48,56},{56,48},{64,72... | collective-permute-start | bytes 4718600 | tf_op jit(solution)/shard_map/ppermute | solution.py:31
  0.0 25.7 %collective-permute-start.1 = (bf16[2048,384]{1,0:T(8,128)(2,1)}, bf16[2048,384]{1,0:T(8,128)(2,1)S(1)}, u32[]{:S(2)}, u32[]{:S(2)}) collective-permute-start(bf16[2048,384]{1,0:T(8,128)(2,1)} %refs_1_.11), channel_id=1, source_target_pairs={{0,8},{8,0},{16,24},{24,16},{32,40},{40,32},{48,56},{56,48},{64,72... | collective-permute-start | bytes 4718600 | tf_op jit(solution)/shard_map/ppermute | solution.py:31
  0.5 0.8 copy-start.4
  1.3 14.3 %copy-start.1 = (bf16[3072,384]{1,0:T(8,128)(2,1)S(1)}, bf16[3072,384]{1,0:T(8,128)(2,1)}, u32[]{:S(2)}) copy-start(bf16[3072,384]{1,0:T(8,128)(2,1)} %weight.1) | copy-start | bytes 7077892
  15.6 3.3 %copy-start.3 = (bf16[2048,384]{1,0:T(8,128)(2,1)S(1)}, bf16[2048,384]{1,0:T(8,128)(2,1)}, u32[]{:S(2)}) copy-start(bf16[2048,384]{1,0:T(8,128)(2,1)} %value.2) | copy-start | bytes 4718596
  16.1 5.7 %collective-permute-start = (bf16[64,384]{1,0:T(8,128)(2,1)S(1)}, bf16[64,384]{1,0:T(8,128)(2,1)S(1)}, u32[]{:S(2)}, u32[]{:S(2)}) collective-permute-start(bf16[64,384]{1,0:T(8,128)(2,1)S(1)} %project.1), channel_id=1, source_target_pairs={{0,16},{8,24},{16,0},{24,8},{32,48},{40,56},{48,32},{56,40},{64,80... | collective-permute-start | bytes 147464 | tf_op jit(solution)/shard_map/ppermute | solution.py:31
  21.8 1.4 %collective-permute-start.2 = (bf16[128,384]{1,0:T(8,128)(2,1)S(1)}, bf16[128,384]{1,0:T(8,128)(2,1)S(1)}, u32[]{:S(2)}, u32[]{:S(2)}) collective-permute-start(bf16[128,384]{1,0:T(8,128)(2,1)S(1)} %constant_dynamic-update-slice_fusion.refs_0_), channel_id=1, source_target_pairs={{0,8},{8,0},{16,24},{24,16},{32,40},{40,32},{48,56},{56,48},{64,72... | collective-permute-start | bytes 294920 | tf_op jit(solution)/shard_map/ppermute | solution.py:31
  23.3 2.5 %copy-start = (bf16[2048,384]{1,0:T(8,128)(2,1)S(1)}, bf16[2048,384]{1,0:T(8,128)(2,1)}, u32[]{:S(2)}) copy-start(bf16[2048,384]{1,0:T(8,128)(2,1)} %refs_1_.11) | copy-start | bytes 4718596
  23.3 5.7 %collective-permute-start.4 = (bf16[256,384]{1,0:T(8,128)(2,1)S(1)}, bf16[256,384]{1,0:T(8,128)(2,1)S(1)}, u32[]{:S(2)}, u32[]{:S(2)}) collective-permute-start(bf16[256,384]{1,0:T(8,128)(2,1)S(1)} %pad_maximum_fusion), channel_id=1, source_target_pairs={{0,32},{8,232},{16,48},{24,248},{32,64},{40,8},{48,80},{56,24},{64... | collective-permute-start | bytes 589832 | tf_op jit(solution)/shard_map/ppermute | solution.py:39
  29.0 7.0 %collective-permute-start.5 = (bf16[256,384]{1,0:T(8,128)(2,1)S(1)}, bf16[256,384]{1,0:T(8,128)(2,1)S(1)}, u32[]{:S(2)}, u32[]{:S(2)}) collective-permute-start(bf16[256,384]{1,0:T(8,128)(2,1)S(1)} %collective-permute-done.4.refs_0_), channel_id=1, source_target_pairs={{0,32},{8,232},{16,48},{24,248},{32,64},{40,8},{48,80},{56,24},{64... | collective-permute-start | bytes 589832 | tf_op jit(solution)/shard_map/ppermute | solution.py:39
  36.1 10.5 %collective-permute-start.7 = (bf16[272,384]{1,0:T(8,128)(2,1)S(1)}, bf16[272,384]{1,0:T(8,128)(2,1)S(1)}, u32[]{:S(2)}, u32[]{:S(2)}) collective-permute-start(bf16[272,384]{1,0:T(8,128)(2,1)S(1)} %attend.7), channel_id=1, source_target_pairs={{0,224},{8,40},{16,240},{24,56},{32,0},{40,72},{48,16},{56,88},{64... | collective-permute-start | bytes 626696 | tf_op jit(solution)/shard_map/ppermute | solution.py:39
  36.7 9.8 %collective-permute-start.6 = (bf16[256,384]{1,0:T(8,128)(2,1)S(1)}, bf16[256,384]{1,0:T(8,128)(2,1)S(1)}, u32[]{:S(2)}, u32[]{:S(2)}) collective-permute-start(bf16[256,384]{1,0:T(8,128)(2,1)S(1)} %collective-permute-done.5), channel_id=1, source_target_pairs={{0,32},{8,232},{16,48},{24,248},{32,64},{40,8},{48,80},{56,24},{64... | collective-permute-start | bytes 589832 | tf_op jit(solution)/shard_map/ppermute | solution.py:39
  39.9 10.9 %collective-permute-start.8 = (bf16[128,384]{1,0:T(8,128)(2,1)S(1)}, bf16[128,384]{1,0:T(8,128)(2,1)S(1)}, u32[]{:S(2)}, u32[]{:S(2)}) collective-permute-start(bf16[128,384]{1,0:T(8,128)(2,1)S(1)} %get-tuple-element.51), channel_id=1, source_target_pairs={{0,64},{8,200},{16,80},{24,216},{32,96},{40,232},{48,112},{56,248}... | collective-permute-start | bytes 294920 | tf_op jit(solution)/shard_map/ppermute | solution.py:39
  50.9 17.4 %collective-permute-start.12 = (bf16[272,384]{1,0:T(8,128)(2,1)S(1)}, bf16[272,384]{1,0:T(8,128)(2,1)S(1)}, u32[]{:S(2)}, u32[]{:S(2)}) collective-permute-start(bf16[272,384]{1,0:T(8,128)(2,1)S(1)} %attend.9), channel_id=1, source_target_pairs={{0,160},{8,104},{16,176},{24,120},{32,192},{40,136},{48,208},{56,1... | collective-permute-start | bytes 626696 | tf_op jit(solution)/shard_map/ppermute | solution.py:39
  56.3 9.9 %collective-permute-start.9 = (bf16[144,384]{1,0:T(8,128)(2,1)S(1)}, bf16[144,384]{1,0:T(8,128)(2,1)S(1)}, u32[]{:S(2)}, u32[]{:S(2)}) collective-permute-start(bf16[144,384]{1,0:T(8,128)(2,1)S(1)} %attend.8), channel_id=1, source_target_pairs={{0,192},{8,72},{16,208},{24,88},{32,224},{40,104},{48,240},{56,120... | collective-permute-start | bytes 331784 | tf_op jit(solution)/shard_map/ppermute | solution.py:39
  57.7 11.5 %collective-permute-start.11 = (bf16[144,384]{1,0:T(8,128)(2,1)S(1)}, bf16[144,384]{1,0:T(8,128)(2,1)S(1)}, u32[]{:S(2)}, u32[]{:S(2)}) collective-permute-start(bf16[144,384]{1,0:T(8,128)(2,1)S(1)} %attend.10), channel_id=1, source_target_pairs={{0,128},{8,136},{16,144},{24,152},{32,160},{40,168},{48,176},{56,1... | collective-permute-start | bytes 331784 | tf_op jit(solution)/shard_map/ppermute | solution.py:39
  66.1 10.2 %collective-permute-start.10 = (bf16[144,384]{1,0:T(8,128)(2,1)S(1)}, bf16[144,384]{1,0:T(8,128)(2,1)S(1)}, u32[]{:S(2)}, u32[]{:S(2)}) collective-permute-start(bf16[144,384]{1,0:T(8,128)(2,1)S(1)} %attend.11), channel_id=1, source_target_pairs={{0,192},{8,72},{16,208},{24,88},{32,224},{40,104},{48,240},{56,120... | collective-permute-start | bytes 331784 | tf_op jit(solution)/shard_map/ppermute | solution.py:39
  68.6 7.7 %collective-permute-start.13 = (bf16[144,384]{1,0:T(8,128)(2,1)S(1)}, bf16[144,384]{1,0:T(8,128)(2,1)S(1)}, u32[]{:S(2)}, u32[]{:S(2)}) collective-permute-start(bf16[144,384]{1,0:T(8,128)(2,1)S(1)} %merge.5), channel_id=1, source_target_pairs={{0,8},{8,0},{16,24},{24,16},{32,40},{40,32},{48,56},{56,48},{64,72... | collective-permute-start | bytes 331784 | tf_op jit(solution)/shard_map/ppermute | solution.py:31
  69.2 13.9 %copy-start.2 = (bf16[384,3072]{1,0:T(8,128)(2,1)S(1)}, bf16[384,3072]{1,0:T(8,128)(2,1)}, u32[]{:S(2)}) copy-start(bf16[384,3072]{1,0:T(8,128)(2,1)} %refs_3_.1) | copy-start | bytes 7077892
  77.0 6.1 %collective-permute-start.14 = (bf16[80,384]{1,0:T(8,128)(2,1)S(1)}, bf16[80,384]{1,0:T(8,128)(2,1)S(1)}, u32[]{:S(2)}, u32[]{:S(2)}) collective-permute-start(bf16[80,384]{1,0:T(8,128)(2,1)S(1)} %merge.7), channel_id=1, source_target_pairs={{0,16},{8,24},{16,0},{24,8},{32,48},{40,56},{48,32},{56,40},{64,80... | collective-permute-start | bytes 184328 | tf_op jit(solution)/shard_map/ppermute | solution.py:31
